TPU v7x, 32 devices: a whole 2x2x4 slice. The times are simulated.
32 devices in a mesh: mode: 4 (over y, core), ex: 2 (over x), ey: 4 (over z).
Axes of the slice: x: 2, y: 2, z: 4, core: 2. Of those that a mesh axis runs over, the one named last changes fastest.
Arguments:
- forcing: float32 [64, 81, 2048], P('mode', None, ('ex', 'ey')), may hold values from -6 to 6
- eigen_basis: float32 [7, 7], replicated, may hold values from -2 to 2
- eigen_values: float32 [7], replicated, may hold values from 1 to 20
- coupling: float32 [32, 49], replicated, may hold values from -0.875 to 0.875
- inverse_blocks: float32 [64, 256, 256], P('mode'), may hold values from -0.0625 to 0.0625
- slots: int32 [32, 2048], P(None, ('ex', 'ey')), may hold values from 0 to 255
- sides: int32 [8, 256], P(('ex', 'ey')), may hold values from 0 to 4
- partners: int32 [8, 256], P(('ex', 'ey')), may hold values from 0 to 255
Outputs:
- interior: float32 [64, 49, 2048], P('mode', None, ('ex', 'ey'))
- interface: float32 [64, 8, 256], P('mode', ('ex', 'ey'))
Inputs may be any that keep to these rules, and one draw needn't show every extreme that they name: slots of one quadrilateral name unknowns of its own group. `sides`: 0 means not shared; 1 to 4 name the neighbour at +ex, -ex, +ey, -ey.
All inputs are finite; a program needn't handle non-finite values.
Results may differ from a plain program's by a relative error of at most 0.000075.
Values sent between devices are 32-bit elements; how exact they have to be, the bound alone decides.
No kernel may reach another device: no remote copies, remote signals or barrier semaphores. Data moves between devices by JAX's collectives and lax.ppermute only.
A program may use at most 64 MiB of HBM per device.

v0:
```python
import math

import jax
import jax.numpy as jnp
import numpy as np
from jax import lax
from jax.sharding import PartitionSpec as P

helm_base = 0.5
wave_unit = 1.0 / 64.0


def extended(block, sides, width):
    for axis, dim in sides:
        count = lax.axis_size(axis)
        forward = [(i, i + 1) for i in range(count - 1)]
        backward = [(target, source) for source, target in forward]
        low = lax.ppermute(
            lax.slice_in_dim(block, block.shape[dim] - width, None, axis=dim), axis, forward
        )
        high = lax.ppermute(lax.slice_in_dim(block, 0, width, axis=dim), axis, backward)
        block = jnp.concatenate([low, block, high], axis=dim)
    return block


def is_inner(node_id):
    return 1 <= node_id // 9 <= 7 and 1 <= node_id % 9 <= 7


def node_lists():
    inner_nodes = np.array([node_id for node_id in range(81) if is_inner(node_id)], dtype=np.int32)
    rim_nodes = np.array(
        [node_id for node_id in range(81) if not is_inner(node_id)], dtype=np.int32
    )
    return (inner_nodes, rim_nodes)


def wave_numbers(row_ids, count):
    return jnp.where(row_ids == 1, count // 2, row_ids // 2)


def dft_table(count):
    row_ids = jnp.arange(count, dtype=jnp.int32)
    wave_ids = wave_numbers(row_ids, count)
    phase_ids = wave_ids[:, None] * row_ids[None, :] % count
    angles = 2.0 * math.pi / count * phase_ids.astype(jnp.float32)
    odd_rows = (row_ids % 2 == 1) & (row_ids != 1)
    scales = jnp.where(row_ids <= 1, math.sqrt(1.0 / count), math.sqrt(2.0 / count)).astype(
        jnp.float32
    )
    return jnp.where(odd_rows[:, None], jnp.sin(angles), jnp.cos(angles)) * scales[:, None]


def mode_shifts(row_ids, count):
    waves = wave_numbers(row_ids, count).astype(jnp.float32) * wave_unit
    return helm_base + waves * waves


def fast_solve(values, eigen_basis, eigen_values, shifts):
    kron_basis = jnp.kron(eigen_basis, eigen_basis)
    pair_sums = (eigen_values[:, None] + eigen_values[None, :]).reshape(-1)
    spectra = jnp.einsum("ji,rje->rie", kron_basis, values, precision=lax.Precision.HIGHEST)
    spectra = spectra / (pair_sums[None, :, None] + shifts[:, None, None])
    return jnp.einsum("ij,rje->rie", kron_basis, spectra, precision=lax.Precision.HIGHEST)


def on_device(forcing, eigen_basis, eigen_values, coupling, inverse_blocks, slots, sides, partners):
    inner_nodes, rim_nodes = node_lists()
    plane_dev = forcing.shape[0]
    elem_dev = forcing.shape[2]
    unknowns = inverse_blocks.shape[1]
    modes_axis = lax.axis_size("mode")
    plane_count = modes_axis * plane_dev
    table = dft_table(plane_count)
    row_ids = lax.axis_index("mode") * plane_dev + jnp.arange(plane_dev, dtype=jnp.int32)
    shifts = mode_shifts(row_ids, plane_count)
    onehot = (slots.reshape(-1)[:, None] == jnp.arange(unknowns, dtype=jnp.int32)[None, :]).astype(
        jnp.float32
    )
    inner_width = len(inner_nodes) * elem_dev
    rim_planes = forcing[:, rim_nodes, :].reshape(plane_dev, -1)
    condensed = jnp.dot(rim_planes, onehot, precision=lax.Precision.HIGHEST)
    payload = jnp.concatenate(
        [forcing[:, inner_nodes, :].reshape(plane_dev, -1), condensed], axis=1
    )
    total_width = payload.shape[1]
    sectioned = payload.reshape(plane_dev, modes_axis, total_width // modes_axis)
    spectra = jnp.einsum(
        "rp,pkc->rkc",
        table,
        lax.all_to_all(sectioned, "mode", split_axis=1, concat_axis=0, tiled=True),
        precision=lax.Precision.HIGHEST,
    )
    spectral = lax.all_to_all(spectra, "mode", split_axis=0, concat_axis=1, tiled=True).reshape(
        plane_dev, total_width
    )
    inner_part = spectral[:, :inner_width].reshape(plane_dev, len(inner_nodes), elem_dev)
    condensed_hat = spectral[:, inner_width:]
    solved = fast_solve(inner_part, eigen_basis, eigen_values, shifts)
    coupled = jnp.einsum("ji,rie->rje", coupling, solved, precision=lax.Precision.HIGHEST)
    local_sums = condensed_hat - jnp.dot(
        coupled.reshape(plane_dev, -1), onehot, precision=lax.Precision.HIGHEST
    )
    padded = extended(local_sums.reshape(1, 1, -1), (("ex", 0), ("ey", 1)), 1)
    neighbours = (
        padded[2, 1].reshape(plane_dev, unknowns),
        padded[0, 1].reshape(plane_dev, unknowns),
        padded[1, 2].reshape(plane_dev, unknowns),
        padded[1, 0].reshape(plane_dev, unknowns),
    )
    assembled = local_sums
    for side_code, neighbour in enumerate(neighbours):
        picked = jnp.take(neighbour, partners[0], axis=1)
        assembled = assembled + jnp.where(
            (sides[0] == side_code + 1)[None, :], picked, jnp.zeros_like(picked)
        )
    interface = jnp.einsum("rst,rt->rs", inverse_blocks, assembled, precision=lax.Precision.HIGHEST)
    boundary = jnp.dot(interface, onehot.T, precision=lax.Precision.HIGHEST).reshape(
        plane_dev, len(rim_nodes), elem_dev
    )
    lifted = jnp.einsum("ji,rje->rie", coupling, boundary, precision=lax.Precision.HIGHEST)
    interior = solved - fast_solve(lifted, eigen_basis, eigen_values, shifts)
    return (interior, interface[:, None, :])


def solution(mesh):
    placed = (
        P("mode", None, ("ex", "ey")),
        P(),
        P(),
        P(),
        P("mode", None, None),
        P(None, ("ex", "ey")),
        P(("ex", "ey"), None),
        P(("ex", "ey"), None),
    )
    return jax.shard_map(
        on_device,
        mesh=mesh,
        in_specs=placed,
        out_specs=(P("mode", None, ("ex", "ey")), P("mode", ("ex", "ey"), None)),
        check_vma=False,
    )
```

profile of v0, /device:TPU:0, one launch (start us, length us, event | category | flops | bytes accessed | tf_op | source)
XLA Modules:
  0.0 87.3 jit_solution(13009220939497586723)
XLA Ops:
  0.6 0.8 compare_select_fusion
  2.1 0.8 copy.58
  4.9 2.7 %fusion.2 = f32[16,256]{1,0:T(8,128)S(1)} fusion(f32[16,8192]{1,0:T(8,128)S(1)} %bitcast.107, s32[8192]{0:T(1024)S(1)} %bitcast.112), kind=kOutput, calls=%fused_computation.9 | convolution fusion | flops 404750336 | bytes 573440 | tf_op jit(solution)/shard_map/dot_general | solution.py:82
  7.6 0.9 %copy.67 = f32[2,4,8,3200]{3,2,0,1:T(8,128)} copy(f32[2,4,8,3200]{3,2,1,0:T(8,128)S(1)} %bitcast.98) | data formatting | bytes 1638400 | tf_op jit(solution)/shard_map/reshape | solution.py:87
  8.6 4.2 %all-to-all-start = ((f32[16,4,3200]{2,0,1:T(8,128)}), f32[16,4,3200]{2,0,1:T(8,128)S(1)}, u32[]{:S(2)}, u32[]{:S(2)}) async-start(f32[16,4,3200]{2,0,1:T(8,128)} %bitcast.94), calls=%async_computation | async-start | bytes 1638400 | tf_op jit(solution)/shard_map/all_to_all | solution.py:91
  12.8 12.0 %all-to-all-done = f32[16,4,3200]{2,0,1:T(8,128)S(1)} async-done(((f32[16,4,3200]{2,0,1:T(8,128)}), f32[16,4,3200]{2,0,1:T(8,128)S(1)}, u32[]{:S(2)}, u32[]{:S(2)}) %all-to-all-start) | async-done | bytes 819232 | tf_op jit(solution)/shard_map/all_to_all | solution.py:91
  24.8 1.0 %convolution_bitcast_fusion = f32[64,1,3200]{2,0,1:T(8,128)S(1)} fusion(f32[64,3200]{1,0:T(8,128)S(1)} %bitcast.100, f32[64]{0:T(128)S(1)} %compare_select_fusion.2, s32[64]{0:T(128)S(1)} %compare_select_fusion.3, pred[64]{0:T(512)(128)(4,1)S(1)} %compare_and_fusion.1), kind=kOutput, calls=%fused_computation.10 | convolution fusion | flops 157351936 | bytes 1638976 | tf_op jit(solution)/shard_map/rp,pkc->rkc/dot_general | solution.py:88
  25.9 1.7 %copy.36 = f32[64,1,3200]{2,1,0:T(1,128)} copy(f32[64,1,3200]{2,0,1:T(8,128)S(1)} %convolution_bitcast_fusion) | data formatting | bytes 1638400 | tf_op jit(solution)/shard_map/rp,pkc->rkc/dot_general | solution.py:88
  27.6 3.5 %all-to-all-start.1 = ((f32[64,1,3200]{2,1,0:T(1,128)}), f32[64,1,3200]{2,1,0:T(1,128)S(1)}, u32[]{:S(2)}, u32[]{:S(2)}) async-start(f32[64,1,3200]{2,1,0:T(1,128)} %copy.36), calls=%async_computation.1 | async-start | bytes 1638400 | tf_op jit(solution)/shard_map/all_to_all | solution.py:94
  31.7 11.4 %all-to-all-done.1 = f32[64,1,3200]{2,1,0:T(1,128)S(1)} async-done(((f32[64,1,3200]{2,1,0:T(1,128)}), f32[64,1,3200]{2,1,0:T(1,128)S(1)}, u32[]{:S(2)}, u32[]{:S(2)}) %all-to-all-start.1) | async-done | bytes 819232 | tf_op jit(solution)/shard_map/all_to_all | solution.py:94
  43.5 1.1 %reshape.170 = f32[16,49,256]{2,1,0:T(8,128)} reshape(f32[16,12544]{1,0:T(8,128)S(1)} %slice.28) | data formatting | bytes 1605632 | tf_op jit(solution)/shard_map/reshape | solution.py:97
  44.6 2.1 %fusion.8 = f32[16,49,256]{2,1,0:T(8,128)S(1)} fusion(f32[16,49,256]{2,1,0:T(8,128)} %reshape.170, f32[16,49]{1,0:T(8,128)S(1)} %broadcast_add_fusion, f32[49,49]{1,0:T(8,128)S(1)} %mul.92), kind=kOutput, calls=%fused_computation.21 | convolution fusion | flops 118214656 | bytes 1618372 | tf_op jit(solution)/shard_map/ji,rje->rie/dot_general | solution.py:62
  46.7 0.9 %convolution_bitcast_fusion.3 = f32[16,49,256]{2,1,0:T(8,128)S(1)} fusion(f32[16,49,256]{2,1,0:T(8,128)S(1)} %fusion.8, f32[49,49,1]{1,0,2:T(8,128)S(1)} %reshape.235), kind=kOutput, calls=%fused_computation.19 | convolution fusion | flops 118013952 | bytes 1615236 | tf_op jit(solution)/shard_map/ij,rje->rie/dot_general | solution.py:64
  48.7 2.7 %fusion.9 = f32[16,256]{1,0:T(8,128)S(1)} fusion(f32[16,8192]{1,0:T(8,128)S(1)} %bitcast.109, s32[8192]{0:T(1024)S(1)} %bitcast.113, f32[16,12800]{1,0:T(8,128)S(1)} %bitcast.102), kind=kOutput, calls=%fused_computation.22 | convolution fusion | flops 404754432 | bytes 589824 | tf_op jit(solution)/shard_map/dot_general | solution.py:101
  51.4 4.1 %collective-permute-start.1 = (f32[1,1,4096]{2,1,0:T(1,128)S(1)}, f32[1,1,4096]{2,1,0:T(1,128)S(1)}, u32[]{:S(2)}, u32[]{:S(2)}) collective-permute-start(f32[1,1,4096]{2,1,0:T(1,128)S(1)} %reshape.172), channel_id=1, source_target_pairs={{0,4},{1,5},{2,6},{3,7},{8,12},{9,13},{10,14},{11,15},{16,20},{17,... | collective-permute-start | bytes 49160 | tf_op jit(solution)/shard_map/ppermute | solution.py:18
  55.5 1.3 %collective-permute-start = (f32[1,1,4096]{2,1,0:T(1,128)S(1)}, f32[1,1,4096]{2,1,0:T(1,128)S(1)}, u32[]{:S(2)}, u32[]{:S(2)}) collective-permute-start(f32[1,1,4096]{2,1,0:T(1,128)S(1)} %reshape.172), channel_id=1, source_target_pairs={{4,0},{5,1},{6,2},{7,3},{12,8},{13,9},{14,10},{15,11},{20,16},{21,... | collective-permute-start | bytes 49160 | tf_op jit(solution)/shard_map/ppermute | solution.py:21
  57.4 0.7 fusion.47
  58.1 3.0 %collective-permute-done = f32[1,1,4096]{2,1,0:T(1,128)S(1)} collective-permute-done((f32[1,1,4096]{2,1,0:T(1,128)S(1)}, f32[1,1,4096]{2,1,0:T(1,128)S(1)}, u32[]{:S(2)}, u32[]{:S(2)}) %collective-permute-start) | collective-permute-done | bytes 16416 | tf_op jit(solution)/shard_map/ppermute | solution.py:21
  61.1 0.7 fusion.46
  61.8 3.5 %collective-permute-start.3 = (f32[3,1,4096]{2,1,0:T(1,128)S(1)}, f32[3,1,4096]{2,1,0:T(1,128)S(1)}, u32[]{:S(2)}, u32[]{:S(2)}) collective-permute-start(f32[3,1,4096]{2,1,0:T(1,128)S(1)} %get-tuple-element.14), channel_id=1, source_target_pairs={{0,1},{1,2},{2,3},{4,5},{5,6},{6,7},{8,9},{9,10},{10,11},{12,13},{... | collective-permute-start | bytes 147464 | tf_op jit(solution)/shard_map/ppermute | solution.py:18
  65.3 1.5 %collective-permute-start.2 = (f32[3,1,4096]{2,1,0:T(1,128)S(1)}, f32[3,1,4096]{2,1,0:T(1,128)S(1)}, u32[]{:S(2)}, u32[]{:S(2)}) collective-permute-start(f32[3,1,4096]{2,1,0:T(1,128)S(1)} %get-tuple-element.14), channel_id=1, source_target_pairs={{1,0},{2,1},{3,2},{5,4},{6,5},{7,6},{9,8},{10,9},{11,10},{13,12},{... | collective-permute-start | bytes 147464 | tf_op jit(solution)/shard_map/ppermute | solution.py:21
  66.9 0.7 gather_fusion.2
  67.8 0.7 gather_fusion.3
  68.7 2.6 %collective-permute-done.2 = f32[3,1,4096]{2,1,0:T(1,128)S(1)} collective-permute-done((f32[3,1,4096]{2,1,0:T(1,128)S(1)}, f32[3,1,4096]{2,1,0:T(1,128)S(1)}, u32[]{:S(2)}, u32[]{:S(2)}) %collective-permute-start.2) | collective-permute-done | bytes 49184 | tf_op jit(solution)/shard_map/ppermute | solution.py:21
  71.5 0.7 gather_fusion.4
  72.4 0.7 gather_fusion.5
  73.2 5.7 %fusion.33 = f32[16,1,256]{2,1,0:T(1,128)S(1)} fusion(f32[16,256,256]{2,1,0:T(8,128)} %param.18, f32[16,256,1]{1,0,2:T(8,128)S(1)} %fusion.26), kind=kOutput, calls=%fused_computation.56 | convolution fusion | flops 12582912 | bytes 4227072 | tf_op jit(solution)/shard_map/rst,rt->rs/dot_general | solution.py:117
  78.9 3.7 %fusion = f32[16,8192]{1,0:T(8,128)S(1)} fusion(s32[8192]{0:T(1024)S(1)} %bitcast.114, f32[16,1,256]{2,1,0:T(1,128)S(1)} %fusion.33), kind=kOutput, calls=%fused_computation.7 | convolution fusion | flops 404750336 | bytes 573440 | tf_op jit(solution)/shard_map/dot_general | solution.py:118
  83.4 0.9 %convolution_bitcast_fusion.1 = f32[16,49,256]{2,1,0:T(8,128)S(1)} fusion(f32[16,32,256]{2,1,0:T(8,128)S(1)} %bitcast.105, f32[32,49]{1,0:T(8,128)S(1)} %copy-done.1), kind=kOutput, calls=%fused_computation.14 | convolution fusion | flops 77070336 | bytes 1333376 | tf_op jit(solution)/shard_map/ji,rje->rie/dot_general | solution.py:121
  84.3 0.9 %fusion.7 = f32[16,49,256]{2,1,0:T(8,128)S(1)} fusion(f32[16,49,256]{2,1,0:T(8,128)S(1)} %convolution_bitcast_fusion.1, f32[16,49]{1,0:T(8,128)S(1)} %broadcast_add_fusion, f32[49,49]{1,0:T(8,128)S(1)} %mul.92), kind=kOutput, calls=%fused_computation.18 | convolution fusion | flops 118214656 | bytes 1618372 | tf_op jit(solution)/shard_map/ji,rje->rie/dot_general | solution.py:62
  85.2 0.9 %fusion.6 = f32[16,49,256]{2,1,0:T(8,128)S(1)} fusion(f32[16,49,256]{2,1,0:T(8,128)S(1)} %convolution_bitcast_fusion.3, f32[16,49,256]{2,1,0:T(8,128)S(1)} %fusion.7, f32[49,49,1]{1,0,2:T(8,128)S(1)} %reshape.235), kind=kOutput, calls=%fused_computation.16 | convolution fusion | flops 118214656 | bytes 2418052 | tf_op jit(solution)/shard_map/ij,rje->rie/dot_general | solution.py:64
  86.1 1.1 %copy.48 = f32[16,49,256]{2,0,1:T(8,128)} copy(f32[16,49,256]{2,1,0:T(8,128)S(1)} %fusion.6) | data formatting | bytes 1605632
  (59 shorter events, 6.9 us)
Async XLA Ops:
  0.6 2.9 %copy-start = (f32[16,81,256]{2,0,1:T(8,128)S(1)}, f32[16,81,256]{2,0,1:T(8,128)}, u32[]{:S(2)}) copy-start(f32[16,81,256]{2,0,1:T(8,128)} %param.14) | copy-start | bytes 3981316
  7.6 23.5 %copy-start.2 = (f32[7,7]{1,0:T(8,128)S(1)}, f32[7,7]{1,0:T(8,128)}, u32[]{:S(2)}) copy-start(f32[7,7]{1,0:T(8,128)} %param.15) | copy-start | bytes 592
  7.6 23.8 %copy-start.3 = (f32[7]{0:T(128)S(1)}, f32[7]{0:T(128)}, u32[]{:S(2)}) copy-start(f32[7]{0:T(128)} %param.16) | copy-start | bytes 88
  8.6 16.2 %all-to-all-start = ((f32[16,4,3200]{2,0,1:T(8,128)}), f32[16,4,3200]{2,0,1:T(8,128)S(1)}, u32[]{:S(2)}, u32[]{:S(2)}) async-start(f32[16,4,3200]{2,0,1:T(8,128)} %bitcast.94), calls=%async_computation | async-start | bytes 1638400 | tf_op jit(solution)/shard_map/all_to_all | solution.py:91
  27.6 15.5 %all-to-all-start.1 = ((f32[64,1,3200]{2,1,0:T(1,128)}), f32[64,1,3200]{2,1,0:T(1,128)S(1)}, u32[]{:S(2)}, u32[]{:S(2)}) async-start(f32[64,1,3200]{2,1,0:T(1,128)} %copy.36), calls=%async_computation.1 | async-start | bytes 1638400 | tf_op jit(solution)/shard_map/all_to_all | solution.py:94
  43.4 4.2 %copy-start.1 = (f32[32,49]{1,0:T(8,128)S(1)}, f32[32,49]{1,0:T(8,128)}, u32[]{:S(2)}) copy-start(f32[32,49]{1,0:T(8,128)} %param.17) | copy-start | bytes 18820
  44.6 10.9 %copy-start.5 = (s32[1,256]{1,0:T(1,128)S(1)}, s32[1,256]{1,0:T(1,128)}, u32[]{:S(2)}) copy-start(s32[1,256]{1,0:T(1,128)} %param.21) | copy-start | bytes 3076
  46.7 18.6 %copy-start.4 = (s32[1,256]{1,0:T(1,128)S(1)}, s32[1,256]{1,0:T(1,128)}, u32[]{:S(2)}) copy-start(s32[1,256]{1,0:T(1,128)} %param.20) | copy-start | bytes 3076
  51.4 5.5 %collective-permute-start.1 = (f32[1,1,4096]{2,1,0:T(1,128)S(1)}, f32[1,1,4096]{2,1,0:T(1,128)S(1)}, u32[]{:S(2)}, u32[]{:S(2)}) collective-permute-start(f32[1,1,4096]{2,1,0:T(1,128)S(1)} %reshape.172), channel_id=1, source_target_pairs={{0,4},{1,5},{2,6},{3,7},{8,12},{9,13},{10,14},{11,15},{16,20},{17,... | collective-permute-start | bytes 49160 | tf_op jit(solution)/shard_map/ppermute | solution.py:18
  55.5 5.6 %collective-permute-start = (f32[1,1,4096]{2,1,0:T(1,128)S(1)}, f32[1,1,4096]{2,1,0:T(1,128)S(1)}, u32[]{:S(2)}, u32[]{:S(2)}) collective-permute-start(f32[1,1,4096]{2,1,0:T(1,128)S(1)} %reshape.172), channel_id=1, source_target_pairs={{4,0},{5,1},{6,2},{7,3},{12,8},{13,9},{14,10},{15,11},{20,16},{21,... | collective-permute-start | bytes 49160 | tf_op jit(solution)/shard_map/ppermute | solution.py:21
  61.8 6.8 %collective-permute-start.3 = (f32[3,1,4096]{2,1,0:T(1,128)S(1)}, f32[3,1,4096]{2,1,0:T(1,128)S(1)}, u32[]{:S(2)}, u32[]{:S(2)}) collective-permute-start(f32[3,1,4096]{2,1,0:T(1,128)S(1)} %get-tuple-element.14), channel_id=1, source_target_pairs={{0,1},{1,2},{2,3},{4,5},{5,6},{6,7},{8,9},{9,10},{10,11},{12,13},{... | collective-permute-start | bytes 147464 | tf_op jit(solution)/shard_map/ppermute | solution.py:18
  65.3 6.0 %collective-permute-start.2 = (f32[3,1,4096]{2,1,0:T(1,128)S(1)}, f32[3,1,4096]{2,1,0:T(1,128)S(1)}, u32[]{:S(2)}, u32[]{:S(2)}) collective-permute-start(f32[3,1,4096]{2,1,0:T(1,128)S(1)} %get-tuple-element.14), channel_id=1, source_target_pairs={{1,0},{2,1},{3,2},{5,4},{6,5},{7,6},{9,8},{10,9},{11,10},{13,12},{... | collective-permute-start | bytes 147464 | tf_op jit(solution)/shard_map/ppermute | solution.py:21
where the time goes:
time: 87.8 us; the launch traced here: 87.3 us
  waiting for transfers between devices  29.1 us (33%)
  matrix products  22.2 us (25%)
  starting transfers between devices  18.1 us (21%)
  local copies, waits for them, and re-layouts  14.4 us (16%)
  other arithmetic  2.48 us (3%)
  between operations  1.05 us (1%)
    all_to_all x1, waiting for transfers between devices, on_device(): lax.all_to_all(sectioned, 'mode', split_axis=1, concat_axis=0, tiled=True)  12 us
    all_to_all x1, waiting for transfers between devices, on_device(): lax.all_to_all(spectra, 'mode', split_axis=0, concat_axis=1, tiled=True)  11.4 us
    ppermute x2, starting transfers between devices, extended(): lax.ppermute(lax.slice_in_dim(block, block.shape[dim] - width, None, axis...  7.56 us
    dot_general x1, matrix products, on_device(): jnp.einsum('rst,rt->rs', inverse_blocks, assembled, precision=lax.Precisi...  5.66 us
    ppermute x2, waiting for transfers between devices, extended(): lax.ppermute(lax.slice_in_dim(block, 0, width, axis=dim), axis, backward)  5.61 us
    all_to_all x1, starting transfers between devices, on_device(): lax.all_to_all(sectioned, 'mode', split_axis=1, concat_axis=0, tiled=True)  4.24 us
    dot_general x1, matrix products, on_device(): jnp.dot(interface, onehot.T, precision=lax.Precision.HIGHEST)  3.7 us
    all_to_all x1, starting transfers between devices, on_device(): lax.all_to_all(spectra, 'mode', split_axis=0, concat_axis=1, tiled=True)  3.5 us
  transfers between devices with their start and end apart: 6, of which 5 were waited for; matrix products, arithmetic and copies ran while one was open for 4% of the time, Pallas kernels for 0%

commit v1 on v0

--- a/solution.py
+++ b/solution.py
@@ -1,13 +1,427 @@
+import functools
 import math
 
 import jax
 import jax.numpy as jnp
 import numpy as np
 from jax import lax
+from jax.experimental import pallas as pl
+from jax.experimental.pallas import tpu as pltpu
 from jax.sharding import PartitionSpec as P
 
 helm_base = 0.5
 wave_unit = 1.0 / 64.0
+f32, bf16 = jnp.float32, jnp.bfloat16
+TILE = 8
+CORES = 2
+RAW_TILES = 2
+
+
+def is_inner(node_id):
+    return 1 <= node_id // 9 <= 7 and 1 <= node_id % 9 <= 7
+
+
+def node_lists():
+    inner_nodes = np.array([node_id for node_id in range(81) if is_inner(node_id)], dtype=np.int32)
+    rim_nodes = np.array(
+        [node_id for node_id in range(81) if not is_inner(node_id)], dtype=np.int32
+    )
+    return (inner_nodes, rim_nodes)
+
+
+def wave_ids(count):
+    rows = np.arange(count)
+    return np.where(rows == 1, count // 2, rows // 2)
+
+
+def table_np(count):
+    rows = np.arange(count)
+    angles = 2.0 * math.pi / count * (wave_ids(count)[:, None] * rows[None, :] % count)
+    odd = (rows % 2 == 1) & (rows != 1)
+    scales = np.where(rows <= 1, math.sqrt(1.0 / count), math.sqrt(2.0 / count))
+    return np.where(odd[:, None], np.sin(angles), np.cos(angles)) * scales[:, None]
+
+
+def split_np(table):
+    high = table.astype(np.float32).astype(jnp.bfloat16)
+    low = (table - high.astype(np.float64)).astype(np.float32).astype(jnp.bfloat16)
+    return np.stack([high, low])
+
+
+def pair_tables(count, share):
+    table = table_np(count)
+    devices = count // share
+    near, far, shifts = [], [], []
+    for dev in range(devices):
+        rows = lambda d: slice(d * share, (d + 1) * share)
+        mate, across = dev ^ 1, dev ^ CORES
+        order = lambda d: np.concatenate([table[:, rows(d)], table[:, rows(d ^ 1)]], axis=1)
+        chip, other = order(dev), order(across)
+        near.append(np.concatenate([chip[rows(across)], chip[rows(dev)]]))
+        far.append(other[rows(dev)])
+        shifts.append((wave_ids(count)[rows(dev)] * wave_unit) ** 2 + helm_base)
+    return np.stack(near), np.stack(far), np.stack(shifts)
+
+
+def split(values):
+    high = values.astype(bf16)
+    return high, (values - high.astype(f32)).astype(bf16)
+
+
+def dot(left, right):
+    return jnp.dot(left, right, preferred_element_type=f32)
+
+
+def dot_t(left, right):
+    return lax.dot_general(left, right, (((1,), (1,)), ((), ())), preferred_element_type=f32)
+
+
+def dot3(left_parts, right):
+    stacked, high = left_parts
+    right_high, right_low = split(right)
+    both = dot(stacked, right_high)
+    rows = high.shape[0]
+    return both[:rows] + both[rows:] + dot(high, right_low)
+
+
+def stacked(matrix):
+    high, low = split(matrix)
+    return jnp.concatenate([high, low], axis=0), high
+
+
+def iota(shape, dim):
+    return lax.broadcasted_iota(jnp.int32, shape, dim)
+
+
+def digits(index, base, most):
+    lead = jnp.zeros_like(index)
+    for step in range(1, most):
+        lead = lead + (index >= step * base).astype(jnp.int32)
+    return lead, index - lead * base
+
+
+def spread(basis_ref, row_digit, col_digit, flip):
+    size = basis_ref.shape[0]
+    out = jnp.zeros(jnp.broadcast_shapes(row_digit.shape, col_digit.shape), f32)
+    for c in range(size):
+        line = jnp.zeros(col_digit.shape, f32)
+        for a in range(size):
+            entry = basis_ref[c, a] if flip else basis_ref[a, c]
+            line = jnp.where(col_digit == a, entry, line)
+        out = jnp.where(row_digit == c, line, out)
+    return out
+
+
+def kron_rows(basis_ref, rows, nodes, all_nodes, flip=False, first=0):
+    size = basis_ref.shape[0]
+    row_ids = iota((rows, 1), 0) + first
+    c, d = digits(row_ids, size, size + 2)
+    col_ids = iota((1, nodes), 1)
+    if all_nodes:
+        a, b = digits(col_ids, size + 2, size + 2)
+        a, b = a - 1, b - 1
+    else:
+        a, b = digits(col_ids, size, size + 2)
+    b = jnp.where((a >= 0) & (a < size), b, -1)
+    d = jnp.where(c < size, d, -1)
+    return spread(basis_ref, c, a, flip) * spread(basis_ref, d, b, flip)
+
+
+def member(slots_row, unknowns):
+    ids = iota((unknowns, slots_row.shape[1]), 0)
+    return jnp.where(ids == slots_row, 1.0, 0.0).astype(bf16)
+
+
+def stack_split(values):
+    high, low = split(values)
+    return jnp.concatenate([high, low], axis=0)
+
+
+def fold(values):
+    half = values.shape[0] // 2
+    return values[:half] + values[half:]
+
+
+def raw_kernel(forcing, basis, out):
+    rows = out.shape[1]
+    lift = stacked(kron_rows(basis, rows, forcing.shape[1], True))
+    for plane in range(forcing.shape[0]):
+        out[plane] = dot3(lift, forcing[plane])
+
+
+def near_kernel(dev, own, mate, basis, slots, near, small, out, mid, rem, raw, lifted, *, rim_nodes, inner):
+    share, nodes, elems = own.shape
+    rows = lifted.shape[1]
+    unknowns = out.shape[1]
+    raw_rows = raw.shape[1]
+    mid_rows = mid.shape[1]
+    lift = stacked(kron_rows(basis, rows, nodes, True))
+    for part, source in enumerate((own, mate)):
+        for plane in range(share):
+            lifted[part * share + plane] = dot3(lift, source[plane])
+    total = jnp.zeros((4 * share, unknowns), f32)
+    for j, node in enumerate(rim_nodes):
+        both = jnp.concatenate([own[:, int(node), :], mate[:, int(node), :]], axis=0)
+        total = total + dot_t(stack_split(both), member(slots[j : j + 1, :], unknowns))
+    condensed = fold(total)
+    near_high, near_low = near[0], near[1]
+    near_parts = jnp.concatenate([near_high, near_low], axis=0), near_high
+    half = share * TILE
+    for tile in range((raw_rows + mid_rows) // TILE):
+        block = lifted[:, tile * TILE : (tile + 1) * TILE, :].reshape(2 * share * TILE, elems)
+        if tile * TILE < raw_rows:
+            parts = jnp.concatenate([near_high[half:], near_low[half:]], axis=0), near_high[half:]
+            raw[:, tile * TILE : (tile + 1) * TILE, :] = dot3(parts, block).reshape(share, TILE, elems)
+        else:
+            spectra = dot3(near_parts, block)
+            place = slice(tile * TILE - raw_rows, (tile + 1) * TILE - raw_rows)
+            out_rows = spectra[:half].reshape(share, TILE, elems)
+            for r in range(share):
+                out[r * mid_rows + place.start : r * mid_rows + place.stop, :] = out_rows[r]
+            mid[:, place, :] = spectra[half:].reshape(share, TILE, elems)
+    small_parts = jnp.concatenate([small[0], small[1]], axis=0), small[0]
+    tail = [lifted[:, row, :] for row in range(raw_rows + mid_rows, inner)] + [condensed]
+    for i, block in enumerate(tail):
+        spectra = dot3(small_parts, block)
+        start = share * (mid_rows + i)
+        out[start : start + share, :] = spectra[:share]
+        rem[i] = spectra[share:]
+
+
+def far_kernel(dev, raw, first, second, far, out):
+    share, rows, elems = raw.shape
+    parts = jnp.concatenate([far[0], far[1]], axis=0), far[0]
+    for tile in range(rows // TILE):
+        place = slice(tile * TILE, (tile + 1) * TILE)
+        block = jnp.concatenate([first[:, place, :], second[:, place, :]], axis=0)
+        block = block.reshape(2 * share * TILE, elems)
+        out[:, place, :] = raw[:, place, :] + dot3(parts, block).reshape(share, TILE, elems)
+
+
+def inverse_diagonal(values, shifts, mode, rows, lanes):
+    size = values.shape[0]
+    c, d = digits(iota((rows, lanes), 0), size, size + 2)
+    total = jnp.zeros((rows, lanes), f32)
+    for i in range(size):
+        total = total + jnp.where(c == i, values[i], 0.0) + jnp.where(d == i, values[i], 0.0)
+    return 1.0 / (total + shifts[mode])
+
+
+def solve_kernel(raw, mid, rem, received, shifts, basis, values, coupling, slots, spectral, sums, coupled):
+    share, mid_rows, elems = mid.shape
+    raw_rows = raw.shape[1]
+    rows = spectral.shape[1]
+    rim, inner = coupling.shape
+    unknowns = sums.shape[1]
+    split_at = raw_rows + mid_rows
+    for r in range(share):
+        spectral[r, :raw_rows, :] = raw[r]
+        spectral[r, raw_rows:split_at, :] = mid[r] + received[r * mid_rows : (r + 1) * mid_rows, :]
+    spectral[:, split_at:, :] = jnp.zeros((share, rows - split_at, elems), f32)
+    remaining = inner - split_at
+    for i in range(remaining):
+        start = share * (mid_rows + i)
+        spectral[:, split_at + i, :] = rem[i] + received[start : start + share, :]
+    start = share * (mid_rows + remaining)
+    condensed = rem[remaining] + received[start : start + share, :]
+    lift = kron_rows(basis, inner, rows, False, flip=True)
+    couple = stacked(jnp.dot(coupling[...], lift, precision=lax.Precision.HIGHEST, preferred_element_type=f32))
+    for r in range(share):
+        inverse = inverse_diagonal(values, shifts, r, rows, 128)
+        inverse = jnp.concatenate([inverse] * (elems // 128), axis=1)
+        coupled[r] = dot3(couple, spectral[r] * inverse)
+    total = jnp.zeros((2 * share, unknowns), f32)
+    for j in range(rim):
+        total = total + dot_t(stack_split(coupled[:, j, :]), member(slots[j : j + 1, :], unknowns))
+    sums[...] = condensed - fold(total)
+
+
+def back_kernel(*refs, neighbours):
+    sums, near = refs[0], refs[1 : 1 + neighbours]
+    codes, sides, partners, inverse, slots, spectral, shifts, basis, values, coupling = refs[1 + neighbours : 11 + neighbours]
+    interior, interface, boundary = refs[11 + neighbours :]
+    share, unknowns = sums.shape
+    rows, elems = spectral.shape[1:]
+    rim, inner = coupling.shape
+    pick = member(partners[...], unknowns)
+    stack = jnp.concatenate([part for ref in near for part in split(ref[...])], axis=0)
+    picked = dot(stack, pick)
+    assembled = sums[...]
+    for i in range(neighbours):
+        block = picked[2 * share * i : 2 * share * (i + 1)]
+        assembled = assembled + jnp.where(sides[...] == codes[i], fold(block), 0.0)
+    asm_high, asm_low = split(assembled)
+    lines = []
+    for r in range(share):
+        inv_high, inv_low = split(inverse[r])
+        full = dot_t(jnp.concatenate([asm_high, asm_low], axis=0), inv_high)
+        product = full[:share] + full[share:] + dot_t(asm_high, inv_low)
+        lines.append(product[r : r + 1])
+    solved = jnp.concatenate(lines, axis=0)
+    interface[...] = solved
+    solved_parts = stack_split(solved)
+    for j in range(rim):
+        boundary[:, j, :] = fold(dot(solved_parts, member(slots[j : j + 1, :], unknowns)))
+    lift = kron_rows(basis, inner, rows, False, flip=True)
+    couple = jnp.dot(coupling[...], lift, precision=lax.Precision.HIGHEST, preferred_element_type=f32)
+    couple_t = stacked(couple.T)
+    lift_parts = stacked(jnp.concatenate([lift, jnp.zeros((rows - inner, rows), f32)], axis=0))
+    for r in range(share):
+        pull = dot3(couple_t, boundary[r])
+        inverse_d = inverse_diagonal(values, shifts, r, rows, 128)
+        inverse_d = jnp.concatenate([inverse_d] * (elems // 128), axis=1)
+        interior[r] = dot3(lift_parts, (spectral[r] - pull) * inverse_d)[:inner]
+
+
+VMEM = pl.BlockSpec(memory_space=pltpu.VMEM)
+SMEM = pl.BlockSpec(memory_space=pltpu.SMEM)
+
+
+def params():
+    return pltpu.CompilerParams(vmem_limit_bytes=48 * 2**20)
+
+
+def shape(*dims):
+    return jax.ShapeDtypeStruct(dims, f32)
+
+
+def swaps(block, axis):
+    count = lax.axis_size(axis)
+    even = 1 - lax.axis_index(axis) % 2
+    got = []
+    for first in range(2):
+        pairs = [(i, i + 1) for i in range(first, count - 1, 2)]
+        if pairs:
+            moves = pairs + [(b, a) for a, b in pairs]
+            ahead = even if first == 0 else 1 - even
+            got.append((lax.ppermute(block, axis, moves), 1 - ahead))
+    return got
+
+
+def paired(forcing, eigen_basis, eigen_values, coupling, inverse_blocks, slots, sides, partners):
+    inner_nodes, rim_nodes = node_lists()
+    share, nodes, elems = forcing.shape
+    unknowns = inverse_blocks.shape[1]
+    modes = lax.axis_size("mode")
+    inner, rim = len(inner_nodes), len(rim_nodes)
+    rows = -(-inner // TILE) * TILE
+    raw_rows = RAW_TILES * TILE
+    mid_rows = inner // TILE * TILE - raw_rows
+    remaining = inner - raw_rows - mid_rows
+    me = lax.axis_index("mode")
+    near, far, shift_table = pair_tables(modes * share, share)
+    eye = np.eye(TILE)
+    near_big = np.stack([split_np(np.kron(t, eye)) for t in near])
+    near_small = np.stack([split_np(t) for t in near])
+    far_big = np.stack([split_np(np.kron(t, eye)) for t in far])
+    shifts = lax.dynamic_index_in_dim(jnp.asarray(shift_table, f32), me, 0, keepdims=False)
+    index = me.reshape(1).astype(jnp.int32)
+
+    mates = [(i, i ^ 1) for i in range(modes)]
+    across = [(i, i ^ CORES) for i in range(modes)]
+
+    mate_forcing = lax.ppermute(forcing, "mode", mates)
+    raw_out = pl.pallas_call(
+        raw_kernel,
+        out_shape=shape(share, raw_rows, elems),
+        in_specs=[VMEM, SMEM],
+        out_specs=VMEM,
+        compiler_params=params(),
+        name="raw_rows",
+    )(forcing, eigen_basis)
+    raw_first = lax.ppermute(raw_out, "mode", across)
+
+    def mine(*dims):
+        return pl.BlockSpec((None,) + dims, lambda i, dev: (dev[0],) + (0,) * len(dims))
+
+    def whole(*dims):
+        return pl.BlockSpec(dims, lambda i, dev: (0,) * len(dims))
+
+    big, small = near_big.shape[1:], near_small.shape[1:]
+    out_rows = share * (mid_rows + remaining + 1)
+    smem_grid = pl.BlockSpec(memory_space=pltpu.SMEM)
+    send, mid, rem, raw_near = pl.pallas_call(
+        functools.partial(near_kernel, rim_nodes=rim_nodes, inner=inner),
+        out_shape=(
+            shape(out_rows, elems),
+            shape(share, mid_rows, elems),
+            shape(remaining + 1, share, elems),
+            shape(share, raw_rows, elems),
+        ),
+        grid_spec=pltpu.PrefetchScalarGridSpec(
+            num_scalar_prefetch=1,
+            grid=(1,),
+            in_specs=[
+                whole(*forcing.shape),
+                whole(*forcing.shape),
+                smem_grid,
+                whole(*slots.shape),
+                mine(*big),
+                mine(*small),
+            ],
+            out_specs=(
+                whole(out_rows, elems),
+                whole(share, mid_rows, elems),
+                whole(remaining + 1, share, elems),
+                whole(share, raw_rows, elems),
+            ),
+            scratch_shapes=[pltpu.VMEM((2 * share, rows, elems), f32)],
+        ),
+        compiler_params=params(),
+        name="near_spectra",
+    )(index, forcing, mate_forcing, eigen_basis, slots, jnp.asarray(near_big), jnp.asarray(near_small))
+    received = lax.ppermute(send, "mode", across)
+
+    raw_second = lax.ppermute(raw_first, "mode", mates)
+    raw = pl.pallas_call(
+        far_kernel,
+        out_shape=shape(share, raw_rows, elems),
+        grid_spec=pltpu.PrefetchScalarGridSpec(
+            num_scalar_prefetch=1,
+            grid=(1,),
+            in_specs=[whole(share, raw_rows, elems)] * 3 + [mine(*far_big.shape[1:])],
+            out_specs=whole(share, raw_rows, elems),
+        ),
+        compiler_params=params(),
+        name="far_spectra",
+    )(index, raw_near, raw_first, raw_second, jnp.asarray(far_big))
+
+    spectral, sums = pl.pallas_call(
+        solve_kernel,
+        out_shape=(shape(share, rows, elems), shape(share, unknowns)),
+        in_specs=[VMEM] * 4 + [SMEM] * 3 + [VMEM] * 2,
+        out_specs=(VMEM, VMEM),
+        scratch_shapes=[pltpu.VMEM((share, rim, elems), f32)],
+        compiler_params=params(),
+        name="residual",
+    )(raw, mid, rem, received, shifts, eigen_basis, eigen_values, coupling, slots)
+
+    got = [(block, 1 + back) for block, back in swaps(sums, "ex")]
+    got += [(block, 3 + back) for block, back in swaps(sums, "ey")]
+    codes = jnp.stack([jnp.asarray(code, jnp.int32) for _, code in got])
+    interior, interface = pl.pallas_call(
+        functools.partial(back_kernel, neighbours=len(got)),
+        out_shape=(shape(share, inner, elems), shape(share, unknowns)),
+        in_specs=[VMEM] * (1 + len(got)) + [SMEM] + [VMEM] * 5 + [SMEM] * 3 + [VMEM],
+        out_specs=(VMEM, VMEM),
+        scratch_shapes=[pltpu.VMEM((share, rim, elems), f32)],
+        compiler_params=params(),
+        name="back_solve",
+    )(
+        sums,
+        *[block for block, _ in got],
+        codes,
+        sides,
+        partners,
+        inverse_blocks,
+        slots,
+        spectral,
+        shifts,
+        eigen_basis,
+        eigen_values,
+        coupling,
+    )
+    return (interior, interface[:, None, :])
 
 
 def extended(block, sides, width):
@@ -23,18 +437,6 @@
     return block
 
 
-def is_inner(node_id):
-    return 1 <= node_id // 9 <= 7 and 1 <= node_id % 9 <= 7
-
-
-def node_lists():
-    inner_nodes = np.array([node_id for node_id in range(81) if is_inner(node_id)], dtype=np.int32)
-    rim_nodes = np.array(
-        [node_id for node_id in range(81) if not is_inner(node_id)], dtype=np.int32
-    )
-    return (inner_nodes, rim_nodes)
-
-
 def wave_numbers(row_ids, count):
     return jnp.where(row_ids == 1, count // 2, row_ids // 2)
 
@@ -64,7 +466,7 @@
     return jnp.einsum("ij,rje->rie", kron_basis, spectra, precision=lax.Precision.HIGHEST)
 
 
-def on_device(forcing, eigen_basis, eigen_values, coupling, inverse_blocks, slots, sides, partners):
+def general(forcing, eigen_basis, eigen_values, coupling, inverse_blocks, slots, sides, partners):
     inner_nodes, rim_nodes = node_lists()
     plane_dev = forcing.shape[0]
     elem_dev = forcing.shape[2]
@@ -123,6 +525,13 @@
     return (interior, interface[:, None, :])
 
 
+def on_device(*args):
+    modes = lax.axis_size("mode")
+    if modes == CORES * CORES:
+        return paired(*args)
+    return general(*args)
+
+
 def solution(mesh):
     placed = (
         P("mode", None, ("ex", "ey")),

time: 87.8 us -> 56 us (0.64)
  the two profiles are of different devices: /device:TPU:0 before, /device:TPU:16 now
where the time goes in v1:
time: 56 us; the launch traced here: 55.8 us
  waiting for transfers between devices  23 us (41%)
  Pallas kernels  15.8 us (28%)
  local copies, waits for them, and re-layouts  8.86 us (16%)
  starting transfers between devices  7.28 us (13%)
  between operations  0.78 us (1%)
    ppermute x1, waiting for transfers between devices, paired(): raw_first = lax.ppermute(raw_out, 'mode', across)  17.5 us
    pallas_call x1, Pallas kernels, paired(): pl.pallas_call(functools.partial(back_kernel, neighbours=len(got)), out_s...  6.46 us
    unnamed x23, local copies, waits for them, and re-layouts  6.08 us
    ppermute x3, starting transfers between devices, swaps(): got.append((lax.ppermute(block, axis, moves), 1 - ahead))  5.18 us
    pallas_call x1, Pallas kernels, paired(): pl.pallas_call(functools.partial(near_kernel, rim_nodes=rim_nodes, inner=...  4.29 us
    pallas_call x1, Pallas kernels, paired(): pl.pallas_call(solve_kernel, out_shape=(shape(share, rows, elems), shape(...  3.8 us
    ppermute x3, waiting for transfers between devices, swaps(): got.append((lax.ppermute(block, axis, moves), 1 - ahead))  3.44 us
    ppermute x1, local copies, waits for them, and re-layouts, paired(): mate_forcing = lax.ppermute(forcing, 'mode', mates)  2.09 us
  transfers between devices with their start and end apart: 7, of which 4 were waited for; matrix products, arithmetic and copies ran while one was open for 5% of the time, Pallas kernels for 2%

profile of v1, /device:TPU:16, one launch (start us, length us, event | category | flops | bytes accessed | tf_op | source)
XLA Modules:
  0.0 55.8 jit_solution(14026633494643880661)
XLA Ops:
  0.6 0.1 collective-permute-start
  0.7 2.1 %copy.19.own.forcing = f32[16,81,256]{2,1,0:T(8,128)S(1)} copy(f32[16,81,256]{2,0,1:T(8,128)} %param.12) | data formatting | bytes 2654208 | tf_op args[0]
  2.8 0.0 copy-start.1
  2.8 0.0 copy-start.3
  2.8 0.0 copy-start.4
  2.8 0.0 copy-start.6
  2.9 1.2 %collective-permute-done = f32[16,81,256]{2,0,1:T(8,128)} collective-permute-done((f32[16,81,256]{2,0,1:T(8,128)}, f32[16,81,256]{2,0,1:T(8,128)}, u32[]{:S(2)}, u32[]{:S(2)}) %collective-permute-start) | collective-permute-done | bytes 1327136 | tf_op jit(solution)/shard_map/ppermute | solution.py:323
  4.1 2.1 %copy.20.mate = f32[16,81,256]{2,1,0:T(8,128)S(1)} copy(f32[16,81,256]{2,0,1:T(8,128)} %collective-permute-done) | data formatting | bytes 2654208 | tf_op jit(solution)/shard_map/ppermute | solution.py:323
  6.2 4.3 %near_spectra.1 = (f32[544,256]{1,0:T(8,128)}, f32[16,32,256]{2,1,0:T(8,128)S(1)}, f32[2,16,256]{2,1,0:T(8,128)S(1)}, f32[16,16,256]{2,1,0:T(8,128)S(1)}) custom-call(s32[1]{0:T(128)} %bitcast.dev, f32[16,81,256]{2,1,0:T(8,128)S(1)} %copy.19.own.forcing, f32[16,81,256]{2,1,0:T(8,128)S(1)} %copy.20.mate, f32[7,7]{1,0:T(8,128)S(1)} %copy-done.6, ...), custom_call_target="tpu_custom_call" | custom-call | tf_op jit(solution)/shard_map/near_spectra/pallas_call | solution.py:343
  10.5 1.5 %collective-permute-start.3 = (f32[544,256]{1,0:T(8,128)}, f32[544,256]{1,0:T(8,128)S(1)}, u32[]{:S(2)}, u32[]{:S(2)}) collective-permute-start(f32[544,256]{1,0:T(8,128)} %get-tuple-element.13), channel_id=1, source_target_pairs={{0,16},{8,24},{16,0},{24,8},{1,17},{9,25},{17,1},{25,9},{2,18},{10... | collective-permute-start | bytes 1671176 | tf_op jit(solution)/shard_map/ppermute | solution.py:373
  12.1 1.0 %raw_rows.1 = f32[16,16,256]{2,1,0:T(8,128)S(1)} custom-call(f32[16,81,256]{2,1,0:T(8,128)S(1)} %copy.19.own.forcing, f32[7,7]{1,0:T(8,128)S(1)} %copy-done.6), custom_call_target="tpu_custom_call" | custom-call | tf_op jit(solution)/shard_map/raw_rows/pallas_call | solution.py:324
  13.0 0.5 collective-permute-start.1
  13.6 17.5 %collective-permute-done.1.first = f32[16,16,256]{2,1,0:T(8,128)S(1)} collective-permute-done((f32[16,16,256]{2,1,0:T(8,128)S(1)}, f32[16,16,256]{2,1,0:T(8,128)S(1)}, u32[]{:S(2)}, u32[]{:S(2)}) %collective-permute-start.1) | collective-permute-done | bytes 262176 | tf_op jit(solution)/shard_map/ppermute | solution.py:332
  31.0 0.0 collective-permute-start.2
  31.0 0.7 %dynamic-slice_bitcast_fusion.shifts.refs_10_ = f32[16]{0:T(128)S(1)} fusion(f32[4,16]{1,0:T(4,128)} %constant.46.clone, s32[]{:T(128)S(6)} %select_n.15), kind=kLoop, calls=%fused_computation.1 | loop fusion | bytes 132 | tf_op jit(solution)/shard_map/jit(dynamic_index_in_dim)/squeeze | solution.py:317
  31.7 0.8 %collective-permute-done.2.second = f32[16,16,256]{2,1,0:T(8,128)S(1)} collective-permute-done((f32[16,16,256]{2,1,0:T(8,128)S(1)}, f32[16,16,256]{2,1,0:T(8,128)S(1)}, u32[]{:S(2)}, u32[]{:S(2)}) %collective-permute-start.2) | collective-permute-done | bytes 262176 | tf_op jit(solution)/shard_map/ppermute | solution.py:375
  32.6 0.0 copy-done.2
  32.6 0.3 far_spectra.1.raw
  32.9 0.0 collective-permute-done.3.received
  32.9 3.8 %residual.1 = (f32[16,56,256]{2,1,0:T(8,128)S(1)}, f32[16,256]{1,0:T(8,128)S(1)}) custom-call(f32[16,16,256]{2,1,0:T(8,128)S(1)} %far_spectra.1.raw, f32[16,32,256]{2,1,0:T(8,128)S(1)} %get-tuple-element.11.mid, f32[2,16,256]{2,1,0:T(8,128)S(1)} %get-tuple-element.12.rem, f32[544,256]{1,0:T(8,128)S(1)} %collective-permute-done.3.received, ...), custom_call_target="tpu_custom_call" | custom-call | tf_op jit(solution)/shard_map/residual/pallas_call | solution.py:389
  36.7 1.5 %collective-permute-start.4 = (f32[16,256]{1,0:T(8,128)S(1)}, f32[16,256]{1,0:T(8,128)S(1)}, u32[]{:S(2)}, u32[]{:S(2)}) collective-permute-start(f32[16,256]{1,0:T(8,128)S(1)} %get-tuple-element.14.refs_0_), channel_id=1, source_target_pairs={{0,4},{4,0},{1,5},{5,1},{2,6},{6,2},{3,7},{7,3},{8,12},{12,8},{9,1... | collective-permute-start | bytes 49160 | tf_op jit(solution)/shard_map/ppermute | solution.py:297
  38.2 1.6 %collective-permute-start.5 = (f32[16,256]{1,0:T(8,128)S(1)}, f32[16,256]{1,0:T(8,128)S(1)}, u32[]{:S(2)}, u32[]{:S(2)}) collective-permute-start(f32[16,256]{1,0:T(8,128)S(1)} %get-tuple-element.14.refs_0_), channel_id=1, source_target_pairs={{0,1},{2,3},{1,0},{3,2},{4,5},{6,7},{5,4},{7,6},{8,9},{10,11},{9,8... | collective-permute-start | bytes 49160 | tf_op jit(solution)/shard_map/ppermute | solution.py:297
  39.8 2.1 %collective-permute-start.6 = (f32[16,256]{1,0:T(8,128)S(1)}, f32[16,256]{1,0:T(8,128)S(1)}, u32[]{:S(2)}, u32[]{:S(2)}) collective-permute-start(f32[16,256]{1,0:T(8,128)S(1)} %get-tuple-element.14.refs_0_), channel_id=1, source_target_pairs={{1,2},{2,1},{5,6},{6,5},{9,10},{10,9},{13,14},{14,13},{17,18},{18,... | collective-permute-start | bytes 49160 | tf_op jit(solution)/shard_map/ppermute | solution.py:297
  41.9 0.1 pad_add_fusion.refs_4_
  41.9 0.0 collective-permute-done.4.refs_1_
  41.9 0.0 collective-permute-done.5.refs_2_
  42.0 3.4 %collective-permute-done.6.refs_3_ = f32[16,256]{1,0:T(8,128)S(1)} collective-permute-done((f32[16,256]{1,0:T(8,128)S(1)}, f32[16,256]{1,0:T(8,128)S(1)}, u32[]{:S(2)}, u32[]{:S(2)}) %collective-permute-start.6) | collective-permute-done | bytes 16416 | tf_op jit(solution)/shard_map/ppermute | solution.py:297
  45.4 0.0 copy-done.9
  45.4 2.2 %copy-done = f32[16,256,256]{2,1,0:T(8,128)S(1)} copy-done((f32[16,256,256]{2,1,0:T(8,128)S(1)}, f32[16,256,256]{2,1,0:T(8,128)}, u32[]{:S(2)}) %copy-start) | copy-done | bytes 4194328
  47.6 6.5 %back_solve.1 = (f32[16,49,256]{2,1,0:T(8,128)S(1)}, f32[16,256]{1,0:T(8,128)S(1)}) custom-call(f32[16,256]{1,0:T(8,128)S(1)} %get-tuple-element.14.refs_0_, f32[16,256]{1,0:T(8,128)S(1)} %collective-permute-done.4.refs_1_, f32[16,256]{1,0:T(8,128)S(1)} %collective-permute-done.5.refs_2_, f32[16,256]{1,0:T(8,128)S(1)} %collective-permute-done.6.refs_3_, ...), custom_call_target="tpu_custom_call" | custom-call | tf_op jit(solution)/shard_map/back_solve/pallas_call | solution.py:402
  54.0 1.1 %copy.22 = f32[16,49,256]{2,0,1:T(8,128)} copy(f32[16,49,256]{2,1,0:T(8,128)S(1)} %get-tuple-element.20) | data formatting | bytes 1605632
  55.2 0.6 %copy.23 = f32[16,1,256]{2,1,0:T(1,128)} copy(f32[16,1,256]{2,0,1:T(8,128)S(1)} %bitcast.7) | data formatting | bytes 32768
  (13 shorter events, 0.0 us)
Async XLA Ops:
  0.6 3.5 %collective-permute-start = (f32[16,81,256]{2,0,1:T(8,128)}, f32[16,81,256]{2,0,1:T(8,128)}, u32[]{:S(2)}, u32[]{:S(2)}) collective-permute-start(f32[16,81,256]{2,0,1:T(8,128)} %param.12), channel_id=1, source_target_pairs={{0,8},{8,0},{16,24},{24,16},{1,9},{9,1},{17,25},{25,17},{2,10},{10... | collective-permute-start | bytes 3981320 | tf_op jit(solution)/shard_map/ppermute | solution.py:323
  2.8 3.4 %copy-start.1 = (bf16[4,2,256,256]{3,2,1,0:T(8,128)(2,1)S(1)}, bf16[4,2,256,256]{3,2,1,0:T(8,128)(2,1)}, u32[]{:S(2)}) copy-start(bf16[4,2,256,256]{3,2,1,0:T(8,128)(2,1)} %constant.47.clone.near) | copy-start | bytes 3145732
  2.8 3.4 %copy-start.3 = (s32[32,256]{1,0:T(8,128)S(1)}, s32[32,256]{1,0:T(8,128)}, u32[]{:S(2)}) copy-start(s32[32,256]{1,0:T(8,128)} %refs_8_.1) | copy-start | bytes 98308
  2.8 3.4 %copy-start.4 = (bf16[4,2,32,32]{3,2,1,0:T(8,128)(2,1)S(1)}, bf16[4,2,32,32]{3,2,1,0:T(8,128)(2,1)}, u32[]{:S(2)}) copy-start(bf16[4,2,32,32]{3,2,1,0:T(8,128)(2,1)} %constant.48.clone.small) | copy-start | bytes 49156
  2.8 3.4 %copy-start.6 = (f32[7,7]{1,0:T(8,128)S(1)}, f32[7,7]{1,0:T(8,128)}, u32[]{:S(2)}) copy-start(f32[7,7]{1,0:T(8,128)} %refs_11_.1) | copy-start | bytes 592
  10.5 22.0 %copy-start.2 = (bf16[4,2,128,256]{3,2,1,0:T(8,128)(2,1)S(1)}, bf16[4,2,128,256]{3,2,1,0:T(8,128)(2,1)}, u32[]{:S(2)}) copy-start(bf16[4,2,128,256]{3,2,1,0:T(8,128)(2,1)} %constant.49.clone.far) | copy-start | bytes 1572868
  10.5 22.3 %copy-start.5 = (f32[32,49]{1,0:T(8,128)S(1)}, f32[32,49]{1,0:T(8,128)}, u32[]{:S(2)}) copy-start(f32[32,49]{1,0:T(8,128)} %refs_13_.1) | copy-start | bytes 18820
  10.5 22.3 %copy-start.7 = (f32[7]{0:T(128)S(1)}, f32[7]{0:T(128)}, u32[]{:S(2)}) copy-start(f32[7]{0:T(128)} %refs_12_.1) | copy-start | bytes 88
  10.5 22.3 %collective-permute-start.3 = (f32[544,256]{1,0:T(8,128)}, f32[544,256]{1,0:T(8,128)S(1)}, u32[]{:S(2)}, u32[]{:S(2)}) collective-permute-start(f32[544,256]{1,0:T(8,128)} %get-tuple-element.13), channel_id=1, source_target_pairs={{0,16},{8,24},{16,0},{24,8},{1,17},{9,25},{17,1},{25,9},{2,18},{10... | collective-permute-start | bytes 1671176 | tf_op jit(solution)/shard_map/ppermute | solution.py:373
  13.0 18.0 %collective-permute-start.1 = (f32[16,16,256]{2,1,0:T(8,128)S(1)}, f32[16,16,256]{2,1,0:T(8,128)S(1)}, u32[]{:S(2)}, u32[]{:S(2)}) collective-permute-start(f32[16,16,256]{2,1,0:T(8,128)S(1)} %raw_rows.1), channel_id=1, source_target_pairs={{0,16},{8,24},{16,0},{24,8},{1,17},{9,25},{17,1},{25,9},{2,18},{10... | collective-permute-start | bytes 786440 | tf_op jit(solution)/shard_map/ppermute | solution.py:332
  31.0 1.5 %collective-permute-start.2 = (f32[16,16,256]{2,1,0:T(8,128)S(1)}, f32[16,16,256]{2,1,0:T(8,128)S(1)}, u32[]{:S(2)}, u32[]{:S(2)}) collective-permute-start(f32[16,16,256]{2,1,0:T(8,128)S(1)} %collective-permute-done.1.first), channel_id=1, source_target_pairs={{0,8},{8,0},{16,24},{24,16},{1,9},{9,1},{17,25},{25,17},{2,10},{10... | collective-permute-start | bytes 786440 | tf_op jit(solution)/shard_map/ppermute | solution.py:375
  32.6 12.8 %copy-start.8 = (s32[1,256]{1,0:T(1,128)S(1)}, s32[1,256]{1,0:T(1,128)}, u32[]{:S(2)}) copy-start(s32[1,256]{1,0:T(1,128)} %refs_5_.1) | copy-start | bytes 3076
  32.6 12.8 %copy-start.9 = (s32[1,256]{1,0:T(1,128)S(1)}, s32[1,256]{1,0:T(1,128)}, u32[]{:S(2)}) copy-start(s32[1,256]{1,0:T(1,128)} %refs_6_.1) | copy-start | bytes 3076
  36.7 5.3 %collective-permute-start.4 = (f32[16,256]{1,0:T(8,128)S(1)}, f32[16,256]{1,0:T(8,128)S(1)}, u32[]{:S(2)}, u32[]{:S(2)}) collective-permute-start(f32[16,256]{1,0:T(8,128)S(1)} %get-tuple-element.14.refs_0_), channel_id=1, source_target_pairs={{0,4},{4,0},{1,5},{5,1},{2,6},{6,2},{3,7},{7,3},{8,12},{12,8},{9,1... | collective-permute-start | bytes 49160 | tf_op jit(solution)/shard_map/ppermute | solution.py:297
  38.2 3.8 %collective-permute-start.5 = (f32[16,256]{1,0:T(8,128)S(1)}, f32[16,256]{1,0:T(8,128)S(1)}, u32[]{:S(2)}, u32[]{:S(2)}) collective-permute-start(f32[16,256]{1,0:T(8,128)S(1)} %get-tuple-element.14.refs_0_), channel_id=1, source_target_pairs={{0,1},{2,3},{1,0},{3,2},{4,5},{6,7},{5,4},{7,6},{8,9},{10,11},{9,8... | collective-permute-start | bytes 49160 | tf_op jit(solution)/shard_map/ppermute | solution.py:297
  39.8 5.6 %collective-permute-start.6 = (f32[16,256]{1,0:T(8,128)S(1)}, f32[16,256]{1,0:T(8,128)S(1)}, u32[]{:S(2)}, u32[]{:S(2)}) collective-permute-start(f32[16,256]{1,0:T(8,128)S(1)} %get-tuple-element.14.refs_0_), channel_id=1, source_target_pairs={{1,2},{2,1},{5,6},{6,5},{9,10},{10,9},{13,14},{14,13},{17,18},{18,... | collective-permute-start | bytes 49160 | tf_op jit(solution)/shard_map/ppermute | solution.py:297
  45.4 2.2 %copy-start = (f32[16,256,256]{2,1,0:T(8,128)S(1)}, f32[16,256,256]{2,1,0:T(8,128)}, u32[]{:S(2)}) copy-start(f32[16,256,256]{2,1,0:T(8,128)} %refs_7_.1) | copy-start | bytes 12582916

commit v2 on v0

--- a/solution.py
+++ b/solution.py
@@ -1,13 +1,458 @@
+import functools
 import math
 
 import jax
 import jax.numpy as jnp
 import numpy as np
 from jax import lax
+from jax.experimental import pallas as pl
+from jax.experimental.pallas import tpu as pltpu
 from jax.sharding import PartitionSpec as P
 
 helm_base = 0.5
 wave_unit = 1.0 / 64.0
+f32, bf16 = jnp.float32, jnp.bfloat16
+TILE = 8
+CORES = 2
+SPAN = 256
+LIMIT = 12 * 2**20
+
+
+def is_inner(node_id):
+    return 1 <= node_id // 9 <= 7 and 1 <= node_id % 9 <= 7
+
+
+def node_lists():
+    inner_nodes = np.array([node_id for node_id in range(81) if is_inner(node_id)], dtype=np.int32)
+    rim_nodes = np.array(
+        [node_id for node_id in range(81) if not is_inner(node_id)], dtype=np.int32
+    )
+    return (inner_nodes, rim_nodes)
+
+
+def split(values):
+    high = values.astype(bf16)
+    return high, (values - high.astype(f32)).astype(bf16)
+
+
+def stack_split(values):
+    return jnp.concatenate(split(values), axis=0)
+
+
+def dot(left, right):
+    return jnp.dot(left, right, preferred_element_type=f32)
+
+
+def exact(left, right):
+    return jnp.dot(left, right, preferred_element_type=f32, precision=lax.Precision.HIGHEST)
+
+
+def dot_t(left, right):
+    return lax.dot_general(left, right, (((1,), (1,)), ((), ())), preferred_element_type=f32)
+
+
+def fold(values):
+    half = values.shape[0] // 2
+    return values[:half] + values[half:]
+
+
+def dot3(left, high, low):
+    return fold(dot(left, high)) + dot(left[: left.shape[0] // 2], low)
+
+
+def iota(shape, dim):
+    return lax.broadcasted_iota(jnp.int32, shape, dim)
+
+
+def chosen(values, line):
+    rows, width = values.shape
+    lanes = 128
+    out = []
+    for start in range(0, line.shape[1], lanes):
+        index = jnp.broadcast_to(line[:, start : start + lanes], (rows, lanes))
+        place = index % lanes
+        block = jnp.take_along_axis(values[:, :lanes], place, axis=1)
+        for first in range(lanes, width, lanes):
+            other = jnp.take_along_axis(values[:, first : first + lanes], place, axis=1)
+            block = jnp.where(index >= first, other, block)
+        out.append(block)
+    return jnp.concatenate(out, axis=1)
+
+
+def member(line, unknowns):
+    return jnp.where(iota((unknowns, line.shape[1]), 0) == line, 1.0, 0.0).astype(bf16)
+
+
+def weighted(scalars, blocks):
+    total = scalars[0] * blocks[0]
+    for scalar, block in zip(scalars[1:], blocks[1:]):
+        total = total + scalar * block
+    return total
+
+
+def kron_matrix(basis):
+    size = basis.shape[0]
+    count = size * size
+
+    def digits(index):
+        lead = jnp.zeros_like(index)
+        for step in range(1, size):
+            lead = lead + (index >= step * size).astype(jnp.int32)
+        return lead, index - lead * size
+
+    def spread(row_digit, col_digit):
+        out = jnp.zeros((count, count), f32)
+        for i in range(size):
+            line = jnp.zeros((1, count), f32)
+            for j in range(size):
+                line = jnp.where(col_digit == j, basis[i, j], line)
+            out = jnp.where(row_digit == i, line, out)
+        return out
+
+    (a, b), (c, d) = digits(iota((count, 1), 0)), digits(iota((1, count), 1))
+    return spread(a, c) * spread(b, d)
+
+
+def wave_of(row, count):
+    return jnp.where(row == 1, count // 2, row // 2)
+
+
+def dft_blocks(device, devices, share, rows_of, cols_of):
+    count = devices * share
+    tall, width = share * len(rows_of), share * len(cols_of)
+    copies = SPAN // width
+
+    def index_of(ids, offsets):
+        part = ids // share
+        owner = jnp.where(part == 0, device ^ offsets[0], 0)
+        for i, offset in enumerate(offsets[1:]):
+            owner = jnp.where(part == i + 1, device ^ offset, owner)
+        return owner * share + ids % share
+
+    row = index_of(iota((tall, SPAN), 0), rows_of)
+    plane = index_of(iota((tall, SPAN), 1) % width, cols_of)
+    angle = 2.0 * math.pi / count * (wave_of(row, count) * plane % count).astype(f32)
+    odd = (row % 2 == 1) & (row != 1)
+    scale = jnp.where(row <= 1, math.sqrt(1.0 / count), math.sqrt(2.0 / count))
+    block = jnp.where(odd, jnp.sin(angle), jnp.cos(angle)) * scale
+    full = jnp.concatenate([block] * copies, axis=0)
+    same = iota(full.shape, 0) // tall == iota(full.shape, 1) // width
+    return stack_split(jnp.where(same, full, 0.0))
+
+
+def corner(left, rows, cols):
+    height = left.shape[0] // 2
+    if (rows, cols) == (height, left.shape[1]):
+        return left
+    return jnp.concatenate([left[:rows, :cols], left[height : height + rows, :cols]], axis=0)
+
+
+def octet(block, part):
+    rows, _, elems = block.shape
+    return block[:, part * TILE : (part + 1) * TILE, :].reshape(rows * TILE, elems)
+
+
+def take_kernel(nodes, out, ready):
+    lines, side = out.shape[:2]
+    move = pltpu.make_async_copy(nodes.at[1 : 1 + lines, 1 : 1 + side], out, ready)
+    move.start()
+    move.wait()
+
+
+def near_kernel(dev, own, mate, slots, send, keep, *, devices, nodes, rim_nodes):
+    _, share, elems = own.shape
+    unknowns = send.shape[2]
+    pair = 2 * share
+    left = dft_blocks(dev[0], devices, share, (CORES, 0), (0, 1))
+    total = jnp.zeros((2 * pair, unknowns), f32)
+    for j, node in enumerate(rim_nodes):
+        both = jnp.concatenate([own[node], mate[node]], axis=0)
+        total = total + dot_t(stack_split(both), member(slots[j : j + 1, :], unknowns))
+    spectra = dot3(corner(left, pair, pair), *split(fold(total)))
+    send[len(nodes)] = spectra[:share]
+    keep[len(nodes)] = spectra[share:]
+    group = left.shape[1] // pair
+    for first in range(0, len(nodes), group):
+        part = nodes[first : first + group]
+        block = jnp.concatenate([ref[node] for node in part for ref in (own, mate)], axis=0)
+        rows = block.shape[0]
+        spectra = dot3(corner(left, rows, rows), *split(block))
+        for k in range(len(part)):
+            send[first + k] = spectra[pair * k : pair * k + share]
+            keep[first + k] = spectra[pair * k + share : pair * (k + 1)]
+
+
+def prepare_kernel(
+    dev, basis, values, coupling, slots, after, lead, rest, lead_solve, rest_solve, pull, where, modes, *, devices
+):
+    del after
+    size = basis.shape[0]
+    rim, inner = coupling.shape
+    elems = slots.shape[1]
+    octets = lead.shape[0]
+    first = lead.shape[2]
+    edge = inner * TILE
+    kron = kron_matrix(basis)
+    couple = exact(coupling[...], kron)
+    left = stack_split(jnp.concatenate([kron, couple], axis=0))
+    right = jnp.concatenate([kron, couple], axis=0).T
+    total = right.shape[1]
+    n = iota((inner, total), 0)
+    sums = jnp.zeros(n.shape, f32)
+    for c in range(size):
+        sums = sums + jnp.where((n >= c * size) & (n < (c + 1) * size), values[c], 0.0)
+        for d in range(size):
+            sums = sums + jnp.where(n == c * size + d, values[d], 0.0)
+    for r in range(octets * TILE):
+        wave = wave_of(dev[0] * (octets * TILE) + r, devices * octets * TILE).astype(f32) * wave_unit
+        modes[r, :total, :] = dot3(left, *split(right / (sums + (helm_base + wave * wave))))
+    spread = jnp.where(iota((total, total * TILE), 0) == iota((total, total * TILE), 1) // TILE, 1.0, 0.0).astype(bf16)
+
+    def widened(matrix):
+        rows = matrix.shape[0]
+        out = []
+        for half in split(matrix):
+            full = dot(half, spread)
+            same = iota(full.shape, 0) % TILE == iota(full.shape, 1) % TILE
+            out.append(jnp.where(same, full, 0.0).astype(bf16))
+        return out
+
+    for part in range(octets):
+        block = jnp.transpose(modes[part * TILE : (part + 1) * TILE], (1, 0, 2))[:total]
+        high, low = widened(block.reshape(total * TILE, total))
+
+        def put(out, rows, cols):
+            out[part] = jnp.concatenate([high[rows, cols], low[rows, cols]], axis=0)
+
+        put(lead, slice(edge, None), slice(0, first))
+        put(rest, slice(edge, None), slice(first, edge))
+        put(lead_solve, slice(0, edge), slice(0, first))
+        put(rest_solve, slice(0, edge), slice(first, edge))
+        put(pull, slice(0, edge), slice(edge, None))
+    columns = slots[...].astype(f32).T
+    ids = iota((elems, where.shape[1]), 1).astype(f32)
+    for j in range(rim):
+        where[j * elems : (j + 1) * elems, :] = jnp.where(ids == columns[:, j : j + 1], 1.0, 0.0).astype(bf16)
+
+
+def far_kernel(dev, own, mate, first, second, lead, lead_solve, coupled, solved, spectral, *, devices, nodes):
+    share, elems = first.shape[1:]
+    left = dft_blocks(dev[0], devices, share, (0,), (0, 1, CORES, CORES + 1))
+    group = left.shape[1] // (4 * share)
+    for start in range(0, len(nodes), group):
+        rows = range(start, min(start + group, len(nodes)))
+        block = jnp.concatenate([x for k in rows for x in (own[nodes[k]], mate[nodes[k]], first[k], second[k])], axis=0)
+        spectra = dot3(corner(left, share * len(rows), 4 * share * len(rows)), *split(block))
+        for i, k in enumerate(rows):
+            spectral[k] = spectra[share * i : share * (i + 1)]
+    for part in range(share // TILE):
+        block = split(octet(spectral[...], part))
+        for table, out in ((lead, coupled), (lead_solve, solved)):
+            out[:, part * TILE : (part + 1) * TILE, :] = dot3(table[part], *block).reshape(-1, TILE, elems)
+
+
+def residual_kernel(keep, received, lead, rest, where, spectral, sums):
+    rows, share, elems = spectral.shape
+    rim = lead.shape[0]
+    spectral[...] = keep[:rows] + received[:rows]
+    parts = []
+    for part in range(share // TILE):
+        block = dot3(rest[part], *split(octet(spectral[...], part)))
+        parts.append(block.reshape(rim, TILE, elems) + octet(lead[...], part).reshape(rim, TILE, elems))
+    coupled = jnp.concatenate(parts, axis=1)
+    line = jnp.concatenate([stack_split(coupled[j]) for j in range(rim)], axis=1)
+    sums[...] = keep[rows] + received[rows] - fold(dot(line, where[...]))
+
+
+def solved_kernel(lead, rest, table, inverse, solved, held, ready):
+    parts = ready.shape[0]
+    size = inverse.shape[0] // parts
+    moves = [
+        pltpu.make_async_copy(inverse.at[i * size : (i + 1) * size], held.at[i * size : (i + 1) * size], ready.at[i])
+        for i in range(parts)
+    ]
+    for move in moves:
+        move.start()
+    inner, share, elems = solved.shape
+    for part in range(share // TILE):
+        block = dot3(table[part], *split(octet(rest[...], part))).reshape(inner, TILE, elems)
+        place = slice(part * TILE, (part + 1) * TILE)
+        solved[:, place, :] = lead[:, place, :] + block
+    for move in moves:
+        move.wait()
+
+
+def back_kernel(group, sums, *refs, codes):
+    neighbours = len(codes)
+    near = refs[:neighbours]
+    sides, partners, inverse, slots, pull, solved, interior, interface = refs[neighbours:]
+    share, unknowns = sums.shape
+    inner, _, elems = interior.shape
+    rim = slots.shape[0]
+    assembled = sums[...]
+    for i in range(neighbours):
+        code = jnp.int32(codes[i][0])
+        for g, other in enumerate(codes[i][1:], 1):
+            code = jnp.where(group[0] == g, other, code)
+        assembled = assembled + jnp.where(sides[...] == code, chosen(near[i][...], partners[...]), 0.0)
+    lines = []
+    for r in range(share):
+        line = jnp.sum(inverse[r] * assembled[r : r + 1, :], axis=1).reshape(1, unknowns)
+        interface[r] = line
+        lines.append(line)
+    values = jnp.concatenate(lines, axis=0)
+    boundary = [chosen(values, slots[j : j + 1, :]) for j in range(rim)]
+    for part in range(share // TILE):
+        place = slice(part * TILE, (part + 1) * TILE)
+        block = jnp.concatenate([block[place] for block in boundary], axis=0)
+        lifted = dot3(pull[part], *split(block)).reshape(inner, TILE, elems)
+        interior[:, place, :] = solved[:, place, :] - lifted
+
+
+VMEM = pl.BlockSpec(memory_space=pltpu.VMEM)
+ANY = pl.BlockSpec(memory_space=pl.ANY)
+SMEM = pl.BlockSpec(memory_space=pltpu.SMEM)
+
+
+def shape(*dims, dtype=f32):
+    return jax.ShapeDtypeStruct(dims, dtype)
+
+
+def kernel_call(body, outs, ins, name, micros, scratch=()):
+    in_specs, arrays = [], []
+    for item in ins:
+        place, array = item if isinstance(item, tuple) else ("", item)
+        in_specs.append({"smem": SMEM, "any": ANY}.get(place, VMEM))
+        if place in ("any", "hbm", "vmem"):
+            array = pltpu.with_memory_space_constraint(array, pltpu.VMEM if place == "vmem" else pltpu.HBM)
+        arrays.append(array)
+    return pl.pallas_call(
+        body,
+        out_shape=outs,
+        in_specs=in_specs,
+        out_specs=(VMEM,) * len(outs) if isinstance(outs, tuple) else VMEM,
+        scratch_shapes=scratch,
+        compiler_params=pltpu.CompilerParams(vmem_limit_bytes=LIMIT),
+        cost_estimate=pl.CostEstimate(flops=0, transcendentals=0, bytes_accessed=int(micros * 3e6)),
+        name=name,
+    )(*arrays)
+
+
+def exchanges(block):
+    wide, tall = lax.axis_size("ex"), lax.axis_size("ey")
+    group = lambda x, y: x * tall + y
+    rounds = []
+    for first in range(min(2, tall - 1)):
+        pairs = {group(x, y): group(x, y + 1) for x in range(wide) for y in range(first, tall - 1, 2)}
+        rounds.append(pairs)
+    if len(rounds) == 2:
+        busy = set(rounds[1]) | set(rounds[1].values())
+        for y in range(tall):
+            for x in range(0, wide - 1, 2):
+                if not {group(x, y), group(x + 1, y)} & busy:
+                    rounds[1][group(x, y)] = group(x + 1, y)
+    for first in range(min(2, wide - 1)):
+        rounds.append({group(x, y): group(x + 1, y) for x in range(first, wide - 1, 2) for y in range(tall)})
+    got, known = [], set()
+    for pairs in rounds:
+        moves = [*pairs.items(), *((b, a) for a, b in pairs.items())]
+        code = [-1] * (wide * tall)
+        for a, b in moves:
+            if (a, b) not in known:
+                known.add((a, b))
+                near = abs(a - b) == 1
+                code[b] = (3 if near else 1) + (1 if a < b else 0)
+        got.append((lax.ppermute(block, ("ex", "ey"), moves), tuple(code)))
+    return got
+
+
+def paired(forcing, eigen_basis, eigen_values, coupling, inverse_blocks, slots, sides, partners):
+    inner_nodes, rim_nodes = node_lists()
+    share, nodes, elems = forcing.shape
+    unknowns = inverse_blocks.shape[1]
+    modes = lax.axis_size("mode")
+    inner, rim = len(inner_nodes), len(rim_nodes)
+    side = round(math.sqrt(nodes))
+    lines = -(-(inner - SPAN // TILE) // (side - 2))
+    raw_rows = lines * (side - 2)
+    rest_rows = inner - raw_rows
+    octets = share // TILE
+    dev = ("smem", lax.axis_index("mode").astype(jnp.int32).reshape(1))
+    mates = [(i, i ^ 1) for i in range(modes)]
+    across = [(i, i ^ CORES) for i in range(modes)]
+    planes = jnp.transpose(forcing, (1, 0, 2))
+    basis = ("smem", eigen_basis)
+    raw_nodes = [int(node) for node in inner_nodes[:raw_rows]]
+    rest_nodes = [int(node) for node in inner_nodes[raw_rows:]]
+
+    own_raw = kernel_call(
+        take_kernel,
+        shape(lines, side - 2, share, elems),
+        [("any", planes.reshape(side, side, share, elems))],
+        "raw_rows",
+        0.5,
+        [pltpu.SemaphoreType.DMA],
+    ).reshape(raw_rows, share, elems)
+    planes, own_raw = lax.optimization_barrier((planes, own_raw))
+    first = lax.ppermute(own_raw, "mode", across)
+    mate_planes = lax.ppermute(planes, "mode", mates)
+    send, keep = kernel_call(
+        functools.partial(near_kernel, devices=modes, nodes=rest_nodes, rim_nodes=[int(node) for node in rim_nodes]),
+        (shape(rest_rows + 1, share, elems), shape(rest_rows + 1, share, elems)),
+        [dev, ("hbm", planes), mate_planes, ("hbm", slots)],
+        "near_spectra",
+        2.5,
+    )
+    received = lax.ppermute(send, "mode", across)
+    tall = 2 * TILE
+    lead, rest, lead_solve, rest_solve, pull, where = kernel_call(
+        functools.partial(prepare_kernel, devices=modes),
+        (
+            shape(octets, tall * rim, raw_rows * TILE, dtype=bf16),
+            shape(octets, tall * rim, rest_rows * TILE, dtype=bf16),
+            shape(octets, tall * inner, raw_rows * TILE, dtype=bf16),
+            shape(octets, tall * inner, rest_rows * TILE, dtype=bf16),
+            shape(octets, tall * inner, rim * TILE, dtype=bf16),
+            shape(rim * elems, unknowns, dtype=bf16),
+        ),
+        [dev, basis, ("smem", eigen_values), ("hbm", coupling), ("hbm", slots), keep],
+        "prepare",
+        4.0,
+        [pltpu.VMEM((share, -(-(inner + rim) // TILE) * TILE, inner + rim), f32)],
+    )
+    second = lax.ppermute(first, "mode", mates)
+    coupled_raw, solved_raw, _ = kernel_call(
+        functools.partial(far_kernel, devices=modes, nodes=raw_nodes),
+        (shape(rim, share, elems), shape(inner, share, elems), shape(raw_rows, share, elems)),
+        [dev, ("hbm", planes), mate_planes, first, second, lead, lead_solve],
+        "far_spectra",
+        1.0,
+    )
+    spectral, sums = kernel_call(
+        residual_kernel,
+        (shape(rest_rows, share, elems), shape(share, unknowns)),
+        [("vmem", x) for x in (keep, received, coupled_raw, rest, where)],
+        "residual",
+        1.5,
+    )
+    got = exchanges(sums)
+    group = lax.axis_index(("ex", "ey")).astype(jnp.int32).reshape(1)
+    solved, inverse_held = kernel_call(
+        solved_kernel,
+        (shape(inner, share, elems), shape(*inverse_blocks.shape)),
+        [solved_raw, spectral, rest_solve, ("any", inverse_blocks)],
+        "solved",
+        1.0,
+        [pltpu.SemaphoreType.DMA((4,))],
+    )
+    interior, interface = kernel_call(
+        functools.partial(back_kernel, codes=[codes for _, codes in got]),
+        (shape(inner, share, elems), shape(share, 1, unknowns)),
+        [("smem", group), sums, *[block for block, _ in got], sides, partners, ("vmem", inverse_held), slots, ("vmem", pull), ("vmem", solved)],
+        "back_solve",
+        2.0,
+    )
+    return (jnp.transpose(interior, (1, 0, 2)), interface)
 
 
 def extended(block, sides, width):
@@ -23,18 +468,6 @@
     return block
 
 
-def is_inner(node_id):
-    return 1 <= node_id // 9 <= 7 and 1 <= node_id % 9 <= 7
-
-
-def node_lists():
-    inner_nodes = np.array([node_id for node_id in range(81) if is_inner(node_id)], dtype=np.int32)
-    rim_nodes = np.array(
-        [node_id for node_id in range(81) if not is_inner(node_id)], dtype=np.int32
-    )
-    return (inner_nodes, rim_nodes)
-
-
 def wave_numbers(row_ids, count):
     return jnp.where(row_ids == 1, count // 2, row_ids // 2)
 
@@ -64,7 +497,7 @@
     return jnp.einsum("ij,rje->rie", kron_basis, spectra, precision=lax.Precision.HIGHEST)
 
 
-def on_device(forcing, eigen_basis, eigen_values, coupling, inverse_blocks, slots, sides, partners):
+def general(forcing, eigen_basis, eigen_values, coupling, inverse_blocks, slots, sides, partners):
     inner_nodes, rim_nodes = node_lists()
     plane_dev = forcing.shape[0]
     elem_dev = forcing.shape[2]
@@ -123,6 +556,13 @@
     return (interior, interface[:, None, :])
 
 
+def on_device(*args):
+    modes = lax.axis_size("mode")
+    if modes == CORES * CORES:
+        return paired(*args)
+    return general(*args)
+
+
 def solution(mesh):
     placed = (
         P("mode", None, ("ex", "ey")),

time: 87.8 us -> 35.3 us (0.40)
  waiting for transfers between devices: 29.1 us -> 4.79 us
  matrix products: 22.2 us -> 0 us
  Pallas kernels: 0 us -> 17.5 us
  local copies, waits for them, and re-layouts: 14.4 us -> 0.92 us
  starting transfers between devices: 18.1 us -> 11 us
  other arithmetic: 2.48 us -> 0 us
    all_to_all x2 -> x0, waiting for transfers between devices: 23.4 us -> none  [the longest x1 12 us: on_device(): lax.all_to_all(sectioned, 'mode', split_axis=1, concat_axis=0, tiled=True)]
    dot_general x11 -> x0, matrix products: 22.2 us -> none  [the longest x1 5.66 us: on_device(): jnp.einsum('rst,rt->rs', inverse_blocks, assembled, precision=lax.Precisi...]
    pallas_call x0 -> x7, Pallas kernels: none -> 17.5 us  [kernel_call(): pl.pallas_call(body, out_shape=outs, in_specs=in_specs, out_specs=(VMEM,)...]
    all_to_all x2 -> x0, starting transfers between devices: 7.73 us -> none  [the longest x1 4.24 us: on_device(): lax.all_to_all(sectioned, 'mode', split_axis=1, concat_axis=0, tiled=True)]
    gather x10 -> x0, local copies, waits for them, and re-layouts: 4.36 us -> none  [the longest x8 3.17 us: on_device(): picked = jnp.take(neighbour, partners[0], axis=1)]
    reshape x5 -> x0, local copies, waits for them, and re-layouts: 2.1 us -> none  [the longest x1 1.05 us: on_device(): spectral[:, :inner_width].reshape(plane_dev, len(inner_nodes), elem_dev)]
    ppermute x3 -> x0, local copies, waits for them, and re-layouts: 1.89 us -> none  [the longest x2 1.2 us: extended(): lax.ppermute(lax.slice_in_dim(block, block.shape[dim] - width, None, axis...]
    dot_general x2 -> x0, local copies, waits for them, and re-layouts: 1.74 us -> none  [the longest x1 1.73 us: on_device(): jnp.einsum('rp,pkc->rkc', table, lax.all_to_all(sectioned, 'mode', split_...]
  transfers between devices with their start and end apart: 6 -> 7, of which waited for: 5 -> 3; matrix products, arithmetic and copies ran while one was open for 4% -> 0% of each run, Pallas kernels for 0% -> 35%
where the time goes in v2:
time: 35.3 us; the launch traced here: 35 us
  Pallas kernels  17.5 us (50%)
  starting transfers between devices  11 us (31%)
  waiting for transfers between devices  4.79 us (14%)
  local copies, waits for them, and re-layouts  0.92 us (3%)
  between operations  0.76 us (2%)
    pallas_call x7, Pallas kernels, kernel_call(): pl.pallas_call(body, out_shape=outs, in_specs=in_specs, out_specs=(VMEM,)...  17.5 us
    ppermute x3, starting transfers between devices, exchanges(): got.append((lax.ppermute(block, ('ex', 'ey'), moves), tuple(code)))  4.95 us
    ppermute x1, starting transfers between devices, paired(): received = lax.ppermute(send, 'mode', across)  2.95 us
    ppermute x1, waiting for transfers between devices, paired(): received = lax.ppermute(send, 'mode', across)  2.71 us
    ppermute x1, starting transfers between devices, paired(): first = lax.ppermute(own_raw, 'mode', across)  2.59 us
    ppermute x1, waiting for transfers between devices, paired(): first = lax.ppermute(own_raw, 'mode', across)  1.77 us
    unnamed x14, local copies, waits for them, and re-layouts  0.92 us
  transfers between devices with their start and end apart: 7, of which 3 were waited for; matrix products, arithmetic and copies ran while one was open for 0% of the time, Pallas kernels for 35%

profile of v2, /device:TPU:0, one launch (start us, length us, event | category | flops | bytes accessed | tf_op | source)
XLA Modules:
  0.0 35.0 jit_solution(18151101197209344674)
XLA Ops:
  0.6 0.0 copy-start.6
  0.6 0.0 copy-start.3
  0.6 1.0 %raw_rows.1 = f32[3,7,16,256]{3,2,1,0:T(8,128)S(1)} custom-call(f32[9,9,16,256]{3,2,1,0:T(8,128)} %bitcast.8), custom_call_target="tpu_custom_call" | custom-call | bytes 1500000 | tf_op jit(solution)/shard_map/raw_rows/pallas_call | solution.py:329
  1.7 0.5 %collective-permute-start = (f32[81,16,256]{2,1,0:T(8,128)}, f32[81,16,256]{2,1,0:T(8,128)S(1)}, u32[]{:S(2)}, u32[]{:S(2)}) collective-permute-start(f32[81,16,256]{2,1,0:T(8,128)} %bitcast.9), channel_id=1, source_target_pairs={{0,8},{8,0},{16,24},{24,16},{1,9},{9,1},{17,25},{25,17},{2,10},{10... | collective-permute-start | bytes 3981320 | tf_op jit(solution)/shard_map/ppermute | solution.py:398
  2.2 2.6 %collective-permute-start.2 = (f32[21,16,256]{2,1,0:T(8,128)S(1)}, f32[21,16,256]{2,1,0:T(8,128)S(1)}, u32[]{:S(2)}, u32[]{:S(2)}) collective-permute-start(f32[21,16,256]{2,1,0:T(8,128)S(1)} %bitcast.7), channel_id=1, source_target_pairs={{0,16},{8,24},{16,0},{24,8},{1,17},{9,25},{17,1},{25,9},{2,18},{10... | collective-permute-start | bytes 1032200 | tf_op jit(solution)/shard_map/ppermute | solution.py:397
  4.8 0.3 collective-permute-done.mate
  5.1 3.9 %near_spectra.1 = (f32[29,16,256]{2,1,0:T(8,128)S(1)}, f32[29,16,256]{2,1,0:T(8,128)S(1)}) custom-call(s32[1]{0:T(128)} %bitcast.1.dev, f32[81,16,256]{2,1,0:T(8,128)} %bitcast.10, f32[81,16,256]{2,1,0:T(8,128)S(1)} %collective-permute-done.mate, s32[32,256]{1,0:T(8,128)} %refs_6_.1), custom_call_target="tpu_custom_call" | custom-call | bytes 7500000 | tf_op jit(solution)/shard_map/near_spectra/pallas_call | solution.py:329
  9.0 2.9 %collective-permute-start.1 = (f32[29,16,256]{2,1,0:T(8,128)S(1)}, f32[29,16,256]{2,1,0:T(8,128)S(1)}, u32[]{:S(2)}, u32[]{:S(2)}) collective-permute-start(f32[29,16,256]{2,1,0:T(8,128)S(1)} %get-tuple-element.22), channel_id=1, source_target_pairs={{0,16},{8,24},{16,0},{24,8},{1,17},{9,25},{17,1},{25,9},{2,18},{10... | collective-permute-start | bytes 1425416 | tf_op jit(solution)/shard_map/ppermute | solution.py:406
  11.9 1.8 %collective-permute-done.2.first = f32[21,16,256]{2,1,0:T(8,128)S(1)} collective-permute-done((f32[21,16,256]{2,1,0:T(8,128)S(1)}, f32[21,16,256]{2,1,0:T(8,128)S(1)}, u32[]{:S(2)}, u32[]{:S(2)}) %collective-permute-start.2) | collective-permute-done | bytes 344096 | tf_op jit(solution)/shard_map/ppermute | solution.py:397
  13.7 0.0 collective-permute-start.3
  13.7 0.0 copy-done.6
  13.7 0.0 copy-done.3
  13.7 3.7 %prepare.1 = (bf16[2,512,168]{2,1,0:T(8,128)(2,1)S(1)}, bf16[2,512,224]{2,1,0:T(8,128)(2,1)S(1)}, bf16[2,784,168]{2,1,0:T(8,128)(2,1)S(1)}, bf16[2,784,224]{2,1,...) custom-call(s32[1]{0:T(128)} %bitcast.1.dev, f32[7,7]{1,0:T(8,128)S(1)} %copy-done.3, ...), custom_call_target="tpu_custom_call" | custom-call | bytes 12000000 | tf_op jit(solution)/shard_map/prepare/pallas_call | solution.py:329
  17.5 0.0 copy-start
  17.5 0.9 %copy-done = bf16[2,784,256]{2,1,0:T(8,128)(2,1)} copy-done((bf16[2,784,256]{2,1,0:T(8,128)(2,1)}, bf16[2,784,256]{2,1,0:T(8,128)(2,1)S(1)}, u32[]{:S(2)}) %copy-start) | copy-done | bytes 802840
  18.3 0.0 collective-permute-done.3.second
  18.3 2.6 %far_spectra.1 = (f32[32,16,256]{2,1,0:T(8,128)S(1)}, f32[49,16,256]{2,1,0:T(8,128)S(1)}, f32[21,16,256]{2,1,0:T(8,128)}) custom-call(s32[1]{0:T(128)} %bitcast.1.dev, f32[81,16,256]{2,1,0:T(8,128)} %bitcast.11, f32[81,16,256]{2,1,0:T(8,128)S(1)} %collective-permute-done.mate, f32[21,16,256]{2,1,0:T(8,128)S(1)} %collective-permute-done.2.first, ...), custom_call_target="tpu_custom_call" | custom-call | bytes 3000000 | tf_op jit(solution)/shard_map/far_spectra/pallas_call | solution.py:329
  20.9 2.7 %collective-permute-done.1.received = f32[29,16,256]{2,1,0:T(8,128)S(1)} collective-permute-done((f32[29,16,256]{2,1,0:T(8,128)S(1)}, f32[29,16,256]{2,1,0:T(8,128)S(1)}, u32[]{:S(2)}, u32[]{:S(2)}) %collective-permute-start.1) | collective-permute-done | bytes 475168 | tf_op jit(solution)/shard_map/ppermute | solution.py:406
  23.6 1.4 %residual.1 = (f32[28,16,256]{2,1,0:T(8,128)S(1)}, f32[16,256]{1,0:T(8,128)S(1)}) custom-call(f32[29,16,256]{2,1,0:T(8,128)S(1)} %get-tuple-element.21.after.keep, f32[29,16,256]{2,1,0:T(8,128)S(1)} %collective-permute-done.1.received, f32[32,16,256]{2,1,0:T(8,128)S(1)} %get-tuple-element.26.lead, bf16[2,512,224]{2,1,0:T(8,128)(2,1)S(1)} %get-tuple-element.27.rest, ...), custom_call_target="tpu_custom_call" | custom-call | bytes 4500000 | tf_op jit(solution)/shard_map/residual/pallas_call | solution.py:329
  25.0 0.0 copy-start.4
  25.0 0.0 copy-start.5
  25.0 1.8 %collective-permute-start.6 = (f32[16,256]{1,0:T(8,128)S(1)}, f32[16,256]{1,0:T(8,128)S(1)}, u32[]{:S(2)}, u32[]{:S(2)}) collective-permute-start(f32[16,256]{1,0:T(8,128)S(1)} %get-tuple-element.29.sums), channel_id=1, source_target_pairs={{0,4},{1,5},{2,6},{3,7},{4,0},{5,1},{6,2},{7,3},{8,12},{9,13},{10,... | collective-permute-start | bytes 49160 | tf_op jit(solution)/shard_map/ppermute | solution.py:365
  26.8 0.3 collective-permute-start.5
  27.1 2.9 %collective-permute-start.4 = (f32[16,256]{1,0:T(8,128)S(1)}, f32[16,256]{1,0:T(8,128)S(1)}, u32[]{:S(2)}, u32[]{:S(2)}) collective-permute-start(f32[16,256]{1,0:T(8,128)S(1)} %get-tuple-element.29.sums), channel_id=1, source_target_pairs={{0,1},{2,3},{4,5},{6,7},{1,0},{3,2},{5,4},{7,6},{8,9},{10,11},{12,... | collective-permute-start | bytes 49160 | tf_op jit(solution)/shard_map/ppermute | solution.py:365
  30.0 2.2 %solved.1 = (f32[49,16,256]{2,1,0:T(8,128)S(1)}, f32[16,256,256]{2,1,0:T(8,128)S(1)}) custom-call(f32[49,16,256]{2,1,0:T(8,128)S(1)} %get-tuple-element.30.lead, f32[28,16,256]{2,1,0:T(8,128)S(1)} %get-tuple-element.31.rest, bf16[2,784,224]{2,1,0:T(8,128)(2,1)S(1)} %get-tuple-element.32.table, f32[16,256,256]{2,1,0:T(8,128)} %inverse.1), custom_call_target="tpu_custom_call" | custom-call | bytes 3000000 | tf_op jit(solution)/shard_map/solved/pallas_call | solution.py:329
  32.2 0.0 collective-permute-done.6.refs_2_
  32.2 0.0 collective-permute-done.5.refs_1_
  32.2 0.0 collective-permute-done.4.refs_0_
  32.2 0.0 copy-done.1
  32.2 0.0 copy-done.2
  32.2 0.0 copy-done.4
  32.3 2.8 %back_solve.1 = (f32[49,16,256]{2,1,0:T(8,128)}, f32[16,1,256]{2,1,0:T(1,128)}) custom-call(s32[1]{0:T(128)} %bitcast.group, f32[16,256]{1,0:T(8,128)S(1)} %get-tuple-element.29.sums, f32[16,256]{1,0:T(8,128)S(1)} %collective-permute-done.4.refs_0_, f32[16,256]{1,0:T(8,128)S(1)} %collective-permute-done.5.refs_1_, ...), custom_call_target="tpu_custom_call" | custom-call | bytes 6000000 | tf_op jit(solution)/shard_map/back_solve/pallas_call | solution.py:329
  (3 shorter events, 0.0 us)
Async XLA Ops:
  0.6 13.1 %copy-start.6 = (f32[7]{0:T(128)S(1)}, f32[7]{0:T(128)}, u32[]{:S(2)}) copy-start(f32[7]{0:T(128)} %values.1) | copy-start | bytes 88
  0.6 13.1 %copy-start.3 = (f32[7,7]{1,0:T(8,128)S(1)}, f32[7,7]{1,0:T(8,128)}, u32[]{:S(2)}) copy-start(f32[7,7]{1,0:T(8,128)} %basis.1) | copy-start | bytes 592
  1.7 3.4 %collective-permute-start = (f32[81,16,256]{2,1,0:T(8,128)}, f32[81,16,256]{2,1,0:T(8,128)S(1)}, u32[]{:S(2)}, u32[]{:S(2)}) collective-permute-start(f32[81,16,256]{2,1,0:T(8,128)} %bitcast.9), channel_id=1, source_target_pairs={{0,8},{8,0},{16,24},{24,16},{1,9},{9,1},{17,25},{25,17},{2,10},{10... | collective-permute-start | bytes 3981320 | tf_op jit(solution)/shard_map/ppermute | solution.py:398
  2.2 11.5 %collective-permute-start.2 = (f32[21,16,256]{2,1,0:T(8,128)S(1)}, f32[21,16,256]{2,1,0:T(8,128)S(1)}, u32[]{:S(2)}, u32[]{:S(2)}) collective-permute-start(f32[21,16,256]{2,1,0:T(8,128)S(1)} %bitcast.7), channel_id=1, source_target_pairs={{0,16},{8,24},{16,0},{24,8},{1,17},{9,25},{17,1},{25,9},{2,18},{10... | collective-permute-start | bytes 1032200 | tf_op jit(solution)/shard_map/ppermute | solution.py:397
  9.0 14.6 %collective-permute-start.1 = (f32[29,16,256]{2,1,0:T(8,128)S(1)}, f32[29,16,256]{2,1,0:T(8,128)S(1)}, u32[]{:S(2)}, u32[]{:S(2)}) collective-permute-start(f32[29,16,256]{2,1,0:T(8,128)S(1)} %get-tuple-element.22), channel_id=1, source_target_pairs={{0,16},{8,24},{16,0},{24,8},{1,17},{9,25},{17,1},{25,9},{2,18},{10... | collective-permute-start | bytes 1425416 | tf_op jit(solution)/shard_map/ppermute | solution.py:406
  13.7 4.7 %collective-permute-start.3 = (f32[21,16,256]{2,1,0:T(8,128)S(1)}, f32[21,16,256]{2,1,0:T(8,128)S(1)}, u32[]{:S(2)}, u32[]{:S(2)}) collective-permute-start(f32[21,16,256]{2,1,0:T(8,128)S(1)} %collective-permute-done.2.first), channel_id=1, source_target_pairs={{0,8},{8,0},{16,24},{24,16},{1,9},{9,1},{17,25},{25,17},{2,10},{10... | collective-permute-start | bytes 1032200 | tf_op jit(solution)/shard_map/ppermute | solution.py:423
  17.5 0.9 %copy-start = (bf16[2,784,256]{2,1,0:T(8,128)(2,1)}, bf16[2,784,256]{2,1,0:T(8,128)(2,1)S(1)}, u32[]{:S(2)}) copy-start(bf16[2,784,256]{2,1,0:T(8,128)(2,1)S(1)} %get-tuple-element.34.refs_7_) | copy-start | bytes 2408452
  25.0 7.2 %copy-start.1 = (bf16[2,784,256]{2,1,0:T(8,128)(2,1)S(1)}, bf16[2,784,256]{2,1,0:T(8,128)(2,1)}, u32[]{:S(2)}) copy-start(bf16[2,784,256]{2,1,0:T(8,128)(2,1)} %copy-done) | copy-start | bytes 2408452
  25.0 7.2 %copy-start.2 = (s32[32,256]{1,0:T(8,128)S(1)}, s32[32,256]{1,0:T(8,128)}, u32[]{:S(2)}) copy-start(s32[32,256]{1,0:T(8,128)} %refs_6_.1) | copy-start | bytes 98308
  25.0 7.2 %copy-start.4 = (s32[1,256]{1,0:T(1,128)S(1)}, s32[1,256]{1,0:T(1,128)}, u32[]{:S(2)}) copy-start(s32[1,256]{1,0:T(1,128)} %refs_3_.1) | copy-start | bytes 3076
  25.0 7.2 %copy-start.5 = (s32[1,256]{1,0:T(1,128)S(1)}, s32[1,256]{1,0:T(1,128)}, u32[]{:S(2)}) copy-start(s32[1,256]{1,0:T(1,128)} %refs_4_.1) | copy-start | bytes 3076
  25.0 7.2 %collective-permute-start.6 = (f32[16,256]{1,0:T(8,128)S(1)}, f32[16,256]{1,0:T(8,128)S(1)}, u32[]{:S(2)}, u32[]{:S(2)}) collective-permute-start(f32[16,256]{1,0:T(8,128)S(1)} %get-tuple-element.29.sums), channel_id=1, source_target_pairs={{0,4},{1,5},{2,6},{3,7},{4,0},{5,1},{6,2},{7,3},{8,12},{9,13},{10,... | collective-permute-start | bytes 49160 | tf_op jit(solution)/shard_map/ppermute | solution.py:365
  26.8 5.4 %collective-permute-start.5 = (f32[16,256]{1,0:T(8,128)S(1)}, f32[16,256]{1,0:T(8,128)S(1)}, u32[]{:S(2)}, u32[]{:S(2)}) collective-permute-start(f32[16,256]{1,0:T(8,128)S(1)} %get-tuple-element.29.sums), channel_id=1, source_target_pairs={{1,2},{5,6},{0,4},{3,7},{2,1},{6,5},{4,0},{7,3},{9,10},{13,14},{8,... | collective-permute-start | bytes 49160 | tf_op jit(solution)/shard_map/ppermute | solution.py:365
  27.1 5.1 %collective-permute-start.4 = (f32[16,256]{1,0:T(8,128)S(1)}, f32[16,256]{1,0:T(8,128)S(1)}, u32[]{:S(2)}, u32[]{:S(2)}) collective-permute-start(f32[16,256]{1,0:T(8,128)S(1)} %get-tuple-element.29.sums), channel_id=1, source_target_pairs={{0,1},{2,3},{4,5},{6,7},{1,0},{3,2},{5,4},{7,6},{8,9},{10,11},{12,... | collective-permute-start | bytes 49160 | tf_op jit(solution)/shard_map/ppermute | solution.py:365

commit v3 on v2

--- a/solution.py
+++ b/solution.py
@@ -64,19 +64,21 @@
     return lax.broadcasted_iota(jnp.int32, shape, dim)
 
 
-def chosen(values, line):
-    rows, width = values.shape
+def chosen(blocks, line):
     lanes = 128
-    out = []
+    width = blocks[0].shape[1]
+    out = [[] for _ in blocks]
     for start in range(0, line.shape[1], lanes):
-        index = jnp.broadcast_to(line[:, start : start + lanes], (rows, lanes))
-        place = index % lanes
-        block = jnp.take_along_axis(values[:, :lanes], place, axis=1)
-        for first in range(lanes, width, lanes):
-            other = jnp.take_along_axis(values[:, first : first + lanes], place, axis=1)
-            block = jnp.where(index >= first, other, block)
-        out.append(block)
-    return jnp.concatenate(out, axis=1)
+        index = jnp.broadcast_to(line[:, start : start + lanes], (TILE, lanes))
+        place = index & (lanes - 1)
+        beyond = [index >= first for first in range(lanes, width, lanes)]
+        for block, parts in zip(blocks, out):
+            found = jnp.take_along_axis(block[:, :lanes], place, axis=1)
+            for i, mask in enumerate(beyond):
+                first = (i + 1) * lanes
+                found = jnp.where(mask, jnp.take_along_axis(block[:, first : first + lanes], place, axis=1), found)
+            parts.append(found)
+    return [jnp.concatenate(parts, axis=1) for parts in out]
 
 
 def member(line, unknowns):
@@ -159,11 +161,11 @@
     move.wait()
 
 
-def near_kernel(dev, own, mate, slots, send, keep, *, devices, nodes, rim_nodes):
+def near_kernel(own, mate, slots, send, keep, *, devices, nodes, rim_nodes):
     _, share, elems = own.shape
     unknowns = send.shape[2]
     pair = 2 * share
-    left = dft_blocks(dev[0], devices, share, (CORES, 0), (0, 1))
+    left = dft_blocks(lax.axis_index("mode"), devices, share, (CORES, 0), (0, 1))
     total = jnp.zeros((2 * pair, unknowns), f32)
     for j, node in enumerate(rim_nodes):
         both = jnp.concatenate([own[node], mate[node]], axis=0)
@@ -183,7 +185,7 @@
 
 
 def prepare_kernel(
-    dev, basis, values, coupling, slots, after, lead, rest, lead_solve, rest_solve, pull, where, modes, *, devices
+    basis, values, coupling, slots, after, lead, rest, lead_solve, rest_solve, pull, where, modes, *, devices
 ):
     del after
     size = basis.shape[0]
@@ -204,7 +206,7 @@
         for d in range(size):
             sums = sums + jnp.where(n == c * size + d, values[d], 0.0)
     for r in range(octets * TILE):
-        wave = wave_of(dev[0] * (octets * TILE) + r, devices * octets * TILE).astype(f32) * wave_unit
+        wave = wave_of(lax.axis_index("mode") * (octets * TILE) + r, devices * octets * TILE).astype(f32) * wave_unit
         modes[r, :total, :] = dot3(left, *split(right / (sums + (helm_base + wave * wave))))
     spread = jnp.where(iota((total, total * TILE), 0) == iota((total, total * TILE), 1) // TILE, 1.0, 0.0).astype(bf16)
 
@@ -235,9 +237,9 @@
         where[j * elems : (j + 1) * elems, :] = jnp.where(ids == columns[:, j : j + 1], 1.0, 0.0).astype(bf16)
 
 
-def far_kernel(dev, own, mate, first, second, lead, lead_solve, coupled, solved, spectral, *, devices, nodes):
+def far_kernel(own, mate, first, second, lead, lead_solve, coupled, solved, spectral, *, devices, nodes):
     share, elems = first.shape[1:]
-    left = dft_blocks(dev[0], devices, share, (0,), (0, 1, CORES, CORES + 1))
+    left = dft_blocks(lax.axis_index("mode"), devices, share, (0,), (0, 1, CORES, CORES + 1))
     group = left.shape[1] // (4 * share)
     for start in range(0, len(nodes), group):
         rows = range(start, min(start + group, len(nodes)))
@@ -264,47 +266,41 @@
     sums[...] = keep[rows] + received[rows] - fold(dot(line, where[...]))
 
 
-def solved_kernel(lead, rest, table, inverse, solved, held, ready):
-    parts = ready.shape[0]
-    size = inverse.shape[0] // parts
-    moves = [
-        pltpu.make_async_copy(inverse.at[i * size : (i + 1) * size], held.at[i * size : (i + 1) * size], ready.at[i])
-        for i in range(parts)
-    ]
-    for move in moves:
-        move.start()
+def solved_kernel(lead, rest, table, solved):
     inner, share, elems = solved.shape
     for part in range(share // TILE):
         block = dot3(table[part], *split(octet(rest[...], part))).reshape(inner, TILE, elems)
         place = slice(part * TILE, (part + 1) * TILE)
         solved[:, place, :] = lead[:, place, :] + block
-    for move in moves:
-        move.wait()
-
-
-def back_kernel(group, sums, *refs, codes):
+
+
+def back_kernel(sums, *refs, codes):
     neighbours = len(codes)
     near = refs[:neighbours]
     sides, partners, inverse, slots, pull, solved, interior, interface = refs[neighbours:]
     share, unknowns = sums.shape
     inner, _, elems = interior.shape
     rim = slots.shape[0]
-    assembled = sums[...]
+    group = lax.axis_index("ex") * lax.axis_size("ey") + lax.axis_index("ey")
+    octets = [slice(start, start + TILE) for start in range(0, share, TILE)]
+    assembled = [sums[place] for place in octets]
     for i in range(neighbours):
         code = jnp.int32(codes[i][0])
         for g, other in enumerate(codes[i][1:], 1):
-            code = jnp.where(group[0] == g, other, code)
-        assembled = assembled + jnp.where(sides[...] == code, chosen(near[i][...], partners[...]), 0.0)
-    lines = []
-    for r in range(share):
-        line = jnp.sum(inverse[r] * assembled[r : r + 1, :], axis=1).reshape(1, unknowns)
-        interface[r] = line
-        lines.append(line)
-    values = jnp.concatenate(lines, axis=0)
+            code = jnp.where(group == g, other, code)
+        picked = chosen([near[i][place] for place in octets], partners[...])
+        assembled = [part + jnp.where(sides[...] == code, new, 0.0) for part, new in zip(assembled, picked)]
+    values = []
+    for place, part in zip(octets, assembled):
+        lines = []
+        for r in range(TILE):
+            line = jnp.sum(inverse[place.start + r] * part[r : r + 1, :], axis=1).reshape(1, unknowns)
+            interface[place.start + r] = line
+            lines.append(line)
+        values.append(jnp.concatenate(lines, axis=0))
     boundary = [chosen(values, slots[j : j + 1, :]) for j in range(rim)]
-    for part in range(share // TILE):
-        place = slice(part * TILE, (part + 1) * TILE)
-        block = jnp.concatenate([block[place] for block in boundary], axis=0)
+    for part, place in enumerate(octets):
+        block = jnp.concatenate([blocks[part] for blocks in boundary], axis=0)
         lifted = dot3(pull[part], *split(block)).reshape(inner, TILE, elems)
         interior[:, place, :] = solved[:, place, :] - lifted
 
@@ -377,7 +373,6 @@
     raw_rows = lines * (side - 2)
     rest_rows = inner - raw_rows
     octets = share // TILE
-    dev = ("smem", lax.axis_index("mode").astype(jnp.int32).reshape(1))
     mates = [(i, i ^ 1) for i in range(modes)]
     across = [(i, i ^ CORES) for i in range(modes)]
     planes = jnp.transpose(forcing, (1, 0, 2))
@@ -399,7 +394,7 @@
     send, keep = kernel_call(
         functools.partial(near_kernel, devices=modes, nodes=rest_nodes, rim_nodes=[int(node) for node in rim_nodes]),
         (shape(rest_rows + 1, share, elems), shape(rest_rows + 1, share, elems)),
-        [dev, ("hbm", planes), mate_planes, ("hbm", slots)],
+        [("hbm", planes), mate_planes, ("hbm", slots)],
         "near_spectra",
         2.5,
     )
@@ -415,7 +410,7 @@
             shape(octets, tall * inner, rim * TILE, dtype=bf16),
             shape(rim * elems, unknowns, dtype=bf16),
         ),
-        [dev, basis, ("smem", eigen_values), ("hbm", coupling), ("hbm", slots), keep],
+        [basis, ("smem", eigen_values), ("hbm", coupling), ("hbm", slots), keep],
         "prepare",
         4.0,
         [pltpu.VMEM((share, -(-(inner + rim) // TILE) * TILE, inner + rim), f32)],
@@ -424,7 +419,7 @@
     coupled_raw, solved_raw, _ = kernel_call(
         functools.partial(far_kernel, devices=modes, nodes=raw_nodes),
         (shape(rim, share, elems), shape(inner, share, elems), shape(raw_rows, share, elems)),
-        [dev, ("hbm", planes), mate_planes, first, second, lead, lead_solve],
+        [("hbm", planes), mate_planes, first, second, lead, lead_solve],
         "far_spectra",
         1.0,
     )
@@ -436,19 +431,13 @@
         1.5,
     )
     got = exchanges(sums)
-    group = lax.axis_index(("ex", "ey")).astype(jnp.int32).reshape(1)
-    solved, inverse_held = kernel_call(
-        solved_kernel,
-        (shape(inner, share, elems), shape(*inverse_blocks.shape)),
-        [solved_raw, spectral, rest_solve, ("any", inverse_blocks)],
-        "solved",
-        1.0,
-        [pltpu.SemaphoreType.DMA((4,))],
+    solved = kernel_call(
+        solved_kernel, shape(inner, share, elems), [solved_raw, spectral, rest_solve], "solved", 1.0
     )
     interior, interface = kernel_call(
         functools.partial(back_kernel, codes=[codes for _, codes in got]),
         (shape(inner, share, elems), shape(share, 1, unknowns)),
-        [("smem", group), sums, *[block for block, _ in got], sides, partners, ("vmem", inverse_held), slots, ("vmem", pull), ("vmem", solved)],
+        [sums, *[block for block, _ in got], sides, partners, inverse_blocks, slots, pull, solved],
         "back_solve",
         2.0,
     )

time: 35.3 us -> 34.7 us (0.983)
  waiting for transfers between devices: 4.79 us -> 6.88 us
  Pallas kernels: 17.5 us -> 15.8 us
  local copies, waits for them, and re-layouts: 0.92 us -> 0.02 us
    pallas_call x7, Pallas kernels: 17.5 us -> 15.8 us  [kernel_call(): pl.pallas_call(body, out_shape=outs, in_specs=in_specs, out_specs=(VMEM,)...]
    ppermute x3, waiting for transfers between devices: 0.01 us -> 1.2 us  [exchanges(): got.append((lax.ppermute(block, ('ex', 'ey'), moves), tuple(code)))]
    ppermute x1, waiting for transfers between devices: 2.71 us -> 3.61 us  [paired(): received = lax.ppermute(send, 'mode', across)]
    unnamed x14 -> x12, local copies, waits for them, and re-layouts: 0.92 us -> 0.02 us
  transfers between devices with their start and end apart: 7 -> 7, of which waited for: 3 -> 5; matrix products, arithmetic and copies ran while one was open for 0% -> 0% of each run, Pallas kernels for 35% -> 31%
where the time goes in v3:
time: 34.7 us; the launch traced here: 34.4 us
  Pallas kernels  15.8 us (46%)
  starting transfers between devices  11 us (32%)
  waiting for transfers between devices  6.88 us (20%)
  between operations  0.72 us (2%)
    pallas_call x7, Pallas kernels, kernel_call(): pl.pallas_call(body, out_shape=outs, in_specs=in_specs, out_specs=(VMEM,)...  15.8 us
    ppermute x3, starting transfers between devices, exchanges(): got.append((lax.ppermute(block, ('ex', 'ey'), moves), tuple(code)))  4.9 us
    ppermute x1, waiting for transfers between devices, paired(): received = lax.ppermute(send, 'mode', across)  3.61 us
    ppermute x1, starting transfers between devices, paired(): received = lax.ppermute(send, 'mode', across)  2.95 us
    ppermute x1, starting transfers between devices, paired(): first = lax.ppermute(own_raw, 'mode', across)  2.59 us
    ppermute x1, waiting for transfers between devices, paired(): first = lax.ppermute(own_raw, 'mode', across)  1.76 us
    ppermute x3, waiting for transfers between devices, exchanges(): got.append((lax.ppermute(block, ('ex', 'ey'), moves), tuple(code)))  1.2 us
  transfers between devices with their start and end apart: 7, of which 5 were waited for; matrix products, arithmetic and copies ran while one was open for 0% of the time, Pallas kernels for 31%

profile of v3, /device:TPU:0, one launch (start us, length us, event | category | flops | bytes accessed | tf_op | source)
XLA Modules:
  0.0 34.4 jit_solution(5600749623262947110)
XLA Ops:
  0.6 0.0 copy-start.5
  0.6 0.0 copy-start.2
  0.6 1.0 %raw_rows.1 = f32[3,7,16,256]{3,2,1,0:T(8,128)S(1)} custom-call(f32[9,9,16,256]{3,2,1,0:T(8,128)} %bitcast.6), custom_call_target="tpu_custom_call" | custom-call | bytes 1500000 | tf_op jit(solution)/shard_map/raw_rows/pallas_call | solution.py:325
  1.7 0.5 %collective-permute-start = (f32[81,16,256]{2,1,0:T(8,128)}, f32[81,16,256]{2,1,0:T(8,128)S(1)}, u32[]{:S(2)}, u32[]{:S(2)}) collective-permute-start(f32[81,16,256]{2,1,0:T(8,128)} %bitcast.7), channel_id=1, source_target_pairs={{0,8},{8,0},{16,24},{24,16},{1,9},{9,1},{17,25},{25,17},{2,10},{10... | collective-permute-start | bytes 3981320 | tf_op jit(solution)/shard_map/ppermute | solution.py:393
  2.2 2.6 %collective-permute-start.2 = (f32[21,16,256]{2,1,0:T(8,128)S(1)}, f32[21,16,256]{2,1,0:T(8,128)S(1)}, u32[]{:S(2)}, u32[]{:S(2)}) collective-permute-start(f32[21,16,256]{2,1,0:T(8,128)S(1)} %bitcast.5), channel_id=1, source_target_pairs={{0,16},{8,24},{16,0},{24,8},{1,17},{9,25},{17,1},{25,9},{2,18},{10... | collective-permute-start | bytes 1032200 | tf_op jit(solution)/shard_map/ppermute | solution.py:392
  4.8 0.3 collective-permute-done.mate
  5.1 3.9 %near_spectra.1 = (f32[29,16,256]{2,1,0:T(8,128)S(1)}, f32[29,16,256]{2,1,0:T(8,128)S(1)}) custom-call(f32[81,16,256]{2,1,0:T(8,128)} %bitcast.8, f32[81,16,256]{2,1,0:T(8,128)S(1)} %collective-permute-done.mate, s32[32,256]{1,0:T(8,128)} %refs_6_.1), custom_call_target="tpu_custom_call" | custom-call | bytes 7500000 | tf_op jit(solution)/shard_map/near_spectra/pallas_call | solution.py:325
  9.0 2.9 %collective-permute-start.1 = (f32[29,16,256]{2,1,0:T(8,128)S(1)}, f32[29,16,256]{2,1,0:T(8,128)S(1)}, u32[]{:S(2)}, u32[]{:S(2)}) collective-permute-start(f32[29,16,256]{2,1,0:T(8,128)S(1)} %get-tuple-element.20), channel_id=1, source_target_pairs={{0,16},{8,24},{16,0},{24,8},{1,17},{9,25},{17,1},{25,9},{2,18},{10... | collective-permute-start | bytes 1425416 | tf_op jit(solution)/shard_map/ppermute | solution.py:401
  11.9 1.8 %collective-permute-done.2.first = f32[21,16,256]{2,1,0:T(8,128)S(1)} collective-permute-done((f32[21,16,256]{2,1,0:T(8,128)S(1)}, f32[21,16,256]{2,1,0:T(8,128)S(1)}, u32[]{:S(2)}, u32[]{:S(2)}) %collective-permute-start.2) | collective-permute-done | bytes 344096 | tf_op jit(solution)/shard_map/ppermute | solution.py:392
  13.7 0.0 collective-permute-start.3
  13.7 0.0 copy-done.5
  13.7 0.0 copy-done.2
  13.7 3.7 %prepare.1 = (bf16[2,512,168]{2,1,0:T(8,128)(2,1)S(1)}, bf16[2,512,224]{2,1,0:T(8,128)(2,1)S(1)}, bf16[2,784,168]{2,1,0:T(8,128)(2,1)S(1)}, bf16[2,784,224]{2,1,...) custom-call(f32[7,7]{1,0:T(8,128)S(1)} %copy-done.2, f32[7]{0:T(128)S(1)} %copy-done.5, ...), custom_call_target="tpu_custom_call" | custom-call | bytes 12000000 | tf_op jit(solution)/shard_map/prepare/pallas_call | solution.py:325
  17.4 0.0 collective-permute-done.3.second
  17.4 2.5 %far_spectra.1 = (f32[32,16,256]{2,1,0:T(8,128)S(1)}, f32[49,16,256]{2,1,0:T(8,128)S(1)}, f32[21,16,256]{2,1,0:T(8,128)}) custom-call(f32[81,16,256]{2,1,0:T(8,128)} %bitcast.9, f32[81,16,256]{2,1,0:T(8,128)S(1)} %collective-permute-done.mate, f32[21,16,256]{2,1,0:T(8,128)S(1)} %collective-permute-done.2.first, ...), custom_call_target="tpu_custom_call" | custom-call | bytes 3000000 | tf_op jit(solution)/shard_map/far_spectra/pallas_call | solution.py:325
  20.0 3.6 %collective-permute-done.1.received = f32[29,16,256]{2,1,0:T(8,128)S(1)} collective-permute-done((f32[29,16,256]{2,1,0:T(8,128)S(1)}, f32[29,16,256]{2,1,0:T(8,128)S(1)}, u32[]{:S(2)}, u32[]{:S(2)}) %collective-permute-start.1) | collective-permute-done | bytes 475168 | tf_op jit(solution)/shard_map/ppermute | solution.py:401
  23.6 0.0 copy-start
  23.6 0.0 copy-start.1
  23.6 0.0 copy-start.3
  23.6 1.4 %residual.1 = (f32[28,16,256]{2,1,0:T(8,128)S(1)}, f32[16,256]{1,0:T(8,128)S(1)}) custom-call(f32[29,16,256]{2,1,0:T(8,128)S(1)} %get-tuple-element.19.after.keep, f32[29,16,256]{2,1,0:T(8,128)S(1)} %collective-permute-done.1.received, f32[32,16,256]{2,1,0:T(8,128)S(1)} %get-tuple-element.24.lead, bf16[2,512,224]{2,1,0:T(8,128)(2,1)S(1)} %get-tuple-element.25.rest, ...), custom_call_target="tpu_custom_call" | custom-call | bytes 4500000 | tf_op jit(solution)/shard_map/residual/pallas_call | solution.py:325
  25.0 1.7 %collective-permute-start.6 = (f32[16,256]{1,0:T(8,128)S(1)}, f32[16,256]{1,0:T(8,128)S(1)}, u32[]{:S(2)}, u32[]{:S(2)}) collective-permute-start(f32[16,256]{1,0:T(8,128)S(1)} %get-tuple-element.27.sums), channel_id=1, source_target_pairs={{0,4},{1,5},{2,6},{3,7},{4,0},{5,1},{6,2},{7,3},{8,12},{9,13},{10,... | collective-permute-start | bytes 49160 | tf_op jit(solution)/shard_map/ppermute | solution.py:361
  26.8 0.3 collective-permute-start.5
  27.1 2.9 %collective-permute-start.4 = (f32[16,256]{1,0:T(8,128)S(1)}, f32[16,256]{1,0:T(8,128)S(1)}, u32[]{:S(2)}, u32[]{:S(2)}) collective-permute-start(f32[16,256]{1,0:T(8,128)S(1)} %get-tuple-element.27.sums), channel_id=1, source_target_pairs={{0,1},{2,3},{4,5},{6,7},{1,0},{3,2},{5,4},{7,6},{8,9},{10,11},{12,... | collective-permute-start | bytes 49160 | tf_op jit(solution)/shard_map/ppermute | solution.py:361
  29.9 0.5 %solved.1.refs_8_ = f32[49,16,256]{2,1,0:T(8,128)S(1)} custom-call(f32[49,16,256]{2,1,0:T(8,128)S(1)} %get-tuple-element.29.lead, f32[28,16,256]{2,1,0:T(8,128)S(1)} %get-tuple-element.30.rest, bf16[2,784,224]{2,1,0:T(8,128)(2,1)S(1)} %get-tuple-element.31.table), custom_call_target="tpu_custom_call" | custom-call | bytes 3000000 | tf_op jit(solution)/shard_map/solved/pallas_call | solution.py:325
  30.4 0.0 collective-permute-done.6.refs_2_
  30.4 0.1 collective-permute-done.5.refs_1_
  30.5 1.1 %collective-permute-done.4.refs_0_ = f32[16,256]{1,0:T(8,128)S(1)} collective-permute-done((f32[16,256]{1,0:T(8,128)S(1)}, f32[16,256]{1,0:T(8,128)S(1)}, u32[]{:S(2)}, u32[]{:S(2)}) %collective-permute-start.4) | collective-permute-done | bytes 16416 | tf_op jit(solution)/shard_map/ppermute | solution.py:361
  31.6 0.0 copy-done
  31.6 0.0 copy-done.1
  31.6 0.0 copy-done.3
  31.6 0.0 copy-done.4
  31.6 2.8 %back_solve.1 = (f32[49,16,256]{2,1,0:T(8,128)}, f32[16,1,256]{2,1,0:T(1,128)}) custom-call(f32[16,256]{1,0:T(8,128)S(1)} %get-tuple-element.27.sums, f32[16,256]{1,0:T(8,128)S(1)} %collective-permute-done.4.refs_0_, f32[16,256]{1,0:T(8,128)S(1)} %collective-permute-done.5.refs_1_, f32[16,256]{1,0:T(8,128)S(1)} %collective-permute-done.6.refs_2_, ...), custom_call_target="tpu_custom_call" | custom-call | bytes 6000000 | tf_op jit(solution)/shard_map/back_solve/pallas_call | solution.py:325
  (1 shorter events, 0.0 us)
Async XLA Ops:
  0.6 13.1 %copy-start.5 = (f32[7]{0:T(128)S(1)}, f32[7]{0:T(128)}, u32[]{:S(2)}) copy-start(f32[7]{0:T(128)} %values.1) | copy-start | bytes 88
  0.6 13.1 %copy-start.2 = (f32[7,7]{1,0:T(8,128)S(1)}, f32[7,7]{1,0:T(8,128)}, u32[]{:S(2)}) copy-start(f32[7,7]{1,0:T(8,128)} %basis.1) | copy-start | bytes 592
  1.7 3.4 %collective-permute-start = (f32[81,16,256]{2,1,0:T(8,128)}, f32[81,16,256]{2,1,0:T(8,128)S(1)}, u32[]{:S(2)}, u32[]{:S(2)}) collective-permute-start(f32[81,16,256]{2,1,0:T(8,128)} %bitcast.7), channel_id=1, source_target_pairs={{0,8},{8,0},{16,24},{24,16},{1,9},{9,1},{17,25},{25,17},{2,10},{10... | collective-permute-start | bytes 3981320 | tf_op jit(solution)/shard_map/ppermute | solution.py:393
  2.2 11.5 %collective-permute-start.2 = (f32[21,16,256]{2,1,0:T(8,128)S(1)}, f32[21,16,256]{2,1,0:T(8,128)S(1)}, u32[]{:S(2)}, u32[]{:S(2)}) collective-permute-start(f32[21,16,256]{2,1,0:T(8,128)S(1)} %bitcast.5), channel_id=1, source_target_pairs={{0,16},{8,24},{16,0},{24,8},{1,17},{9,25},{17,1},{25,9},{2,18},{10... | collective-permute-start | bytes 1032200 | tf_op jit(solution)/shard_map/ppermute | solution.py:392
  9.0 14.6 %collective-permute-start.1 = (f32[29,16,256]{2,1,0:T(8,128)S(1)}, f32[29,16,256]{2,1,0:T(8,128)S(1)}, u32[]{:S(2)}, u32[]{:S(2)}) collective-permute-start(f32[29,16,256]{2,1,0:T(8,128)S(1)} %get-tuple-element.20), channel_id=1, source_target_pairs={{0,16},{8,24},{16,0},{24,8},{1,17},{9,25},{17,1},{25,9},{2,18},{10... | collective-permute-start | bytes 1425416 | tf_op jit(solution)/shard_map/ppermute | solution.py:401
  13.7 3.8 %collective-permute-start.3 = (f32[21,16,256]{2,1,0:T(8,128)S(1)}, f32[21,16,256]{2,1,0:T(8,128)S(1)}, u32[]{:S(2)}, u32[]{:S(2)}) collective-permute-start(f32[21,16,256]{2,1,0:T(8,128)S(1)} %collective-permute-done.2.first), channel_id=1, source_target_pairs={{0,8},{8,0},{16,24},{24,16},{1,9},{9,1},{17,25},{25,17},{2,10},{10... | collective-permute-start | bytes 1032200 | tf_op jit(solution)/shard_map/ppermute | solution.py:418
  23.6 8.0 %copy-start = (f32[16,256,256]{2,1,0:T(8,128)S(1)}, f32[16,256,256]{2,1,0:T(8,128)}, u32[]{:S(2)}) copy-start(f32[16,256,256]{2,1,0:T(8,128)} %refs_5_.1) | copy-start | bytes 12582916
  23.6 8.0 %copy-start.1 = (s32[32,256]{1,0:T(8,128)S(1)}, s32[32,256]{1,0:T(8,128)}, u32[]{:S(2)}) copy-start(s32[32,256]{1,0:T(8,128)} %refs_6_.1) | copy-start | bytes 98308
  23.6 8.0 %copy-start.3 = (s32[1,256]{1,0:T(1,128)S(1)}, s32[1,256]{1,0:T(1,128)}, u32[]{:S(2)}) copy-start(s32[1,256]{1,0:T(1,128)} %refs_3_.1) | copy-start | bytes 3076
  23.6 8.0 %copy-start.4 = (s32[1,256]{1,0:T(1,128)S(1)}, s32[1,256]{1,0:T(1,128)}, u32[]{:S(2)}) copy-start(s32[1,256]{1,0:T(1,128)} %refs_4_.1) | copy-start | bytes 3076
  25.0 5.4 %collective-permute-start.6 = (f32[16,256]{1,0:T(8,128)S(1)}, f32[16,256]{1,0:T(8,128)S(1)}, u32[]{:S(2)}, u32[]{:S(2)}) collective-permute-start(f32[16,256]{1,0:T(8,128)S(1)} %get-tuple-element.27.sums), channel_id=1, source_target_pairs={{0,4},{1,5},{2,6},{3,7},{4,0},{5,1},{6,2},{7,3},{8,12},{9,13},{10,... | collective-permute-start | bytes 49160 | tf_op jit(solution)/shard_map/ppermute | solution.py:361
  26.8 3.7 %collective-permute-start.5 = (f32[16,256]{1,0:T(8,128)S(1)}, f32[16,256]{1,0:T(8,128)S(1)}, u32[]{:S(2)}, u32[]{:S(2)}) collective-permute-start(f32[16,256]{1,0:T(8,128)S(1)} %get-tuple-element.27.sums), channel_id=1, source_target_pairs={{1,2},{5,6},{0,4},{3,7},{2,1},{6,5},{4,0},{7,3},{9,10},{13,14},{8,... | collective-permute-start | bytes 49160 | tf_op jit(solution)/shard_map/ppermute | solution.py:361
  27.1 4.6 %collective-permute-start.4 = (f32[16,256]{1,0:T(8,128)S(1)}, f32[16,256]{1,0:T(8,128)S(1)}, u32[]{:S(2)}, u32[]{:S(2)}) collective-permute-start(f32[16,256]{1,0:T(8,128)S(1)} %get-tuple-element.27.sums), channel_id=1, source_target_pairs={{0,1},{2,3},{4,5},{6,7},{1,0},{3,2},{5,4},{7,6},{8,9},{10,11},{12,... | collective-permute-start | bytes 49160 | tf_op jit(solution)/shard_map/ppermute | solution.py:361

commit v4 on v3

--- a/solution.py
+++ b/solution.py
@@ -161,37 +161,16 @@
     move.wait()
 
 
-def near_kernel(own, mate, slots, send, keep, *, devices, nodes, rim_nodes):
-    _, share, elems = own.shape
-    unknowns = send.shape[2]
-    pair = 2 * share
-    left = dft_blocks(lax.axis_index("mode"), devices, share, (CORES, 0), (0, 1))
-    total = jnp.zeros((2 * pair, unknowns), f32)
-    for j, node in enumerate(rim_nodes):
-        both = jnp.concatenate([own[node], mate[node]], axis=0)
-        total = total + dot_t(stack_split(both), member(slots[j : j + 1, :], unknowns))
-    spectra = dot3(corner(left, pair, pair), *split(fold(total)))
-    send[len(nodes)] = spectra[:share]
-    keep[len(nodes)] = spectra[share:]
-    group = left.shape[1] // pair
-    for first in range(0, len(nodes), group):
-        part = nodes[first : first + group]
-        block = jnp.concatenate([ref[node] for node in part for ref in (own, mate)], axis=0)
-        rows = block.shape[0]
-        spectra = dot3(corner(left, rows, rows), *split(block))
-        for k in range(len(part)):
-            send[first + k] = spectra[pair * k : pair * k + share]
-            keep[first + k] = spectra[pair * k + share : pair * (k + 1)]
-
-
 def prepare_kernel(
-    basis, values, coupling, slots, after, lead, rest, lead_solve, rest_solve, pull, where, modes, *, devices
+    basis, values, coupling, slots, planes, residual, lead, rest, pull, where, held, modes, ready, *, devices
 ):
-    del after
+    move = pltpu.make_async_copy(planes, held, ready)
+    move.start()
     size = basis.shape[0]
     rim, inner = coupling.shape
     elems = slots.shape[1]
     octets = lead.shape[0]
+    share = octets * TILE
     first = lead.shape[2]
     edge = inner * TILE
     kron = kron_matrix(basis)
@@ -205,73 +184,91 @@
         sums = sums + jnp.where((n >= c * size) & (n < (c + 1) * size), values[c], 0.0)
         for d in range(size):
             sums = sums + jnp.where(n == c * size + d, values[d], 0.0)
-    for r in range(octets * TILE):
-        wave = wave_of(lax.axis_index("mode") * (octets * TILE) + r, devices * octets * TILE).astype(f32) * wave_unit
+    device = lax.axis_index("mode")
+    for r in range(2 * share):
+        owner = device ^ CORES if r < share else device
+        wave = wave_of(owner * share + r % share, devices * share).astype(f32) * wave_unit
         modes[r, :total, :] = dot3(left, *split(right / (sums + (helm_base + wave * wave))))
     spread = jnp.where(iota((total, total * TILE), 0) == iota((total, total * TILE), 1) // TILE, 1.0, 0.0).astype(bf16)
 
-    def widened(matrix):
-        rows = matrix.shape[0]
+    def widened(matrix, cols):
         out = []
         for half in split(matrix):
-            full = dot(half, spread)
+            full = dot(half, spread[:, :cols])
             same = iota(full.shape, 0) % TILE == iota(full.shape, 1) % TILE
             out.append(jnp.where(same, full, 0.0).astype(bf16))
         return out
 
-    for part in range(octets):
+    for part in range(2 * octets):
         block = jnp.transpose(modes[part * TILE : (part + 1) * TILE], (1, 0, 2))[:total]
-        high, low = widened(block.reshape(total * TILE, total))
-
-        def put(out, rows, cols):
-            out[part] = jnp.concatenate([high[rows, cols], low[rows, cols]], axis=0)
-
-        put(lead, slice(edge, None), slice(0, first))
-        put(rest, slice(edge, None), slice(first, edge))
-        put(lead_solve, slice(0, edge), slice(0, first))
-        put(rest_solve, slice(0, edge), slice(first, edge))
-        put(pull, slice(0, edge), slice(edge, None))
+        block = block.reshape(total * TILE, total)
+        if part < octets:
+            residual[part] = jnp.concatenate(widened(block[edge:], edge), axis=0)
+            continue
+        high, low = widened(block, total * TILE)
+
+        def put(out, place, rows, cols):
+            out[place] = jnp.concatenate([high[rows, cols], low[rows, cols]], axis=0)
+
+        put(residual, part, slice(edge, None), slice(0, edge))
+        put(lead, part - octets, slice(0, edge), slice(0, first))
+        put(rest, part - octets, slice(0, edge), slice(first, edge))
+        put(pull, part - octets, slice(0, edge), slice(edge, None))
     columns = slots[...].astype(f32).T
     ids = iota((elems, where.shape[1]), 1).astype(f32)
     for j in range(rim):
         where[j * elems : (j + 1) * elems, :] = jnp.where(ids == columns[:, j : j + 1], 1.0, 0.0).astype(bf16)
-
-
-def far_kernel(own, mate, first, second, lead, lead_solve, coupled, solved, spectral, *, devices, nodes):
-    share, elems = first.shape[1:]
-    left = dft_blocks(lax.axis_index("mode"), devices, share, (0,), (0, 1, CORES, CORES + 1))
-    group = left.shape[1] // (4 * share)
-    for start in range(0, len(nodes), group):
-        rows = range(start, min(start + group, len(nodes)))
-        block = jnp.concatenate([x for k in rows for x in (own[nodes[k]], mate[nodes[k]], first[k], second[k])], axis=0)
-        spectra = dot3(corner(left, share * len(rows), 4 * share * len(rows)), *split(block))
-        for i, k in enumerate(rows):
-            spectral[k] = spectra[share * i : share * (i + 1)]
+    move.wait()
+
+
+def near_kernel(
+    own, mate, where, table, sums_out, sums_own, send, keep, spectra, *, devices, inner_nodes, rim_nodes
+):
+    _, share, elems = own.shape
+    pair = 2 * share
+    inner, rim = len(inner_nodes), len(rim_nodes)
+    raw_rows = inner - send.shape[0]
+    left = dft_blocks(lax.axis_index("mode"), devices, share, (CORES, 0), (0, 1))
+    group = left.shape[1] // pair
+    base = 0
+    for nodes in (inner_nodes, rim_nodes):
+        for first in range(0, len(nodes), group):
+            part = nodes[first : first + group]
+            block = jnp.concatenate([ref[node] for node in part for ref in (own, mate)], axis=0)
+            rows = block.shape[0]
+            out = dot3(corner(left, rows, rows), *split(block)).reshape(len(part), pair, elems)
+            spectra[base + first : base + first + len(part)] = out
+        base += len(nodes)
+    send[...] = spectra[raw_rows:inner, :share, :]
+    keep[...] = spectra[:inner, share:, :]
+    parts = []
+    for part in range(pair // TILE):
+        place = slice(part * TILE, (part + 1) * TILE)
+        block = spectra[:inner, place, :].reshape(inner * TILE, elems)
+        coupled = dot3(table[part], *split(block)).reshape(rim, TILE, elems)
+        parts.append(spectra[inner:, place, :] - coupled)
+    residual = jnp.concatenate(parts, axis=1)
+    line = jnp.concatenate([stack_split(residual[j]) for j in range(rim)], axis=1)
+    sums = fold(dot(line, where[...]))
+    sums_out[...] = sums[:share]
+    sums_own[...] = sums[share:]
+
+
+def far_kernel(keep, first, second, lead, rest, solved, spectral, *, devices):
+    rows, share, elems = first.shape
+    inner = keep.shape[0]
+    left = dft_blocks(lax.axis_index("mode"), devices, share, (0,), (CORES, CORES + 1))
+    group = left.shape[1] // (2 * share)
+    for start in range(0, rows, group):
+        part = range(start, min(start + group, rows))
+        block = jnp.concatenate([x for k in part for x in (first[k], second[k])], axis=0)
+        out = dot3(corner(left, share * len(part), 2 * share * len(part)), *split(block))
+        spectral[start : start + len(part)] = keep[start : start + len(part)] + out.reshape(-1, share, elems)
     for part in range(share // TILE):
-        block = split(octet(spectral[...], part))
-        for table, out in ((lead, coupled), (lead_solve, solved)):
-            out[:, part * TILE : (part + 1) * TILE, :] = dot3(table[part], *block).reshape(-1, TILE, elems)
-
-
-def residual_kernel(keep, received, lead, rest, where, spectral, sums):
-    rows, share, elems = spectral.shape
-    rim = lead.shape[0]
-    spectral[...] = keep[:rows] + received[:rows]
-    parts = []
-    for part in range(share // TILE):
-        block = dot3(rest[part], *split(octet(spectral[...], part)))
-        parts.append(block.reshape(rim, TILE, elems) + octet(lead[...], part).reshape(rim, TILE, elems))
-    coupled = jnp.concatenate(parts, axis=1)
-    line = jnp.concatenate([stack_split(coupled[j]) for j in range(rim)], axis=1)
-    sums[...] = keep[rows] + received[rows] - fold(dot(line, where[...]))
-
-
-def solved_kernel(lead, rest, table, solved):
-    inner, share, elems = solved.shape
-    for part in range(share // TILE):
-        block = dot3(table[part], *split(octet(rest[...], part))).reshape(inner, TILE, elems)
         place = slice(part * TILE, (part + 1) * TILE)
-        solved[:, place, :] = lead[:, place, :] + block
+        block = dot3(lead[part], *split(octet(spectral[...], part)))
+        block = block + dot3(rest[part], *split(keep[rows:, place, :].reshape(-1, elems)))
+        solved[:, place, :] = block.reshape(inner, TILE, elems)
 
 
 def back_kernel(sums, *refs, codes):
@@ -305,6 +302,14 @@
         interior[:, place, :] = solved[:, place, :] - lifted
 
 
+def final_kernel(base, received, rest, interior):
+    inner, share, elems = interior.shape
+    for part in range(share // TILE):
+        place = slice(part * TILE, (part + 1) * TILE)
+        block = dot3(rest[part], *split(octet(received[...], part)))
+        interior[:, place, :] = base[:, place, :] + block.reshape(inner, TILE, elems)
+
+
 VMEM = pl.BlockSpec(memory_space=pltpu.VMEM)
 ANY = pl.BlockSpec(memory_space=pl.ANY)
 SMEM = pl.BlockSpec(memory_space=pltpu.SMEM)
@@ -319,7 +324,7 @@
     for item in ins:
         place, array = item if isinstance(item, tuple) else ("", item)
         in_specs.append({"smem": SMEM, "any": ANY}.get(place, VMEM))
-        if place in ("any", "hbm", "vmem"):
+        if place:
             array = pltpu.with_memory_space_constraint(array, pltpu.VMEM if place == "vmem" else pltpu.HBM)
         arrays.append(array)
     return pl.pallas_call(
@@ -377,9 +382,6 @@
     across = [(i, i ^ CORES) for i in range(modes)]
     planes = jnp.transpose(forcing, (1, 0, 2))
     basis = ("smem", eigen_basis)
-    raw_nodes = [int(node) for node in inner_nodes[:raw_rows]]
-    rest_nodes = [int(node) for node in inner_nodes[raw_rows:]]
-
     own_raw = kernel_call(
         take_kernel,
         shape(lines, side - 2, share, elems),
@@ -391,55 +393,65 @@
     planes, own_raw = lax.optimization_barrier((planes, own_raw))
     first = lax.ppermute(own_raw, "mode", across)
     mate_planes = lax.ppermute(planes, "mode", mates)
-    send, keep = kernel_call(
-        functools.partial(near_kernel, devices=modes, nodes=rest_nodes, rim_nodes=[int(node) for node in rim_nodes]),
-        (shape(rest_rows + 1, share, elems), shape(rest_rows + 1, share, elems)),
-        [("hbm", planes), mate_planes, ("hbm", slots)],
-        "near_spectra",
-        2.5,
-    )
-    received = lax.ppermute(send, "mode", across)
     tall = 2 * TILE
-    lead, rest, lead_solve, rest_solve, pull, where = kernel_call(
+    table, lead, rest, pull, where, own_planes = kernel_call(
         functools.partial(prepare_kernel, devices=modes),
         (
-            shape(octets, tall * rim, raw_rows * TILE, dtype=bf16),
-            shape(octets, tall * rim, rest_rows * TILE, dtype=bf16),
+            shape(2 * octets, tall * rim, inner * TILE, dtype=bf16),
             shape(octets, tall * inner, raw_rows * TILE, dtype=bf16),
             shape(octets, tall * inner, rest_rows * TILE, dtype=bf16),
             shape(octets, tall * inner, rim * TILE, dtype=bf16),
             shape(rim * elems, unknowns, dtype=bf16),
+            shape(*planes.shape),
         ),
-        [basis, ("smem", eigen_values), ("hbm", coupling), ("hbm", slots), keep],
+        [basis, ("smem", eigen_values), ("hbm", coupling), ("hbm", slots), ("any", planes)],
         "prepare",
         4.0,
-        [pltpu.VMEM((share, -(-(inner + rim) // TILE) * TILE, inner + rim), f32)],
-    )
+        [
+            pltpu.VMEM((2 * share, -(-(inner + rim) // TILE) * TILE, inner + rim), f32),
+            pltpu.SemaphoreType.DMA,
+        ],
+    )
+    sums_out, sums_own, send, keep = kernel_call(
+        functools.partial(
+            near_kernel,
+            devices=modes,
+            inner_nodes=[int(node) for node in inner_nodes],
+            rim_nodes=[int(node) for node in rim_nodes],
+        ),
+        (
+            shape(share, unknowns),
+            shape(share, unknowns),
+            shape(rest_rows, share, elems),
+            shape(inner, share, elems),
+        ),
+        [own_planes, mate_planes, where, table],
+        "near_spectra",
+        3.0,
+        [pltpu.VMEM((nodes, 2 * share, elems), f32)],
+    )
+    sums_in, send = lax.optimization_barrier((lax.ppermute(sums_out, "mode", across), send))
+    sums = sums_own + sums_in
+    received = lax.ppermute(send, "mode", across)
     second = lax.ppermute(first, "mode", mates)
-    coupled_raw, solved_raw, _ = kernel_call(
-        functools.partial(far_kernel, devices=modes, nodes=raw_nodes),
-        (shape(rim, share, elems), shape(inner, share, elems), shape(raw_rows, share, elems)),
-        [("hbm", planes), mate_planes, first, second, lead, lead_solve],
+    solved = kernel_call(
+        functools.partial(far_kernel, devices=modes),
+        shape(inner, share, elems),
+        [keep, first, second, lead, rest],
         "far_spectra",
-        1.0,
-    )
-    spectral, sums = kernel_call(
-        residual_kernel,
-        (shape(rest_rows, share, elems), shape(share, unknowns)),
-        [("vmem", x) for x in (keep, received, coupled_raw, rest, where)],
-        "residual",
         1.5,
+        [pltpu.VMEM((raw_rows, share, elems), f32)],
     )
     got = exchanges(sums)
-    solved = kernel_call(
-        solved_kernel, shape(inner, share, elems), [solved_raw, spectral, rest_solve], "solved", 1.0
-    )
-    interior, interface = kernel_call(
+    base, interface = kernel_call(
         functools.partial(back_kernel, codes=[codes for _, codes in got]),
         (shape(inner, share, elems), shape(share, 1, unknowns)),
         [sums, *[block for block, _ in got], sides, partners, inverse_blocks, slots, pull, solved],
         "back_solve",
         2.0,
+    )
+    interior = kernel_call(
+        final_kernel, shape(inner, share, elems), [base, ("vmem", received), rest], "interior_solve", 1.0
     )
     return (jnp.transpose(interior, (1, 0, 2)), interface)
 

time: 34.7 us -> 29.6 us (0.85)
  starting transfers between devices: 11 us -> 7.38 us
  Pallas kernels: 15.8 us -> 13.8 us
  waiting for transfers between devices: 6.88 us -> 7.42 us
    ppermute x0 -> x1, waiting for transfers between devices: none -> 3.71 us  [paired(): lax.ppermute(sums_out, 'mode', across)]
    ppermute x1, starting transfers between devices: 2.95 us -> 0.03 us  [paired(): received = lax.ppermute(send, 'mode', across)]
    pallas_call x7 -> x6, Pallas kernels: 15.8 us -> 13.8 us  [kernel_call(): pl.pallas_call(body, out_shape=outs, in_specs=in_specs, out_specs=(VMEM,)...]
    ppermute x1, waiting for transfers between devices: 3.61 us -> 1.71 us  [paired(): received = lax.ppermute(send, 'mode', across)]
    ppermute x1, waiting for transfers between devices: 1.76 us -> 0.01 us  [paired(): first = lax.ppermute(own_raw, 'mode', across)]
    ppermute x3, waiting for transfers between devices: 1.2 us -> 1.99 us  [exchanges(): got.append((lax.ppermute(block, ('ex', 'ey'), moves), tuple(code)))]
    ppermute x3, starting transfers between devices: 4.9 us -> 4.15 us  [exchanges(): got.append((lax.ppermute(block, ('ex', 'ey'), moves), tuple(code)))]
  transfers between devices with their start and end apart: 7 -> 8, of which waited for: 5 -> 4; matrix products, arithmetic and copies ran while one was open for 0% -> 0% of each run, Pallas kernels for 31% -> 39%
where the time goes in v4:
time: 29.6 us; the launch traced here: 29.4 us
  Pallas kernels  13.8 us (47%)
  waiting for transfers between devices  7.42 us (25%)
  starting transfers between devices  7.38 us (25%)
  between operations  0.72 us (2%)
    pallas_call x6, Pallas kernels, kernel_call(): pl.pallas_call(body, out_shape=outs, in_specs=in_specs, out_specs=(VMEM,)...  13.8 us
    ppermute x3, starting transfers between devices, exchanges(): got.append((lax.ppermute(block, ('ex', 'ey'), moves), tuple(code)))  4.15 us
    ppermute x1, waiting for transfers between devices, paired(): lax.ppermute(sums_out, 'mode', across)  3.71 us
    ppermute x1, starting transfers between devices, paired(): first = lax.ppermute(own_raw, 'mode', across)  2.59 us
    ppermute x3, waiting for transfers between devices, exchanges(): got.append((lax.ppermute(block, ('ex', 'ey'), moves), tuple(code)))  1.99 us
    ppermute x1, waiting for transfers between devices, paired(): received = lax.ppermute(send, 'mode', across)  1.71 us
  transfers between devices with their start and end apart: 8, of which 4 were waited for; matrix products, arithmetic and copies ran while one was open for 0% of the time, Pallas kernels for 39%

profile of v4, /device:TPU:0, one launch (start us, length us, event | category | flops | bytes accessed | tf_op | source)
XLA Modules:
  0.0 29.4 jit_solution(7769220029191933648)
XLA Ops:
  0.6 1.0 %raw_rows.1 = f32[3,7,16,256]{3,2,1,0:T(8,128)S(1)} custom-call(f32[9,9,16,256]{3,2,1,0:T(8,128)} %bitcast.6), custom_call_target="tpu_custom_call" | custom-call | bytes 1500000 | tf_op jit(solution)/shard_map/raw_rows/pallas_call | solution.py:330
  1.6 0.5 %collective-permute-start = (f32[81,16,256]{2,1,0:T(8,128)}, f32[81,16,256]{2,1,0:T(8,128)S(1)}, u32[]{:S(2)}, u32[]{:S(2)}) collective-permute-start(f32[81,16,256]{2,1,0:T(8,128)} %bitcast.7), channel_id=1, source_target_pairs={{0,8},{8,0},{16,24},{24,16},{1,9},{9,1},{17,25},{25,17},{2,10},{10... | collective-permute-start | bytes 3981320 | tf_op jit(solution)/shard_map/ppermute | solution.py:395
  2.1 2.6 %collective-permute-start.5 = (f32[21,16,256]{2,1,0:T(8,128)S(1)}, f32[21,16,256]{2,1,0:T(8,128)S(1)}, u32[]{:S(2)}, u32[]{:S(2)}) collective-permute-start(f32[21,16,256]{2,1,0:T(8,128)S(1)} %bitcast.5), channel_id=1, source_target_pairs={{0,16},{8,24},{16,0},{24,8},{1,17},{9,25},{17,1},{25,9},{2,18},{10... | collective-permute-start | bytes 1032200 | tf_op jit(solution)/shard_map/ppermute | solution.py:394
  4.7 4.0 %prepare.1 = (bf16[4,512,392]{2,1,0:T(8,128)(2,1)S(1)}, bf16[2,784,168]{2,1,0:T(8,128)(2,1)S(1)}, bf16[2,784,224]{2,1,0:T(8,128)(2,1)S(1)}, bf16[2,784,256]{2,1,...) custom-call(f32[7,7]{1,0:T(8,128)} %basis.1, f32[7]{0:T(128)} %values.1, ...), custom_call_target="tpu_custom_call" | custom-call | bytes 12000000 | tf_op jit(solution)/shard_map/prepare/pallas_call | solution.py:330
  8.8 0.0 collective-permute-done.mate
  8.8 0.0 copy-start
  8.8 3.9 %near_spectra.1 = (f32[16,256]{1,0:T(8,128)S(1)}, f32[16,256]{1,0:T(8,128)S(1)}, f32[28,16,256]{2,1,0:T(8,128)S(1)}, f32[49,16,256]{2,1,0:T(8,128)S(1)}) custom-call(f32[81,16,256]{2,1,0:T(8,128)S(1)} %get-tuple-element.19.own, f32[81,16,256]{2,1,0:T(8,128)S(1)} %collective-permute-done.mate, bf16[8192,256]{1,0:T(8,128)(2,1)S(1)} %get-tuple-element.20.where, ...), custom_call_target="tpu_custom_call" | custom-call | bytes 9000000 | tf_op jit(solution)/shard_map/near_spectra/pallas_call | solution.py:330
  12.7 0.0 copy-start.1
  12.7 0.0 copy-start.2
  12.7 0.0 copy-start.3
  12.7 0.1 collective-permute-start.1
  12.8 3.7 %collective-permute-done.1 = f32[16,256]{1,0:T(8,128)S(1)} collective-permute-done((f32[16,256]{1,0:T(8,128)S(1)}, f32[16,256]{1,0:T(8,128)S(1)}, u32[]{:S(2)}, u32[]{:S(2)}) %collective-permute-start.1) | collective-permute-done | bytes 16416 | tf_op jit(solution)/shard_map/ppermute | solution.py:433
  16.5 0.0 collective-permute-start.7
  16.6 0.0 collective-permute-done.5.first
  16.6 0.0 collective-permute-start.6
  16.6 2.1 %collective-permute-start.2 = (f32[16,256]{1,0:T(8,128)S(1)}, f32[16,256]{1,0:T(8,128)S(1)}, u32[]{:S(2)}, u32[]{:S(2)}) collective-permute-start(f32[16,256]{1,0:T(8,128)S(1)} %add.3.sums), channel_id=1, source_target_pairs={{0,1},{2,3},{4,5},{6,7},{1,0},{3,2},{5,4},{7,6},{8,9},{10,11},{12,... | collective-permute-start | bytes 49160 | tf_op jit(solution)/shard_map/ppermute | solution.py:366
  18.7 1.5 %collective-permute-start.3 = (f32[16,256]{1,0:T(8,128)S(1)}, f32[16,256]{1,0:T(8,128)S(1)}, u32[]{:S(2)}, u32[]{:S(2)}) collective-permute-start(f32[16,256]{1,0:T(8,128)S(1)} %add.3.sums), channel_id=1, source_target_pairs={{1,2},{5,6},{0,4},{3,7},{2,1},{6,5},{4,0},{7,3},{9,10},{13,14},{8,... | collective-permute-start | bytes 49160 | tf_op jit(solution)/shard_map/ppermute | solution.py:366
  20.2 0.5 %collective-permute-start.4 = (f32[16,256]{1,0:T(8,128)S(1)}, f32[16,256]{1,0:T(8,128)S(1)}, u32[]{:S(2)}, u32[]{:S(2)}) collective-permute-start(f32[16,256]{1,0:T(8,128)S(1)} %add.3.sums), channel_id=1, source_target_pairs={{0,4},{1,5},{2,6},{3,7},{4,0},{5,1},{6,2},{7,3},{8,12},{9,13},{10,... | collective-permute-start | bytes 49160 | tf_op jit(solution)/shard_map/ppermute | solution.py:366
  20.7 0.0 collective-permute-done.6.second
  20.7 1.2 %far_spectra.1.refs_8_ = f32[49,16,256]{2,1,0:T(8,128)S(1)} custom-call(f32[49,16,256]{2,1,0:T(8,128)S(1)} %get-tuple-element.27.keep, f32[21,16,256]{2,1,0:T(8,128)S(1)} %collective-permute-done.5.first, f32[21,16,256]{2,1,0:T(8,128)S(1)} %collective-permute-done.6.second, bf16[2,784,168]{2,1,0:T(8,128)(2,1)S(1)} %get-tuple-element.29.lead, ...), custom_call_target="tpu_custom_call" | custom-call | bytes 4500000 | tf_op jit(solution)/shard_map/far_spectra/pallas_call | solution.py:330
  21.9 0.0 collective-permute-done.2.refs_0_
  21.9 0.5 %collective-permute-done.3.refs_1_ = f32[16,256]{1,0:T(8,128)S(1)} collective-permute-done((f32[16,256]{1,0:T(8,128)S(1)}, f32[16,256]{1,0:T(8,128)S(1)}, u32[]{:S(2)}, u32[]{:S(2)}) %collective-permute-start.3) | collective-permute-done | bytes 16416 | tf_op jit(solution)/shard_map/ppermute | solution.py:366
  22.4 1.5 %collective-permute-done.4.refs_2_ = f32[16,256]{1,0:T(8,128)S(1)} collective-permute-done((f32[16,256]{1,0:T(8,128)S(1)}, f32[16,256]{1,0:T(8,128)S(1)}, u32[]{:S(2)}, u32[]{:S(2)}) %collective-permute-start.4) | collective-permute-done | bytes 16416 | tf_op jit(solution)/shard_map/ppermute | solution.py:366
  23.9 0.0 copy-done
  23.9 0.0 copy-done.1
  23.9 0.0 copy-done.2
  23.9 0.0 copy-done.3
  24.0 2.3 %back_solve.1 = (f32[49,16,256]{2,1,0:T(8,128)S(1)}, f32[16,1,256]{2,1,0:T(1,128)}) custom-call(f32[16,256]{1,0:T(8,128)S(1)} %add.3.sums, f32[16,256]{1,0:T(8,128)S(1)} %collective-permute-done.2.refs_0_, f32[16,256]{1,0:T(8,128)S(1)} %collective-permute-done.3.refs_1_, f32[16,256]{1,0:T(8,128)S(1)} %collective-permute-done.4.refs_2_, ...), custom_call_target="tpu_custom_call" | custom-call | bytes 6000000 | tf_op jit(solution)/shard_map/back_solve/pallas_call | solution.py:330
  26.3 1.7 %collective-permute-done.7.received = f32[28,16,256]{2,1,0:T(8,128)S(1)} collective-permute-done((f32[28,16,256]{2,1,0:T(8,128)S(1)}, f32[28,16,256]{2,1,0:T(8,128)S(1)}, u32[]{:S(2)}, u32[]{:S(2)}) %collective-permute-start.7) | collective-permute-done | bytes 458784 | tf_op jit(solution)/shard_map/ppermute | solution.py:435
  28.0 1.4 %interior_solve.1 = f32[49,16,256]{2,1,0:T(8,128)} custom-call(f32[49,16,256]{2,1,0:T(8,128)S(1)} %get-tuple-element.31.base, f32[28,16,256]{2,1,0:T(8,128)S(1)} %collective-permute-done.7.received, bf16[2,784,224]{2,1,0:T(8,128)(2,1)S(1)} %get-tuple-element.30.rest), custom_call_target="tpu_custom_call" | custom-call | bytes 3000000 | tf_op jit(solution)/shard_map/interior_solve/pallas_call | solution.py:330
  (1 shorter events, 0.0 us)
Async XLA Ops:
  1.6 7.1 %collective-permute-start = (f32[81,16,256]{2,1,0:T(8,128)}, f32[81,16,256]{2,1,0:T(8,128)S(1)}, u32[]{:S(2)}, u32[]{:S(2)}) collective-permute-start(f32[81,16,256]{2,1,0:T(8,128)} %bitcast.7), channel_id=1, source_target_pairs={{0,8},{8,0},{16,24},{24,16},{1,9},{9,1},{17,25},{25,17},{2,10},{10... | collective-permute-start | bytes 3981320 | tf_op jit(solution)/shard_map/ppermute | solution.py:395
  2.1 14.4 %collective-permute-start.5 = (f32[21,16,256]{2,1,0:T(8,128)S(1)}, f32[21,16,256]{2,1,0:T(8,128)S(1)}, u32[]{:S(2)}, u32[]{:S(2)}) collective-permute-start(f32[21,16,256]{2,1,0:T(8,128)S(1)} %bitcast.5), channel_id=1, source_target_pairs={{0,16},{8,24},{16,0},{24,8},{1,17},{9,25},{17,1},{25,9},{2,18},{10... | collective-permute-start | bytes 1032200 | tf_op jit(solution)/shard_map/ppermute | solution.py:394
  8.8 15.2 %copy-start = (f32[16,256,256]{2,1,0:T(8,128)S(1)}, f32[16,256,256]{2,1,0:T(8,128)}, u32[]{:S(2)}) copy-start(f32[16,256,256]{2,1,0:T(8,128)} %refs_5_.1) | copy-start | bytes 12582916
  12.7 11.2 %copy-start.1 = (s32[32,256]{1,0:T(8,128)S(1)}, s32[32,256]{1,0:T(8,128)}, u32[]{:S(2)}) copy-start(s32[32,256]{1,0:T(8,128)} %refs_6_.1) | copy-start | bytes 98308
  12.7 11.2 %copy-start.2 = (s32[1,256]{1,0:T(1,128)S(1)}, s32[1,256]{1,0:T(1,128)}, u32[]{:S(2)}) copy-start(s32[1,256]{1,0:T(1,128)} %refs_3_.1) | copy-start | bytes 3076
  12.7 11.2 %copy-start.3 = (s32[1,256]{1,0:T(1,128)S(1)}, s32[1,256]{1,0:T(1,128)}, u32[]{:S(2)}) copy-start(s32[1,256]{1,0:T(1,128)} %refs_4_.1) | copy-start | bytes 3076
  12.7 3.8 %collective-permute-start.1 = (f32[16,256]{1,0:T(8,128)S(1)}, f32[16,256]{1,0:T(8,128)S(1)}, u32[]{:S(2)}, u32[]{:S(2)}) collective-permute-start(f32[16,256]{1,0:T(8,128)S(1)} %get-tuple-element.23), channel_id=1, source_target_pairs={{0,16},{8,24},{16,0},{24,8},{1,17},{9,25},{17,1},{25,9},{2,18},{10... | collective-permute-start | bytes 49160 | tf_op jit(solution)/shard_map/ppermute | solution.py:433
  16.5 11.4 %collective-permute-start.7 = (f32[28,16,256]{2,1,0:T(8,128)S(1)}, f32[28,16,256]{2,1,0:T(8,128)S(1)}, u32[]{:S(2)}, u32[]{:S(2)}) collective-permute-start(f32[28,16,256]{2,1,0:T(8,128)S(1)} %get-tuple-element.32), channel_id=1, source_target_pairs={{0,16},{8,24},{16,0},{24,8},{1,17},{9,25},{17,1},{25,9},{2,18},{10... | collective-permute-start | bytes 1376264 | tf_op jit(solution)/shard_map/ppermute | solution.py:435
  16.6 4.2 %collective-permute-start.6 = (f32[21,16,256]{2,1,0:T(8,128)S(1)}, f32[21,16,256]{2,1,0:T(8,128)S(1)}, u32[]{:S(2)}, u32[]{:S(2)}) collective-permute-start(f32[21,16,256]{2,1,0:T(8,128)S(1)} %collective-permute-done.5.first), channel_id=1, source_target_pairs={{0,8},{8,0},{16,24},{24,16},{1,9},{9,1},{17,25},{25,17},{2,10},{10... | collective-permute-start | bytes 1032200 | tf_op jit(solution)/shard_map/ppermute | solution.py:436
  16.6 5.4 %collective-permute-start.2 = (f32[16,256]{1,0:T(8,128)S(1)}, f32[16,256]{1,0:T(8,128)S(1)}, u32[]{:S(2)}, u32[]{:S(2)}) collective-permute-start(f32[16,256]{1,0:T(8,128)S(1)} %add.3.sums), channel_id=1, source_target_pairs={{0,1},{2,3},{4,5},{6,7},{1,0},{3,2},{5,4},{7,6},{8,9},{10,11},{12,... | collective-permute-start | bytes 49160 | tf_op jit(solution)/shard_map/ppermute | solution.py:366
  18.7 3.7 %collective-permute-start.3 = (f32[16,256]{1,0:T(8,128)S(1)}, f32[16,256]{1,0:T(8,128)S(1)}, u32[]{:S(2)}, u32[]{:S(2)}) collective-permute-start(f32[16,256]{1,0:T(8,128)S(1)} %add.3.sums), channel_id=1, source_target_pairs={{1,2},{5,6},{0,4},{3,7},{2,1},{6,5},{4,0},{7,3},{9,10},{13,14},{8,... | collective-permute-start | bytes 49160 | tf_op jit(solution)/shard_map/ppermute | solution.py:366
  20.2 3.7 %collective-permute-start.4 = (f32[16,256]{1,0:T(8,128)S(1)}, f32[16,256]{1,0:T(8,128)S(1)}, u32[]{:S(2)}, u32[]{:S(2)}) collective-permute-start(f32[16,256]{1,0:T(8,128)S(1)} %add.3.sums), channel_id=1, source_target_pairs={{0,4},{1,5},{2,6},{3,7},{4,0},{5,1},{6,2},{7,3},{8,12},{9,13},{10,... | collective-permute-start | bytes 49160 | tf_op jit(solution)/shard_map/ppermute | solution.py:366

commit v5 on v4

--- a/solution.py
+++ b/solution.py
@@ -15,6 +15,7 @@
 TILE = 8
 CORES = 2
 SPAN = 256
+RAW_SHARE = 51
 LIMIT = 12 * 2**20
 
 
@@ -154,70 +155,81 @@
     return block[:, part * TILE : (part + 1) * TILE, :].reshape(rows * TILE, elems)
 
 
-def take_kernel(nodes, out, ready):
-    lines, side = out.shape[:2]
-    move = pltpu.make_async_copy(nodes.at[1 : 1 + lines, 1 : 1 + side], out, ready)
-    move.start()
-    move.wait()
-
-
-def prepare_kernel(
-    basis, values, coupling, slots, planes, residual, lead, rest, pull, where, held, modes, ready, *, devices
-):
-    move = pltpu.make_async_copy(planes, held, ready)
-    move.start()
-    size = basis.shape[0]
-    rim, inner = coupling.shape
-    elems = slots.shape[1]
-    octets = lead.shape[0]
-    share = octets * TILE
-    first = lead.shape[2]
-    edge = inner * TILE
-    kron = kron_matrix(basis)
-    couple = exact(coupling[...], kron)
-    left = stack_split(jnp.concatenate([kron, couple], axis=0))
-    right = jnp.concatenate([kron, couple], axis=0).T
-    total = right.shape[1]
-    n = iota((inner, total), 0)
+def take_kernel(nodes, *refs, wanted):
+    count = (len(refs) - 2) // 2
+    sources, out, copies, ready = refs[:count], refs[count], refs[count + 1 : -1], refs[-1]
+    moves = [pltpu.make_async_copy(source, copy, ready.at[i]) for i, (source, copy) in enumerate(zip(sources, copies))]
+    first = 0
+    runs = []
+    for node, length in wanted:
+        run = pltpu.make_async_copy(nodes.at[node : node + length], out.at[first : first + length], ready.at[count + len(runs)])
+        runs.append(run)
+        first += length
+    for move in runs + moves:
+        move.start()
+    for move in runs + moves:
+        move.wait()
+
+
+def per_mode(left, right, values, owner, share, devices, modes):
+    size = values.shape[0]
+    n = iota(right.shape, 0)
     sums = jnp.zeros(n.shape, f32)
     for c in range(size):
         sums = sums + jnp.where((n >= c * size) & (n < (c + 1) * size), values[c], 0.0)
         for d in range(size):
             sums = sums + jnp.where(n == c * size + d, values[d], 0.0)
-    device = lax.axis_index("mode")
-    for r in range(2 * share):
-        owner = device ^ CORES if r < share else device
-        wave = wave_of(owner * share + r % share, devices * share).astype(f32) * wave_unit
-        modes[r, :total, :] = dot3(left, *split(right / (sums + (helm_base + wave * wave))))
-    spread = jnp.where(iota((total, total * TILE), 0) == iota((total, total * TILE), 1) // TILE, 1.0, 0.0).astype(bf16)
-
-    def widened(matrix, cols):
-        out = []
-        for half in split(matrix):
-            full = dot(half, spread[:, :cols])
-            same = iota(full.shape, 0) % TILE == iota(full.shape, 1) % TILE
-            out.append(jnp.where(same, full, 0.0).astype(bf16))
-        return out
-
-    for part in range(2 * octets):
-        block = jnp.transpose(modes[part * TILE : (part + 1) * TILE], (1, 0, 2))[:total]
-        block = block.reshape(total * TILE, total)
-        if part < octets:
-            residual[part] = jnp.concatenate(widened(block[edge:], edge), axis=0)
-            continue
-        high, low = widened(block, total * TILE)
-
-        def put(out, place, rows, cols):
-            out[place] = jnp.concatenate([high[rows, cols], low[rows, cols]], axis=0)
-
-        put(residual, part, slice(edge, None), slice(0, edge))
-        put(lead, part - octets, slice(0, edge), slice(0, first))
-        put(rest, part - octets, slice(0, edge), slice(first, edge))
-        put(pull, part - octets, slice(0, edge), slice(edge, None))
+    rows = left.shape[0] // 2
+    for r in range(share):
+        wave = wave_of(owner * share + r, devices * share).astype(f32) * wave_unit
+        modes[r, :rows, :] = dot3(left, *split(right / (sums + (helm_base + wave * wave))))
+
+
+def widened(modes, part, rows, cols):
+    block = jnp.transpose(modes[part * TILE : (part + 1) * TILE], (1, 0, 2))[:rows, :, :cols]
+    spread = jnp.where(iota((cols, cols * TILE), 0) == iota((cols, cols * TILE), 1) // TILE, 1.0, 0.0).astype(bf16)
+    same = (iota((TILE, cols * TILE), 0) == iota((TILE, cols * TILE), 1) % TILE)[None]
+    out = []
+    for half in split(block.reshape(rows * TILE, cols)):
+        full = dot(half, spread).reshape(rows, TILE, cols * TILE)
+        out.append(jnp.where(same, full, 0.0).reshape(rows * TILE, cols * TILE).astype(bf16))
+    return out
+
+
+def tables_kernel(
+    basis, values, coupling, planes, slots, table, lead, rest, pull, where, held, modes, ready, *, devices
+):
+    move = pltpu.make_async_copy(planes, held, ready)
+    move.start()
+    rim, inner = coupling.shape
+    elems = slots.shape[1]
+    octets, _, first = lead.shape
+    edge = inner * TILE
     columns = slots[...].astype(f32).T
     ids = iota((elems, where.shape[1]), 1).astype(f32)
     for j in range(rim):
         where[j * elems : (j + 1) * elems, :] = jnp.where(ids == columns[:, j : j + 1], 1.0, 0.0).astype(bf16)
+    kron = kron_matrix(basis)
+    couple = exact(coupling[...], kron)
+    device = lax.axis_index("mode")
+    share = octets * TILE
+    both = jnp.concatenate([couple, kron], axis=0)
+    right = jnp.concatenate([kron, couple], axis=0).T
+    per_mode(stack_split(couple), right, values, device ^ CORES, share, devices, modes)
+    for part in range(octets):
+        table[part] = jnp.concatenate(widened(modes, part, rim, inner), axis=0)
+    per_mode(stack_split(both), right, values, device, share, devices, modes)
+    top = rim * TILE
+    for part in range(octets):
+        halves = widened(modes, part, rim + inner, rim + inner)
+
+        def put(out, place, rows, cols):
+            out[place] = jnp.concatenate([half[rows, cols] for half in halves], axis=0)
+
+        put(table, octets + part, slice(0, top), slice(0, edge))
+        put(lead, part, slice(top, None), slice(0, first))
+        put(rest, part, slice(top, None), slice(first, edge))
+        put(pull, part, slice(top, None), slice(edge, None))
     move.wait()
 
 
@@ -324,7 +336,7 @@
     for item in ins:
         place, array = item if isinstance(item, tuple) else ("", item)
         in_specs.append({"smem": SMEM, "any": ANY}.get(place, VMEM))
-        if place:
+        if place in ("any", "hbm", "vmem"):
             array = pltpu.with_memory_space_constraint(array, pltpu.VMEM if place == "vmem" else pltpu.HBM)
         arrays.append(array)
     return pl.pallas_call(
@@ -374,28 +386,33 @@
     modes = lax.axis_size("mode")
     inner, rim = len(inner_nodes), len(rim_nodes)
     side = round(math.sqrt(nodes))
-    lines = -(-(inner - SPAN // TILE) // (side - 2))
-    raw_rows = lines * (side - 2)
+    raw_rows = inner * RAW_SHARE // 100
+    line = side - 2
+    runs = [
+        (int(inner_nodes[first]), min(line, raw_rows - first)) for first in range(0, raw_rows, line)
+    ]
     rest_rows = inner - raw_rows
     octets = share // TILE
     mates = [(i, i ^ 1) for i in range(modes)]
     across = [(i, i ^ CORES) for i in range(modes)]
     planes = jnp.transpose(forcing, (1, 0, 2))
-    basis = ("smem", eigen_basis)
-    own_raw = kernel_call(
-        take_kernel,
-        shape(lines, side - 2, share, elems),
-        [("any", planes.reshape(side, side, share, elems))],
+    small = [eigen_basis, eigen_values, coupling, slots]
+    own_raw, *small = kernel_call(
+        functools.partial(take_kernel, wanted=runs),
+        (shape(raw_rows, share, elems), *[jax.ShapeDtypeStruct(x.shape, x.dtype) for x in small]),
+        [("any", planes), *[("any", x) for x in small]],
         "raw_rows",
         0.5,
-        [pltpu.SemaphoreType.DMA],
-    ).reshape(raw_rows, share, elems)
+        [pltpu.SemaphoreType.DMA((len(small) + len(runs),))],
+    )
+    eigen_basis, eigen_values, coupling, slots_held = small
+    basis, values = ("smem", eigen_basis), ("smem", eigen_values)
     planes, own_raw = lax.optimization_barrier((planes, own_raw))
     first = lax.ppermute(own_raw, "mode", across)
     mate_planes = lax.ppermute(planes, "mode", mates)
     tall = 2 * TILE
     table, lead, rest, pull, where, own_planes = kernel_call(
-        functools.partial(prepare_kernel, devices=modes),
+        functools.partial(tables_kernel, devices=modes),
         (
             shape(2 * octets, tall * rim, inner * TILE, dtype=bf16),
             shape(octets, tall * inner, raw_rows * TILE, dtype=bf16),
@@ -404,13 +421,10 @@
             shape(rim * elems, unknowns, dtype=bf16),
             shape(*planes.shape),
         ),
-        [basis, ("smem", eigen_values), ("hbm", coupling), ("hbm", slots), ("any", planes)],
-        "prepare",
-        4.0,
-        [
-            pltpu.VMEM((2 * share, -(-(inner + rim) // TILE) * TILE, inner + rim), f32),
-            pltpu.SemaphoreType.DMA,
-        ],
+        [basis, values, coupling, ("any", planes), slots_held],
+        "tables",
+        2.5,
+        [pltpu.VMEM((share, -(-(inner + rim) // TILE) * TILE, inner + rim), f32), pltpu.SemaphoreType.DMA],
     )
     sums_out, sums_own, send, keep = kernel_call(
         functools.partial(

time: 29.6 us -> 28.1 us (0.949)
  waiting for transfers between devices: 7.42 us -> 6.21 us
    ppermute x1, waiting for transfers between devices: 1.71 us -> 0.62 us  [paired(): received = lax.ppermute(send, 'mode', across)]
    ppermute x1, starting transfers between devices: 0.03 us -> 0.53 us  [paired(): received = lax.ppermute(send, 'mode', across)]
    ppermute x3, starting transfers between devices: 4.15 us -> 3.67 us  [exchanges(): got.append((lax.ppermute(block, ('ex', 'ey'), moves), tuple(code)))]
  transfers between devices with their start and end apart: 8 -> 8, of which waited for: 4 -> 4; matrix products, arithmetic and copies ran while one was open for 0% -> 0% of each run, Pallas kernels for 39% -> 40%
where the time goes in v5:
time: 28.1 us; the launch traced here: 27.9 us
  Pallas kernels  13.6 us (48%)
  starting transfers between devices  7.4 us (26%)
  waiting for transfers between devices  6.21 us (22%)
  between operations  0.72 us (3%)
    pallas_call x6, Pallas kernels, kernel_call(): pl.pallas_call(body, out_shape=outs, in_specs=in_specs, out_specs=(VMEM,)...  13.6 us
    ppermute x1, waiting for transfers between devices, paired(): lax.ppermute(sums_out, 'mode', across)  3.72 us
    ppermute x3, starting transfers between devices, exchanges(): got.append((lax.ppermute(block, ('ex', 'ey'), moves), tuple(code)))  3.67 us
    ppermute x1, starting transfers between devices, paired(): first = lax.ppermute(own_raw, 'mode', across)  2.59 us
    ppermute x3, waiting for transfers between devices, exchanges(): got.append((lax.ppermute(block, ('ex', 'ey'), moves), tuple(code)))  1.86 us
    ppermute x1, waiting for transfers between devices, paired(): received = lax.ppermute(send, 'mode', across)  0.62 us
  transfers between devices with their start and end apart: 8, of which 4 were waited for; matrix products, arithmetic and copies ran while one was open for 0% of the time, Pallas kernels for 40%

profile of v5, /device:TPU:0, one launch (start us, length us, event | category | flops | bytes accessed | tf_op | source)
XLA Modules:
  0.0 27.9 jit_solution(1627755015949335218)
XLA Ops:
  0.6 1.1 %raw_rows.1 = (f32[24,16,256]{2,1,0:T(8,128)S(1)}, f32[7,7]{1,0:T(8,128)S(1)}, f32[7]{0:T(128)S(1)}, f32[32,49]{1,0:T(8,128)S(1)}, s32[32,256]{1,0:T(8,128)S(1)}) custom-call(f32[81,16,256]{2,1,0:T(8,128)} %bitcast.2, f32[7,7]{1,0:T(8,128)} %refs_0_.1, f32[7]{0:T(128)} %refs_1_.1, f32[32,49]{1,0:T(8,128)} %refs_2_.1, s32[32,256]{1,0:T(8,128)} %refs_6_.1), custom_call_target="tpu_custom_call" | custom-call | bytes 1500000 | tf_op jit(solution)/shard_map/raw_rows/pallas_call | solution.py:342
  1.7 0.5 %collective-permute-start = (f32[81,16,256]{2,1,0:T(8,128)}, f32[81,16,256]{2,1,0:T(8,128)S(1)}, u32[]{:S(2)}, u32[]{:S(2)}) collective-permute-start(f32[81,16,256]{2,1,0:T(8,128)} %bitcast.3), channel_id=1, source_target_pairs={{0,8},{8,0},{16,24},{24,16},{1,9},{9,1},{17,25},{25,17},{2,10},{10... | collective-permute-start | bytes 3981320 | tf_op jit(solution)/shard_map/ppermute | solution.py:412
  2.2 2.6 %collective-permute-start.5 = (f32[24,16,256]{2,1,0:T(8,128)S(1)}, f32[24,16,256]{2,1,0:T(8,128)S(1)}, u32[]{:S(2)}, u32[]{:S(2)}) collective-permute-start(f32[24,16,256]{2,1,0:T(8,128)S(1)} %get-tuple-element.38), channel_id=1, source_target_pairs={{0,16},{8,24},{16,0},{24,8},{1,17},{9,25},{17,1},{25,9},{2,18},{10... | collective-permute-start | bytes 1179656 | tf_op jit(solution)/shard_map/ppermute | solution.py:411
  4.8 3.5 %tables.1 = (bf16[4,512,392]{2,1,0:T(8,128)(2,1)S(1)}, bf16[2,784,192]{2,1,0:T(8,128)(2,1)S(1)}, bf16[2,784,200]{2,1,0:T(8,128)(2,1)S(1)}, bf16[2,784,256]{2,1,0...) custom-call(f32[7,7]{1,0:T(8,128)S(1)} %get-tuple-element.23.basis, ...), custom_call_target="tpu_custom_call" | custom-call | bytes 7500000 | tf_op jit(solution)/shard_map/tables/pallas_call | solution.py:342
  8.3 0.0 collective-permute-done.mate
  8.3 0.0 copy-start
  8.3 3.9 %near_spectra.1 = (f32[16,256]{1,0:T(8,128)S(1)}, f32[16,256]{1,0:T(8,128)S(1)}, f32[25,16,256]{2,1,0:T(8,128)S(1)}, f32[49,16,256]{2,1,0:T(8,128)S(1)}) custom-call(f32[81,16,256]{2,1,0:T(8,128)S(1)} %get-tuple-element.29.own, f32[81,16,256]{2,1,0:T(8,128)S(1)} %collective-permute-done.mate, bf16[8192,256]{1,0:T(8,128)(2,1)S(1)} %get-tuple-element.30.where, ...), custom_call_target="tpu_custom_call" | custom-call | bytes 9000000 | tf_op jit(solution)/shard_map/near_spectra/pallas_call | solution.py:342
  12.3 0.0 copy-start.1
  12.3 0.0 copy-start.2
  12.3 0.0 copy-start.3
  12.3 0.1 collective-permute-start.1
  12.4 3.7 %collective-permute-done.1 = f32[16,256]{1,0:T(8,128)S(1)} collective-permute-done((f32[16,256]{1,0:T(8,128)S(1)}, f32[16,256]{1,0:T(8,128)S(1)}, u32[]{:S(2)}, u32[]{:S(2)}) %collective-permute-start.1) | collective-permute-done | bytes 16416 | tf_op jit(solution)/shard_map/ppermute | solution.py:447
  16.1 0.5 %collective-permute-start.7 = (f32[25,16,256]{2,1,0:T(8,128)S(1)}, f32[25,16,256]{2,1,0:T(8,128)S(1)}, u32[]{:S(2)}, u32[]{:S(2)}) collective-permute-start(f32[25,16,256]{2,1,0:T(8,128)S(1)} %get-tuple-element.42), channel_id=1, source_target_pairs={{0,16},{8,24},{16,0},{24,8},{1,17},{9,25},{17,1},{25,9},{2,18},{10... | collective-permute-start | bytes 1228808 | tf_op jit(solution)/shard_map/ppermute | solution.py:449
  16.7 0.0 collective-permute-done.5.first
  16.7 0.0 collective-permute-start.6
  16.7 1.6 %collective-permute-start.2 = (f32[16,256]{1,0:T(8,128)S(1)}, f32[16,256]{1,0:T(8,128)S(1)}, u32[]{:S(2)}, u32[]{:S(2)}) collective-permute-start(f32[16,256]{1,0:T(8,128)S(1)} %add.3.sums), channel_id=1, source_target_pairs={{0,1},{2,3},{4,5},{6,7},{1,0},{3,2},{5,4},{7,6},{8,9},{10,11},{12,... | collective-permute-start | bytes 49160 | tf_op jit(solution)/shard_map/ppermute | solution.py:378
  18.3 1.5 %collective-permute-start.3 = (f32[16,256]{1,0:T(8,128)S(1)}, f32[16,256]{1,0:T(8,128)S(1)}, u32[]{:S(2)}, u32[]{:S(2)}) collective-permute-start(f32[16,256]{1,0:T(8,128)S(1)} %add.3.sums), channel_id=1, source_target_pairs={{1,2},{5,6},{0,4},{3,7},{2,1},{6,5},{4,0},{7,3},{9,10},{13,14},{8,... | collective-permute-start | bytes 49160 | tf_op jit(solution)/shard_map/ppermute | solution.py:378
  19.8 0.5 %collective-permute-start.4 = (f32[16,256]{1,0:T(8,128)S(1)}, f32[16,256]{1,0:T(8,128)S(1)}, u32[]{:S(2)}, u32[]{:S(2)}) collective-permute-start(f32[16,256]{1,0:T(8,128)S(1)} %add.3.sums), channel_id=1, source_target_pairs={{0,4},{1,5},{2,6},{3,7},{4,0},{5,1},{6,2},{7,3},{8,12},{9,13},{10,... | collective-permute-start | bytes 49160 | tf_op jit(solution)/shard_map/ppermute | solution.py:378
  20.3 0.0 collective-permute-done.6.second
  20.3 1.3 %far_spectra.1.refs_8_ = f32[49,16,256]{2,1,0:T(8,128)S(1)} custom-call(f32[49,16,256]{2,1,0:T(8,128)S(1)} %get-tuple-element.37.keep, f32[24,16,256]{2,1,0:T(8,128)S(1)} %collective-permute-done.5.first, f32[24,16,256]{2,1,0:T(8,128)S(1)} %collective-permute-done.6.second, bf16[2,784,192]{2,1,0:T(8,128)(2,1)S(1)} %get-tuple-element.39.lead, ...), custom_call_target="tpu_custom_call" | custom-call | bytes 4500000 | tf_op jit(solution)/shard_map/far_spectra/pallas_call | solution.py:342
  21.7 0.0 collective-permute-done.2.refs_0_
  21.7 0.4 %collective-permute-done.3.refs_1_ = f32[16,256]{1,0:T(8,128)S(1)} collective-permute-done((f32[16,256]{1,0:T(8,128)S(1)}, f32[16,256]{1,0:T(8,128)S(1)}, u32[]{:S(2)}, u32[]{:S(2)}) %collective-permute-start.3) | collective-permute-done | bytes 16416 | tf_op jit(solution)/shard_map/ppermute | solution.py:378
  22.1 1.5 %collective-permute-done.4.refs_2_ = f32[16,256]{1,0:T(8,128)S(1)} collective-permute-done((f32[16,256]{1,0:T(8,128)S(1)}, f32[16,256]{1,0:T(8,128)S(1)}, u32[]{:S(2)}, u32[]{:S(2)}) %collective-permute-start.4) | collective-permute-done | bytes 16416 | tf_op jit(solution)/shard_map/ppermute | solution.py:378
  23.5 0.0 copy-done
  23.5 0.0 copy-done.1
  23.6 0.0 copy-done.2
  23.6 0.0 copy-done.3
  23.6 2.3 %back_solve.1 = (f32[49,16,256]{2,1,0:T(8,128)S(1)}, f32[16,1,256]{2,1,0:T(1,128)}) custom-call(f32[16,256]{1,0:T(8,128)S(1)} %add.3.sums, f32[16,256]{1,0:T(8,128)S(1)} %collective-permute-done.2.refs_0_, f32[16,256]{1,0:T(8,128)S(1)} %collective-permute-done.3.refs_1_, f32[16,256]{1,0:T(8,128)S(1)} %collective-permute-done.4.refs_2_, ...), custom_call_target="tpu_custom_call" | custom-call | bytes 6000000 | tf_op jit(solution)/shard_map/back_solve/pallas_call | solution.py:342
  25.9 0.6 %collective-permute-done.7.received = f32[25,16,256]{2,1,0:T(8,128)S(1)} collective-permute-done((f32[25,16,256]{2,1,0:T(8,128)S(1)}, f32[25,16,256]{2,1,0:T(8,128)S(1)}, u32[]{:S(2)}, u32[]{:S(2)}) %collective-permute-start.7) | collective-permute-done | bytes 409632 | tf_op jit(solution)/shard_map/ppermute | solution.py:449
  26.5 1.4 %interior_solve.1 = f32[49,16,256]{2,1,0:T(8,128)} custom-call(f32[49,16,256]{2,1,0:T(8,128)S(1)} %get-tuple-element.41.base, f32[25,16,256]{2,1,0:T(8,128)S(1)} %collective-permute-done.7.received, bf16[2,784,200]{2,1,0:T(8,128)(2,1)S(1)} %get-tuple-element.40.rest), custom_call_target="tpu_custom_call" | custom-call | bytes 3000000 | tf_op jit(solution)/shard_map/interior_solve/pallas_call | solution.py:342
  (1 shorter events, 0.0 us)
Async XLA Ops:
  1.7 6.6 %collective-permute-start = (f32[81,16,256]{2,1,0:T(8,128)}, f32[81,16,256]{2,1,0:T(8,128)S(1)}, u32[]{:S(2)}, u32[]{:S(2)}) collective-permute-start(f32[81,16,256]{2,1,0:T(8,128)} %bitcast.3), channel_id=1, source_target_pairs={{0,8},{8,0},{16,24},{24,16},{1,9},{9,1},{17,25},{25,17},{2,10},{10... | collective-permute-start | bytes 3981320 | tf_op jit(solution)/shard_map/ppermute | solution.py:412
  2.2 14.4 %collective-permute-start.5 = (f32[24,16,256]{2,1,0:T(8,128)S(1)}, f32[24,16,256]{2,1,0:T(8,128)S(1)}, u32[]{:S(2)}, u32[]{:S(2)}) collective-permute-start(f32[24,16,256]{2,1,0:T(8,128)S(1)} %get-tuple-element.38), channel_id=1, source_target_pairs={{0,16},{8,24},{16,0},{24,8},{1,17},{9,25},{17,1},{25,9},{2,18},{10... | collective-permute-start | bytes 1179656 | tf_op jit(solution)/shard_map/ppermute | solution.py:411
  8.3 15.2 %copy-start = (f32[16,256,256]{2,1,0:T(8,128)S(1)}, f32[16,256,256]{2,1,0:T(8,128)}, u32[]{:S(2)}) copy-start(f32[16,256,256]{2,1,0:T(8,128)} %refs_5_.1) | copy-start | bytes 12582916
  12.3 11.3 %copy-start.1 = (s32[32,256]{1,0:T(8,128)S(1)}, s32[32,256]{1,0:T(8,128)}, u32[]{:S(2)}) copy-start(s32[32,256]{1,0:T(8,128)} %refs_6_.1) | copy-start | bytes 98308
  12.3 11.3 %copy-start.2 = (s32[1,256]{1,0:T(1,128)S(1)}, s32[1,256]{1,0:T(1,128)}, u32[]{:S(2)}) copy-start(s32[1,256]{1,0:T(1,128)} %refs_3_.3) | copy-start | bytes 3076
  12.3 11.2 %copy-start.3 = (s32[1,256]{1,0:T(1,128)S(1)}, s32[1,256]{1,0:T(1,128)}, u32[]{:S(2)}) copy-start(s32[1,256]{1,0:T(1,128)} %refs_4_.1) | copy-start | bytes 3076
  12.3 3.8 %collective-permute-start.1 = (f32[16,256]{1,0:T(8,128)S(1)}, f32[16,256]{1,0:T(8,128)S(1)}, u32[]{:S(2)}, u32[]{:S(2)}) collective-permute-start(f32[16,256]{1,0:T(8,128)S(1)} %get-tuple-element.33), channel_id=1, source_target_pairs={{0,16},{8,24},{16,0},{24,8},{1,17},{9,25},{17,1},{25,9},{2,18},{10... | collective-permute-start | bytes 49160 | tf_op jit(solution)/shard_map/ppermute | solution.py:447
  16.1 10.4 %collective-permute-start.7 = (f32[25,16,256]{2,1,0:T(8,128)S(1)}, f32[25,16,256]{2,1,0:T(8,128)S(1)}, u32[]{:S(2)}, u32[]{:S(2)}) collective-permute-start(f32[25,16,256]{2,1,0:T(8,128)S(1)} %get-tuple-element.42), channel_id=1, source_target_pairs={{0,16},{8,24},{16,0},{24,8},{1,17},{9,25},{17,1},{25,9},{2,18},{10... | collective-permute-start | bytes 1228808 | tf_op jit(solution)/shard_map/ppermute | solution.py:449
  16.7 3.7 %collective-permute-start.6 = (f32[24,16,256]{2,1,0:T(8,128)S(1)}, f32[24,16,256]{2,1,0:T(8,128)S(1)}, u32[]{:S(2)}, u32[]{:S(2)}) collective-permute-start(f32[24,16,256]{2,1,0:T(8,128)S(1)} %collective-permute-done.5.first), channel_id=1, source_target_pairs={{0,8},{8,0},{16,24},{24,16},{1,9},{9,1},{17,25},{25,17},{2,10},{10... | collective-permute-start | bytes 1179656 | tf_op jit(solution)/shard_map/ppermute | solution.py:450
  16.7 5.0 %collective-permute-start.2 = (f32[16,256]{1,0:T(8,128)S(1)}, f32[16,256]{1,0:T(8,128)S(1)}, u32[]{:S(2)}, u32[]{:S(2)}) collective-permute-start(f32[16,256]{1,0:T(8,128)S(1)} %add.3.sums), channel_id=1, source_target_pairs={{0,1},{2,3},{4,5},{6,7},{1,0},{3,2},{5,4},{7,6},{8,9},{10,11},{12,... | collective-permute-start | bytes 49160 | tf_op jit(solution)/shard_map/ppermute | solution.py:378
  18.3 3.7 %collective-permute-start.3 = (f32[16,256]{1,0:T(8,128)S(1)}, f32[16,256]{1,0:T(8,128)S(1)}, u32[]{:S(2)}, u32[]{:S(2)}) collective-permute-start(f32[16,256]{1,0:T(8,128)S(1)} %add.3.sums), channel_id=1, source_target_pairs={{1,2},{5,6},{0,4},{3,7},{2,1},{6,5},{4,0},{7,3},{9,10},{13,14},{8,... | collective-permute-start | bytes 49160 | tf_op jit(solution)/shard_map/ppermute | solution.py:378
  19.8 3.7 %collective-permute-start.4 = (f32[16,256]{1,0:T(8,128)S(1)}, f32[16,256]{1,0:T(8,128)S(1)}, u32[]{:S(2)}, u32[]{:S(2)}) collective-permute-start(f32[16,256]{1,0:T(8,128)S(1)} %add.3.sums), channel_id=1, source_target_pairs={{0,4},{1,5},{2,6},{3,7},{4,0},{5,1},{6,2},{7,3},{8,12},{9,13},{10,... | collective-permute-start | bytes 49160 | tf_op jit(solution)/shard_map/ppermute | solution.py:378

commit v6 on v5

--- a/solution.py
+++ b/solution.py
@@ -15,6 +15,7 @@
 TILE = 8
 CORES = 2
 SPAN = 256
+RUNS = 4
 RAW_SHARE = 51
 LIMIT = 12 * 2**20
 
@@ -314,12 +315,26 @@
         interior[:, place, :] = solved[:, place, :] - lifted
 
 
-def final_kernel(base, received, rest, interior):
+def final_kernel(base, received, rest, out, interior, ready):
     inner, share, elems = interior.shape
-    for part in range(share // TILE):
-        place = slice(part * TILE, (part + 1) * TILE)
-        block = dot3(rest[part], *split(octet(received[...], part)))
-        interior[:, place, :] = base[:, place, :] + block.reshape(inner, TILE, elems)
+    octets = range(share // TILE)
+    blocks = [split(octet(received[...], part)) for part in octets]
+    runs = ready.shape[0]
+    size = -(-inner // runs)
+    moves = []
+    for i in range(runs):
+        nodes = slice(i * size, min((i + 1) * size, inner))
+        for part in octets:
+            place = slice(part * TILE, (part + 1) * TILE)
+            high, low = (
+                rest[part, first + nodes.start * TILE : first + nodes.stop * TILE, :] for first in (0, inner * TILE)
+            )
+            product = dot(high, blocks[part][0]) + dot(low, blocks[part][0]) + dot(high, blocks[part][1])
+            interior[nodes, place, :] = base[nodes, place, :] + product.reshape(-1, TILE, elems)
+        moves.append(pltpu.make_async_copy(interior.at[nodes], out.at[nodes], ready.at[i]))
+        moves[-1].start()
+    for move in moves:
+        move.wait()
 
 
 VMEM = pl.BlockSpec(memory_space=pltpu.VMEM)
@@ -331,7 +346,7 @@
     return jax.ShapeDtypeStruct(dims, dtype)
 
 
-def kernel_call(body, outs, ins, name, micros, scratch=()):
+def kernel_call(body, outs, ins, name, micros, scratch=(), out_specs=None):
     in_specs, arrays = [], []
     for item in ins:
         place, array = item if isinstance(item, tuple) else ("", item)
@@ -343,7 +358,7 @@
         body,
         out_shape=outs,
         in_specs=in_specs,
-        out_specs=(VMEM,) * len(outs) if isinstance(outs, tuple) else VMEM,
+        out_specs=out_specs or ((VMEM,) * len(outs) if isinstance(outs, tuple) else VMEM),
         scratch_shapes=scratch,
         compiler_params=pltpu.CompilerParams(vmem_limit_bytes=LIMIT),
         cost_estimate=pl.CostEstimate(flops=0, transcendentals=0, bytes_accessed=int(micros * 3e6)),
@@ -465,7 +480,13 @@
         2.0,
     )
     interior = kernel_call(
-        final_kernel, shape(inner, share, elems), [base, ("vmem", received), rest], "interior_solve", 1.0
+        final_kernel,
+        shape(inner, share, elems),
+        [base, ("vmem", received), rest],
+        "interior_solve",
+        1.0,
+        [pltpu.VMEM((inner, share, elems), f32), pltpu.SemaphoreType.DMA((RUNS,))],
+        out_specs=ANY,
     )
     return (jnp.transpose(interior, (1, 0, 2)), interface)
 

time: 28.1 us -> 27.9 us (level)
  no operation moved by 1% of the time
where the time goes in v6:
time: 27.9 us; the launch traced here: 27.8 us
  Pallas kernels  13.4 us (48%)
  starting transfers between devices  7.4 us (27%)
  waiting for transfers between devices  6.21 us (22%)
  between operations  0.72 us (3%)
    pallas_call x6, Pallas kernels, kernel_call(): pl.pallas_call(body, out_shape=outs, in_specs=in_specs, out_specs=out_spe...  13.4 us
    ppermute x1, waiting for transfers between devices, paired(): lax.ppermute(sums_out, 'mode', across)  3.72 us
    ppermute x3, starting transfers between devices, exchanges(): got.append((lax.ppermute(block, ('ex', 'ey'), moves), tuple(code)))  3.67 us
    ppermute x1, starting transfers between devices, paired(): first = lax.ppermute(own_raw, 'mode', across)  2.59 us
    ppermute x3, waiting for transfers between devices, exchanges(): got.append((lax.ppermute(block, ('ex', 'ey'), moves), tuple(code)))  1.86 us
    ppermute x1, waiting for transfers between devices, paired(): received = lax.ppermute(send, 'mode', across)  0.62 us
  transfers between devices with their start and end apart: 8, of which 4 were waited for; matrix products, arithmetic and copies ran while one was open for 0% of the time, Pallas kernels for 40%

profile of v6, /device:TPU:0, one launch (start us, length us, event | category | flops | bytes accessed | tf_op | source)
XLA Modules:
  0.0 27.8 jit_solution(14374185668057116546)
XLA Ops:
  0.6 1.1 %raw_rows.1 = (f32[24,16,256]{2,1,0:T(8,128)S(1)}, f32[7,7]{1,0:T(8,128)S(1)}, f32[7]{0:T(128)S(1)}, f32[32,49]{1,0:T(8,128)S(1)}, s32[32,256]{1,0:T(8,128)S(1)}) custom-call(f32[81,16,256]{2,1,0:T(8,128)} %bitcast.2, f32[7,7]{1,0:T(8,128)} %refs_0_.1, f32[7]{0:T(128)} %refs_1_.1, f32[32,49]{1,0:T(8,128)} %refs_2_.1, s32[32,256]{1,0:T(8,128)} %refs_6_.1), custom_call_target="tpu_custom_call" | custom-call | bytes 1500000 | tf_op jit(solution)/shard_map/raw_rows/pallas_call | solution.py:357
  1.7 0.5 %collective-permute-start = (f32[81,16,256]{2,1,0:T(8,128)}, f32[81,16,256]{2,1,0:T(8,128)S(1)}, u32[]{:S(2)}, u32[]{:S(2)}) collective-permute-start(f32[81,16,256]{2,1,0:T(8,128)} %bitcast.3), channel_id=1, source_target_pairs={{0,8},{8,0},{16,24},{24,16},{1,9},{9,1},{17,25},{25,17},{2,10},{10... | collective-permute-start | bytes 3981320 | tf_op jit(solution)/shard_map/ppermute | solution.py:427
  2.2 2.6 %collective-permute-start.5 = (f32[24,16,256]{2,1,0:T(8,128)S(1)}, f32[24,16,256]{2,1,0:T(8,128)S(1)}, u32[]{:S(2)}, u32[]{:S(2)}) collective-permute-start(f32[24,16,256]{2,1,0:T(8,128)S(1)} %get-tuple-element.38), channel_id=1, source_target_pairs={{0,16},{8,24},{16,0},{24,8},{1,17},{9,25},{17,1},{25,9},{2,18},{10... | collective-permute-start | bytes 1179656 | tf_op jit(solution)/shard_map/ppermute | solution.py:426
  4.8 3.5 %tables.1 = (bf16[4,512,392]{2,1,0:T(8,128)(2,1)S(1)}, bf16[2,784,192]{2,1,0:T(8,128)(2,1)S(1)}, bf16[2,784,200]{2,1,0:T(8,128)(2,1)S(1)}, bf16[2,784,256]{2,1,0...) custom-call(f32[7,7]{1,0:T(8,128)S(1)} %get-tuple-element.23.basis, ...), custom_call_target="tpu_custom_call" | custom-call | bytes 7500000 | tf_op jit(solution)/shard_map/tables/pallas_call | solution.py:357
  8.3 0.0 collective-permute-done.mate
  8.3 0.0 copy-start
  8.3 3.9 %near_spectra.1 = (f32[16,256]{1,0:T(8,128)S(1)}, f32[16,256]{1,0:T(8,128)S(1)}, f32[25,16,256]{2,1,0:T(8,128)S(1)}, f32[49,16,256]{2,1,0:T(8,128)S(1)}) custom-call(f32[81,16,256]{2,1,0:T(8,128)S(1)} %get-tuple-element.29.own, f32[81,16,256]{2,1,0:T(8,128)S(1)} %collective-permute-done.mate, bf16[8192,256]{1,0:T(8,128)(2,1)S(1)} %get-tuple-element.30.where, ...), custom_call_target="tpu_custom_call" | custom-call | bytes 9000000 | tf_op jit(solution)/shard_map/near_spectra/pallas_call | solution.py:357
  12.3 0.0 copy-start.1
  12.3 0.0 copy-start.2
  12.3 0.0 copy-start.3
  12.3 0.1 collective-permute-start.1
  12.4 3.7 %collective-permute-done.1 = f32[16,256]{1,0:T(8,128)S(1)} collective-permute-done((f32[16,256]{1,0:T(8,128)S(1)}, f32[16,256]{1,0:T(8,128)S(1)}, u32[]{:S(2)}, u32[]{:S(2)}) %collective-permute-start.1) | collective-permute-done | bytes 16416 | tf_op jit(solution)/shard_map/ppermute | solution.py:462
  16.1 0.5 %collective-permute-start.7 = (f32[25,16,256]{2,1,0:T(8,128)S(1)}, f32[25,16,256]{2,1,0:T(8,128)S(1)}, u32[]{:S(2)}, u32[]{:S(2)}) collective-permute-start(f32[25,16,256]{2,1,0:T(8,128)S(1)} %get-tuple-element.42), channel_id=1, source_target_pairs={{0,16},{8,24},{16,0},{24,8},{1,17},{9,25},{17,1},{25,9},{2,18},{10... | collective-permute-start | bytes 1228808 | tf_op jit(solution)/shard_map/ppermute | solution.py:464
  16.7 0.0 collective-permute-done.5.first
  16.7 0.0 collective-permute-start.6
  16.7 1.6 %collective-permute-start.2 = (f32[16,256]{1,0:T(8,128)S(1)}, f32[16,256]{1,0:T(8,128)S(1)}, u32[]{:S(2)}, u32[]{:S(2)}) collective-permute-start(f32[16,256]{1,0:T(8,128)S(1)} %add.3.sums), channel_id=1, source_target_pairs={{0,1},{2,3},{4,5},{6,7},{1,0},{3,2},{5,4},{7,6},{8,9},{10,11},{12,... | collective-permute-start | bytes 49160 | tf_op jit(solution)/shard_map/ppermute | solution.py:393
  18.3 1.5 %collective-permute-start.3 = (f32[16,256]{1,0:T(8,128)S(1)}, f32[16,256]{1,0:T(8,128)S(1)}, u32[]{:S(2)}, u32[]{:S(2)}) collective-permute-start(f32[16,256]{1,0:T(8,128)S(1)} %add.3.sums), channel_id=1, source_target_pairs={{1,2},{5,6},{0,4},{3,7},{2,1},{6,5},{4,0},{7,3},{9,10},{13,14},{8,... | collective-permute-start | bytes 49160 | tf_op jit(solution)/shard_map/ppermute | solution.py:393
  19.8 0.5 %collective-permute-start.4 = (f32[16,256]{1,0:T(8,128)S(1)}, f32[16,256]{1,0:T(8,128)S(1)}, u32[]{:S(2)}, u32[]{:S(2)}) collective-permute-start(f32[16,256]{1,0:T(8,128)S(1)} %add.3.sums), channel_id=1, source_target_pairs={{0,4},{1,5},{2,6},{3,7},{4,0},{5,1},{6,2},{7,3},{8,12},{9,13},{10,... | collective-permute-start | bytes 49160 | tf_op jit(solution)/shard_map/ppermute | solution.py:393
  20.3 0.0 collective-permute-done.6.second
  20.3 1.3 %far_spectra.1.refs_8_ = f32[49,16,256]{2,1,0:T(8,128)S(1)} custom-call(f32[49,16,256]{2,1,0:T(8,128)S(1)} %get-tuple-element.37.keep, f32[24,16,256]{2,1,0:T(8,128)S(1)} %collective-permute-done.5.first, f32[24,16,256]{2,1,0:T(8,128)S(1)} %collective-permute-done.6.second, bf16[2,784,192]{2,1,0:T(8,128)(2,1)S(1)} %get-tuple-element.39.lead, ...), custom_call_target="tpu_custom_call" | custom-call | bytes 4500000 | tf_op jit(solution)/shard_map/far_spectra/pallas_call | solution.py:357
  21.7 0.0 collective-permute-done.2.refs_0_
  21.7 0.4 %collective-permute-done.3.refs_1_ = f32[16,256]{1,0:T(8,128)S(1)} collective-permute-done((f32[16,256]{1,0:T(8,128)S(1)}, f32[16,256]{1,0:T(8,128)S(1)}, u32[]{:S(2)}, u32[]{:S(2)}) %collective-permute-start.3) | collective-permute-done | bytes 16416 | tf_op jit(solution)/shard_map/ppermute | solution.py:393
  22.1 1.5 %collective-permute-done.4.refs_2_ = f32[16,256]{1,0:T(8,128)S(1)} collective-permute-done((f32[16,256]{1,0:T(8,128)S(1)}, f32[16,256]{1,0:T(8,128)S(1)}, u32[]{:S(2)}, u32[]{:S(2)}) %collective-permute-start.4) | collective-permute-done | bytes 16416 | tf_op jit(solution)/shard_map/ppermute | solution.py:393
  23.5 0.0 copy-done
  23.5 0.0 copy-done.1
  23.6 0.0 copy-done.2
  23.6 0.0 copy-done.3
  23.6 2.3 %back_solve.1 = (f32[49,16,256]{2,1,0:T(8,128)S(1)}, f32[16,1,256]{2,1,0:T(1,128)}) custom-call(f32[16,256]{1,0:T(8,128)S(1)} %add.3.sums, f32[16,256]{1,0:T(8,128)S(1)} %collective-permute-done.2.refs_0_, f32[16,256]{1,0:T(8,128)S(1)} %collective-permute-done.3.refs_1_, f32[16,256]{1,0:T(8,128)S(1)} %collective-permute-done.4.refs_2_, ...), custom_call_target="tpu_custom_call" | custom-call | bytes 6000000 | tf_op jit(solution)/shard_map/back_solve/pallas_call | solution.py:357
  25.9 0.6 %collective-permute-done.7.received = f32[25,16,256]{2,1,0:T(8,128)S(1)} collective-permute-done((f32[25,16,256]{2,1,0:T(8,128)S(1)}, f32[25,16,256]{2,1,0:T(8,128)S(1)}, u32[]{:S(2)}, u32[]{:S(2)}) %collective-permute-start.7) | collective-permute-done | bytes 409632 | tf_op jit(solution)/shard_map/ppermute | solution.py:464
  26.5 1.3 %interior_solve.1 = f32[49,16,256]{2,1,0:T(8,128)} custom-call(f32[49,16,256]{2,1,0:T(8,128)S(1)} %get-tuple-element.41.base, f32[25,16,256]{2,1,0:T(8,128)S(1)} %collective-permute-done.7.received, bf16[2,784,200]{2,1,0:T(8,128)(2,1)S(1)} %get-tuple-element.40.rest), custom_call_target="tpu_custom_call" | custom-call | bytes 3000000 | tf_op jit(solution)/shard_map/interior_solve/pallas_call | solution.py:357
  (1 shorter events, 0.0 us)
Async XLA Ops:
  1.7 6.6 %collective-permute-start = (f32[81,16,256]{2,1,0:T(8,128)}, f32[81,16,256]{2,1,0:T(8,128)S(1)}, u32[]{:S(2)}, u32[]{:S(2)}) collective-permute-start(f32[81,16,256]{2,1,0:T(8,128)} %bitcast.3), channel_id=1, source_target_pairs={{0,8},{8,0},{16,24},{24,16},{1,9},{9,1},{17,25},{25,17},{2,10},{10... | collective-permute-start | bytes 3981320 | tf_op jit(solution)/shard_map/ppermute | solution.py:427
  2.2 14.4 %collective-permute-start.5 = (f32[24,16,256]{2,1,0:T(8,128)S(1)}, f32[24,16,256]{2,1,0:T(8,128)S(1)}, u32[]{:S(2)}, u32[]{:S(2)}) collective-permute-start(f32[24,16,256]{2,1,0:T(8,128)S(1)} %get-tuple-element.38), channel_id=1, source_target_pairs={{0,16},{8,24},{16,0},{24,8},{1,17},{9,25},{17,1},{25,9},{2,18},{10... | collective-permute-start | bytes 1179656 | tf_op jit(solution)/shard_map/ppermute | solution.py:426
  8.3 15.2 %copy-start = (f32[16,256,256]{2,1,0:T(8,128)S(1)}, f32[16,256,256]{2,1,0:T(8,128)}, u32[]{:S(2)}) copy-start(f32[16,256,256]{2,1,0:T(8,128)} %refs_5_.1) | copy-start | bytes 12582916
  12.3 11.3 %copy-start.1 = (s32[32,256]{1,0:T(8,128)S(1)}, s32[32,256]{1,0:T(8,128)}, u32[]{:S(2)}) copy-start(s32[32,256]{1,0:T(8,128)} %refs_6_.1) | copy-start | bytes 98308
  12.3 11.3 %copy-start.2 = (s32[1,256]{1,0:T(1,128)S(1)}, s32[1,256]{1,0:T(1,128)}, u32[]{:S(2)}) copy-start(s32[1,256]{1,0:T(1,128)} %refs_3_.3) | copy-start | bytes 3076
  12.3 11.2 %copy-start.3 = (s32[1,256]{1,0:T(1,128)S(1)}, s32[1,256]{1,0:T(1,128)}, u32[]{:S(2)}) copy-start(s32[1,256]{1,0:T(1,128)} %refs_4_.1) | copy-start | bytes 3076
  12.3 3.8 %collective-permute-start.1 = (f32[16,256]{1,0:T(8,128)S(1)}, f32[16,256]{1,0:T(8,128)S(1)}, u32[]{:S(2)}, u32[]{:S(2)}) collective-permute-start(f32[16,256]{1,0:T(8,128)S(1)} %get-tuple-element.33), channel_id=1, source_target_pairs={{0,16},{8,24},{16,0},{24,8},{1,17},{9,25},{17,1},{25,9},{2,18},{10... | collective-permute-start | bytes 49160 | tf_op jit(solution)/shard_map/ppermute | solution.py:462
  16.1 10.4 %collective-permute-start.7 = (f32[25,16,256]{2,1,0:T(8,128)S(1)}, f32[25,16,256]{2,1,0:T(8,128)S(1)}, u32[]{:S(2)}, u32[]{:S(2)}) collective-permute-start(f32[25,16,256]{2,1,0:T(8,128)S(1)} %get-tuple-element.42), channel_id=1, source_target_pairs={{0,16},{8,24},{16,0},{24,8},{1,17},{9,25},{17,1},{25,9},{2,18},{10... | collective-permute-start | bytes 1228808 | tf_op jit(solution)/shard_map/ppermute | solution.py:464
  16.7 3.7 %collective-permute-start.6 = (f32[24,16,256]{2,1,0:T(8,128)S(1)}, f32[24,16,256]{2,1,0:T(8,128)S(1)}, u32[]{:S(2)}, u32[]{:S(2)}) collective-permute-start(f32[24,16,256]{2,1,0:T(8,128)S(1)} %collective-permute-done.5.first), channel_id=1, source_target_pairs={{0,8},{8,0},{16,24},{24,16},{1,9},{9,1},{17,25},{25,17},{2,10},{10... | collective-permute-start | bytes 1179656 | tf_op jit(solution)/shard_map/ppermute | solution.py:465
  16.7 5.0 %collective-permute-start.2 = (f32[16,256]{1,0:T(8,128)S(1)}, f32[16,256]{1,0:T(8,128)S(1)}, u32[]{:S(2)}, u32[]{:S(2)}) collective-permute-start(f32[16,256]{1,0:T(8,128)S(1)} %add.3.sums), channel_id=1, source_target_pairs={{0,1},{2,3},{4,5},{6,7},{1,0},{3,2},{5,4},{7,6},{8,9},{10,11},{12,... | collective-permute-start | bytes 49160 | tf_op jit(solution)/shard_map/ppermute | solution.py:393
  18.3 3.7 %collective-permute-start.3 = (f32[16,256]{1,0:T(8,128)S(1)}, f32[16,256]{1,0:T(8,128)S(1)}, u32[]{:S(2)}, u32[]{:S(2)}) collective-permute-start(f32[16,256]{1,0:T(8,128)S(1)} %add.3.sums), channel_id=1, source_target_pairs={{1,2},{5,6},{0,4},{3,7},{2,1},{6,5},{4,0},{7,3},{9,10},{13,14},{8,... | collective-permute-start | bytes 49160 | tf_op jit(solution)/shard_map/ppermute | solution.py:393
  19.8 3.7 %collective-permute-start.4 = (f32[16,256]{1,0:T(8,128)S(1)}, f32[16,256]{1,0:T(8,128)S(1)}, u32[]{:S(2)}, u32[]{:S(2)}) collective-permute-start(f32[16,256]{1,0:T(8,128)S(1)} %add.3.sums), channel_id=1, source_target_pairs={{0,4},{1,5},{2,6},{3,7},{4,0},{5,1},{6,2},{7,3},{8,12},{9,13},{10,... | collective-permute-start | bytes 49160 | tf_op jit(solution)/shard_map/ppermute | solution.py:393

commit v7 on v6

--- a/solution.py
+++ b/solution.py
@@ -214,7 +214,8 @@
     couple = exact(coupling[...], kron)
     device = lax.axis_index("mode")
     share = octets * TILE
-    both = jnp.concatenate([couple, kron], axis=0)
+    spare = lead.shape[1] // (2 * TILE) - inner
+    both = jnp.concatenate([couple, kron, jnp.zeros((spare, inner), f32)], axis=0)
     right = jnp.concatenate([kron, couple], axis=0).T
     per_mode(stack_split(couple), right, values, device ^ CORES, share, devices, modes)
     for part in range(octets):
@@ -222,10 +223,12 @@
     per_mode(stack_split(both), right, values, device, share, devices, modes)
     top = rim * TILE
     for part in range(octets):
-        halves = widened(modes, part, rim + inner, rim + inner)
+        halves = widened(modes, part, rim + inner + spare, rim + inner)
 
         def put(out, place, rows, cols):
-            out[place] = jnp.concatenate([half[rows, cols] for half in halves], axis=0)
+            height = out.shape[1] // 2
+            for i, half in enumerate(halves):
+                out[place, i * height : (i + 1) * height, :] = half[rows, cols]
 
         put(table, octets + part, slice(0, top), slice(0, edge))
         put(lead, part, slice(top, None), slice(0, first))
@@ -281,7 +284,7 @@
         place = slice(part * TILE, (part + 1) * TILE)
         block = dot3(lead[part], *split(octet(spectral[...], part)))
         block = block + dot3(rest[part], *split(keep[rows:, place, :].reshape(-1, elems)))
-        solved[:, place, :] = block.reshape(inner, TILE, elems)
+        solved[:, place, :] = block[: inner * TILE].reshape(inner, TILE, elems)
 
 
 def back_kernel(sums, *refs, codes):
@@ -311,7 +314,7 @@
     boundary = [chosen(values, slots[j : j + 1, :]) for j in range(rim)]
     for part, place in enumerate(octets):
         block = jnp.concatenate([blocks[part] for blocks in boundary], axis=0)
-        lifted = dot3(pull[part], *split(block)).reshape(inner, TILE, elems)
+        lifted = dot3(pull[part], *split(block))[: inner * TILE].reshape(inner, TILE, elems)
         interior[:, place, :] = solved[:, place, :] - lifted
 
 
@@ -319,18 +322,19 @@
     inner, share, elems = interior.shape
     octets = range(share // TILE)
     blocks = [split(octet(received[...], part)) for part in octets]
-    runs = ready.shape[0]
-    size = -(-inner // runs)
+    height = rest.shape[1] // 2
+    size = -(-inner // RUNS)
+    size += size % 2
     moves = []
-    for i in range(runs):
-        nodes = slice(i * size, min((i + 1) * size, inner))
+    for i, first in enumerate(range(0, inner, size)):
+        nodes = slice(first, min(first + size, inner))
+        count = nodes.stop - first
+        tall = (count + count % 2) * TILE
         for part in octets:
             place = slice(part * TILE, (part + 1) * TILE)
-            high, low = (
-                rest[part, first + nodes.start * TILE : first + nodes.stop * TILE, :] for first in (0, inner * TILE)
-            )
+            high, low = (rest[part, start + first * TILE : start + first * TILE + tall, :] for start in (0, height))
             product = dot(high, blocks[part][0]) + dot(low, blocks[part][0]) + dot(high, blocks[part][1])
-            interior[nodes, place, :] = base[nodes, place, :] + product.reshape(-1, TILE, elems)
+            interior[nodes, place, :] = base[nodes, place, :] + product[: count * TILE].reshape(-1, TILE, elems)
         moves.append(pltpu.make_async_copy(interior.at[nodes], out.at[nodes], ready.at[i]))
         moves[-1].start()
     for move in moves:
@@ -426,13 +430,14 @@
     first = lax.ppermute(own_raw, "mode", across)
     mate_planes = lax.ppermute(planes, "mode", mates)
     tall = 2 * TILE
+    padded = inner + inner % 2
     table, lead, rest, pull, where, own_planes = kernel_call(
         functools.partial(tables_kernel, devices=modes),
         (
             shape(2 * octets, tall * rim, inner * TILE, dtype=bf16),
-            shape(octets, tall * inner, raw_rows * TILE, dtype=bf16),
-            shape(octets, tall * inner, rest_rows * TILE, dtype=bf16),
-            shape(octets, tall * inner, rim * TILE, dtype=bf16),
+            shape(octets, tall * padded, raw_rows * TILE, dtype=bf16),
+            shape(octets, tall * padded, rest_rows * TILE, dtype=bf16),
+            shape(octets, tall * padded, rim * TILE, dtype=bf16),
             shape(rim * elems, unknowns, dtype=bf16),
             shape(*planes.shape),
         ),

time: 27.9 us -> 27.8 us (level)
  Pallas kernels: 13.4 us -> 12.8 us
  waiting for transfers between devices: 6.21 us -> 6.71 us
    pallas_call x6, Pallas kernels: 13.4 us -> 12.8 us  [kernel_call(): pl.pallas_call(body, out_shape=outs, in_specs=in_specs, out_specs=out_spe...]
    ppermute x1, waiting for transfers between devices: 0.62 us -> 1.1 us  [paired(): received = lax.ppermute(send, 'mode', across)]
  transfers between devices with their start and end apart: 8 -> 8, of which waited for: 4 -> 4; matrix products, arithmetic and copies ran while one was open for 0% -> 0% of each run, Pallas kernels for 40% -> 38%
where the time goes in v7:
time: 27.8 us; the launch traced here: 27.7 us
  Pallas kernels  12.8 us (46%)
  starting transfers between devices  7.46 us (27%)
  waiting for transfers between devices  6.71 us (24%)
  between operations  0.73 us (3%)
    pallas_call x6, Pallas kernels, kernel_call(): pl.pallas_call(body, out_shape=outs, in_specs=in_specs, out_specs=out_spe...  12.8 us
    ppermute x1, waiting for transfers between devices, paired(): lax.ppermute(sums_out, 'mode', across)  3.72 us
    ppermute x3, starting transfers between devices, exchanges(): got.append((lax.ppermute(block, ('ex', 'ey'), moves), tuple(code)))  3.67 us
    ppermute x1, starting transfers between devices, paired(): first = lax.ppermute(own_raw, 'mode', across)  2.59 us
    ppermute x3, waiting for transfers between devices, exchanges(): got.append((lax.ppermute(block, ('ex', 'ey'), moves), tuple(code)))  1.88 us
    ppermute x1, waiting for transfers between devices, paired(): received = lax.ppermute(send, 'mode', across)  1.1 us
    ppermute x1, starting transfers between devices, paired(): received = lax.ppermute(send, 'mode', across)  0.6 us
  transfers between devices with their start and end apart: 8, of which 4 were waited for; matrix products, arithmetic and copies ran while one was open for 0% of the time, Pallas kernels for 38%

profile of v7, /device:TPU:0, one launch (start us, length us, event | category | flops | bytes accessed | tf_op | source)
XLA Modules:
  0.0 27.7 jit_solution(16361442108041102119)
XLA Ops:
  0.6 1.1 %raw_rows.1 = (f32[24,16,256]{2,1,0:T(8,128)S(1)}, f32[7,7]{1,0:T(8,128)S(1)}, f32[7]{0:T(128)S(1)}, f32[32,49]{1,0:T(8,128)S(1)}, s32[32,256]{1,0:T(8,128)S(1)}) custom-call(f32[81,16,256]{2,1,0:T(8,128)} %bitcast.2, f32[7,7]{1,0:T(8,128)} %refs_0_.1, f32[7]{0:T(128)} %refs_1_.1, f32[32,49]{1,0:T(8,128)} %refs_2_.1, s32[32,256]{1,0:T(8,128)} %refs_6_.1), custom_call_target="tpu_custom_call" | custom-call | bytes 1500000 | tf_op jit(solution)/shard_map/raw_rows/pallas_call | solution.py:361
  1.7 0.5 %collective-permute-start = (f32[81,16,256]{2,1,0:T(8,128)}, f32[81,16,256]{2,1,0:T(8,128)S(1)}, u32[]{:S(2)}, u32[]{:S(2)}) collective-permute-start(f32[81,16,256]{2,1,0:T(8,128)} %bitcast.3), channel_id=1, source_target_pairs={{0,8},{8,0},{16,24},{24,16},{1,9},{9,1},{17,25},{25,17},{2,10},{10... | collective-permute-start | bytes 3981320 | tf_op jit(solution)/shard_map/ppermute | solution.py:431
  2.2 2.6 %collective-permute-start.5 = (f32[24,16,256]{2,1,0:T(8,128)S(1)}, f32[24,16,256]{2,1,0:T(8,128)S(1)}, u32[]{:S(2)}, u32[]{:S(2)}) collective-permute-start(f32[24,16,256]{2,1,0:T(8,128)S(1)} %get-tuple-element.38), channel_id=1, source_target_pairs={{0,16},{8,24},{16,0},{24,8},{1,17},{9,25},{17,1},{25,9},{2,18},{10... | collective-permute-start | bytes 1179656 | tf_op jit(solution)/shard_map/ppermute | solution.py:430
  4.8 3.4 %tables.1 = (bf16[4,512,392]{2,1,0:T(8,128)(2,1)S(1)}, bf16[2,800,192]{2,1,0:T(8,128)(2,1)S(1)}, bf16[2,800,200]{2,1,0:T(8,128)(2,1)S(1)}, bf16[2,800,256]{2,1,0...) custom-call(f32[7,7]{1,0:T(8,128)S(1)} %get-tuple-element.23.basis, ...), custom_call_target="tpu_custom_call" | custom-call | bytes 7500000 | tf_op jit(solution)/shard_map/tables/pallas_call | solution.py:361
  8.3 0.0 collective-permute-done.mate
  8.3 0.0 copy-start
  8.3 3.9 %near_spectra.1 = (f32[16,256]{1,0:T(8,128)S(1)}, f32[16,256]{1,0:T(8,128)S(1)}, f32[25,16,256]{2,1,0:T(8,128)S(1)}, f32[49,16,256]{2,1,0:T(8,128)S(1)}) custom-call(f32[81,16,256]{2,1,0:T(8,128)S(1)} %get-tuple-element.29.own, f32[81,16,256]{2,1,0:T(8,128)S(1)} %collective-permute-done.mate, bf16[8192,256]{1,0:T(8,128)(2,1)S(1)} %get-tuple-element.30.where, ...), custom_call_target="tpu_custom_call" | custom-call | bytes 9000000 | tf_op jit(solution)/shard_map/near_spectra/pallas_call | solution.py:361
  12.2 0.0 copy-start.1
  12.2 0.0 copy-start.2
  12.2 0.0 copy-start.3
  12.3 0.1 collective-permute-start.1
  12.3 3.7 %collective-permute-done.1 = f32[16,256]{1,0:T(8,128)S(1)} collective-permute-done((f32[16,256]{1,0:T(8,128)S(1)}, f32[16,256]{1,0:T(8,128)S(1)}, u32[]{:S(2)}, u32[]{:S(2)}) %collective-permute-start.1) | collective-permute-done | bytes 16416 | tf_op jit(solution)/shard_map/ppermute | solution.py:467
  16.1 0.6 %collective-permute-start.7 = (f32[25,16,256]{2,1,0:T(8,128)S(1)}, f32[25,16,256]{2,1,0:T(8,128)S(1)}, u32[]{:S(2)}, u32[]{:S(2)}) collective-permute-start(f32[25,16,256]{2,1,0:T(8,128)S(1)} %get-tuple-element.42), channel_id=1, source_target_pairs={{0,16},{8,24},{16,0},{24,8},{1,17},{9,25},{17,1},{25,9},{2,18},{10... | collective-permute-start | bytes 1228808 | tf_op jit(solution)/shard_map/ppermute | solution.py:469
  16.7 0.0 collective-permute-done.5.first
  16.7 0.0 collective-permute-start.6
  16.7 1.6 %collective-permute-start.2 = (f32[16,256]{1,0:T(8,128)S(1)}, f32[16,256]{1,0:T(8,128)S(1)}, u32[]{:S(2)}, u32[]{:S(2)}) collective-permute-start(f32[16,256]{1,0:T(8,128)S(1)} %add.3.sums), channel_id=1, source_target_pairs={{0,1},{2,3},{4,5},{6,7},{1,0},{3,2},{5,4},{7,6},{8,9},{10,11},{12,... | collective-permute-start | bytes 49160 | tf_op jit(solution)/shard_map/ppermute | solution.py:397
  18.3 1.5 %collective-permute-start.3 = (f32[16,256]{1,0:T(8,128)S(1)}, f32[16,256]{1,0:T(8,128)S(1)}, u32[]{:S(2)}, u32[]{:S(2)}) collective-permute-start(f32[16,256]{1,0:T(8,128)S(1)} %add.3.sums), channel_id=1, source_target_pairs={{1,2},{5,6},{0,4},{3,7},{2,1},{6,5},{4,0},{7,3},{9,10},{13,14},{8,... | collective-permute-start | bytes 49160 | tf_op jit(solution)/shard_map/ppermute | solution.py:397
  19.8 0.5 %collective-permute-start.4 = (f32[16,256]{1,0:T(8,128)S(1)}, f32[16,256]{1,0:T(8,128)S(1)}, u32[]{:S(2)}, u32[]{:S(2)}) collective-permute-start(f32[16,256]{1,0:T(8,128)S(1)} %add.3.sums), channel_id=1, source_target_pairs={{0,4},{1,5},{2,6},{3,7},{4,0},{5,1},{6,2},{7,3},{8,12},{9,13},{10,... | collective-permute-start | bytes 49160 | tf_op jit(solution)/shard_map/ppermute | solution.py:397
  20.3 0.0 collective-permute-done.6.second
  20.3 1.3 %far_spectra.1.refs_8_ = f32[49,16,256]{2,1,0:T(8,128)S(1)} custom-call(f32[49,16,256]{2,1,0:T(8,128)S(1)} %get-tuple-element.37.keep, f32[24,16,256]{2,1,0:T(8,128)S(1)} %collective-permute-done.5.first, f32[24,16,256]{2,1,0:T(8,128)S(1)} %collective-permute-done.6.second, bf16[2,800,192]{2,1,0:T(8,128)(2,1)S(1)} %get-tuple-element.39.lead, ...), custom_call_target="tpu_custom_call" | custom-call | bytes 4500000 | tf_op jit(solution)/shard_map/far_spectra/pallas_call | solution.py:361
  21.7 0.0 collective-permute-done.2.refs_0_
  21.7 0.4 %collective-permute-done.3.refs_1_ = f32[16,256]{1,0:T(8,128)S(1)} collective-permute-done((f32[16,256]{1,0:T(8,128)S(1)}, f32[16,256]{1,0:T(8,128)S(1)}, u32[]{:S(2)}, u32[]{:S(2)}) %collective-permute-start.3) | collective-permute-done | bytes 16416 | tf_op jit(solution)/shard_map/ppermute | solution.py:397
  22.1 1.5 %collective-permute-done.4.refs_2_ = f32[16,256]{1,0:T(8,128)S(1)} collective-permute-done((f32[16,256]{1,0:T(8,128)S(1)}, f32[16,256]{1,0:T(8,128)S(1)}, u32[]{:S(2)}, u32[]{:S(2)}) %collective-permute-start.4) | collective-permute-done | bytes 16416 | tf_op jit(solution)/shard_map/ppermute | solution.py:397
  23.5 0.0 copy-done
  23.5 0.0 copy-done.1
  23.6 0.0 copy-done.2
  23.6 0.0 copy-done.3
  23.6 1.8 %back_solve.1 = (f32[49,16,256]{2,1,0:T(8,128)S(1)}, f32[16,1,256]{2,1,0:T(1,128)}) custom-call(f32[16,256]{1,0:T(8,128)S(1)} %add.3.sums, f32[16,256]{1,0:T(8,128)S(1)} %collective-permute-done.2.refs_0_, f32[16,256]{1,0:T(8,128)S(1)} %collective-permute-done.3.refs_1_, f32[16,256]{1,0:T(8,128)S(1)} %collective-permute-done.4.refs_2_, ...), custom_call_target="tpu_custom_call" | custom-call | bytes 6000000 | tf_op jit(solution)/shard_map/back_solve/pallas_call | solution.py:361
  25.4 1.1 %collective-permute-done.7.received = f32[25,16,256]{2,1,0:T(8,128)S(1)} collective-permute-done((f32[25,16,256]{2,1,0:T(8,128)S(1)}, f32[25,16,256]{2,1,0:T(8,128)S(1)}, u32[]{:S(2)}, u32[]{:S(2)}) %collective-permute-start.7) | collective-permute-done | bytes 409632 | tf_op jit(solution)/shard_map/ppermute | solution.py:469
  26.4 1.2 %interior_solve.1 = f32[49,16,256]{2,1,0:T(8,128)} custom-call(f32[49,16,256]{2,1,0:T(8,128)S(1)} %get-tuple-element.41.base, f32[25,16,256]{2,1,0:T(8,128)S(1)} %collective-permute-done.7.received, bf16[2,800,200]{2,1,0:T(8,128)(2,1)S(1)} %get-tuple-element.40.rest), custom_call_target="tpu_custom_call" | custom-call | bytes 3000000 | tf_op jit(solution)/shard_map/interior_solve/pallas_call | solution.py:361
  (1 shorter events, 0.0 us)
Async XLA Ops:
  1.7 6.5 %collective-permute-start = (f32[81,16,256]{2,1,0:T(8,128)}, f32[81,16,256]{2,1,0:T(8,128)S(1)}, u32[]{:S(2)}, u32[]{:S(2)}) collective-permute-start(f32[81,16,256]{2,1,0:T(8,128)} %bitcast.3), channel_id=1, source_target_pairs={{0,8},{8,0},{16,24},{24,16},{1,9},{9,1},{17,25},{25,17},{2,10},{10... | collective-permute-start | bytes 3981320 | tf_op jit(solution)/shard_map/ppermute | solution.py:431
  2.2 14.4 %collective-permute-start.5 = (f32[24,16,256]{2,1,0:T(8,128)S(1)}, f32[24,16,256]{2,1,0:T(8,128)S(1)}, u32[]{:S(2)}, u32[]{:S(2)}) collective-permute-start(f32[24,16,256]{2,1,0:T(8,128)S(1)} %get-tuple-element.38), channel_id=1, source_target_pairs={{0,16},{8,24},{16,0},{24,8},{1,17},{9,25},{17,1},{25,9},{2,18},{10... | collective-permute-start | bytes 1179656 | tf_op jit(solution)/shard_map/ppermute | solution.py:430
  8.3 15.3 %copy-start = (f32[16,256,256]{2,1,0:T(8,128)S(1)}, f32[16,256,256]{2,1,0:T(8,128)}, u32[]{:S(2)}) copy-start(f32[16,256,256]{2,1,0:T(8,128)} %refs_5_.1) | copy-start | bytes 12582916
  12.2 11.3 %copy-start.1 = (s32[32,256]{1,0:T(8,128)S(1)}, s32[32,256]{1,0:T(8,128)}, u32[]{:S(2)}) copy-start(s32[32,256]{1,0:T(8,128)} %refs_6_.1) | copy-start | bytes 98308
  12.2 11.3 %copy-start.2 = (s32[1,256]{1,0:T(1,128)S(1)}, s32[1,256]{1,0:T(1,128)}, u32[]{:S(2)}) copy-start(s32[1,256]{1,0:T(1,128)} %refs_3_.3) | copy-start | bytes 3076
  12.2 11.3 %copy-start.3 = (s32[1,256]{1,0:T(1,128)S(1)}, s32[1,256]{1,0:T(1,128)}, u32[]{:S(2)}) copy-start(s32[1,256]{1,0:T(1,128)} %refs_4_.1) | copy-start | bytes 3076
  12.3 3.8 %collective-permute-start.1 = (f32[16,256]{1,0:T(8,128)S(1)}, f32[16,256]{1,0:T(8,128)S(1)}, u32[]{:S(2)}, u32[]{:S(2)}) collective-permute-start(f32[16,256]{1,0:T(8,128)S(1)} %get-tuple-element.33), channel_id=1, source_target_pairs={{0,16},{8,24},{16,0},{24,8},{1,17},{9,25},{17,1},{25,9},{2,18},{10... | collective-permute-start | bytes 49160 | tf_op jit(solution)/shard_map/ppermute | solution.py:467
  16.1 10.4 %collective-permute-start.7 = (f32[25,16,256]{2,1,0:T(8,128)S(1)}, f32[25,16,256]{2,1,0:T(8,128)S(1)}, u32[]{:S(2)}, u32[]{:S(2)}) collective-permute-start(f32[25,16,256]{2,1,0:T(8,128)S(1)} %get-tuple-element.42), channel_id=1, source_target_pairs={{0,16},{8,24},{16,0},{24,8},{1,17},{9,25},{17,1},{25,9},{2,18},{10... | collective-permute-start | bytes 1228808 | tf_op jit(solution)/shard_map/ppermute | solution.py:469
  16.7 3.7 %collective-permute-start.6 = (f32[24,16,256]{2,1,0:T(8,128)S(1)}, f32[24,16,256]{2,1,0:T(8,128)S(1)}, u32[]{:S(2)}, u32[]{:S(2)}) collective-permute-start(f32[24,16,256]{2,1,0:T(8,128)S(1)} %collective-permute-done.5.first), channel_id=1, source_target_pairs={{0,8},{8,0},{16,24},{24,16},{1,9},{9,1},{17,25},{25,17},{2,10},{10... | collective-permute-start | bytes 1179656 | tf_op jit(solution)/shard_map/ppermute | solution.py:470
  16.7 5.0 %collective-permute-start.2 = (f32[16,256]{1,0:T(8,128)S(1)}, f32[16,256]{1,0:T(8,128)S(1)}, u32[]{:S(2)}, u32[]{:S(2)}) collective-permute-start(f32[16,256]{1,0:T(8,128)S(1)} %add.3.sums), channel_id=1, source_target_pairs={{0,1},{2,3},{4,5},{6,7},{1,0},{3,2},{5,4},{7,6},{8,9},{10,11},{12,... | collective-permute-start | bytes 49160 | tf_op jit(solution)/shard_map/ppermute | solution.py:397
  18.3 3.7 %collective-permute-start.3 = (f32[16,256]{1,0:T(8,128)S(1)}, f32[16,256]{1,0:T(8,128)S(1)}, u32[]{:S(2)}, u32[]{:S(2)}) collective-permute-start(f32[16,256]{1,0:T(8,128)S(1)} %add.3.sums), channel_id=1, source_target_pairs={{1,2},{5,6},{0,4},{3,7},{2,1},{6,5},{4,0},{7,3},{9,10},{13,14},{8,... | collective-permute-start | bytes 49160 | tf_op jit(solution)/shard_map/ppermute | solution.py:397
  19.8 3.7 %collective-permute-start.4 = (f32[16,256]{1,0:T(8,128)S(1)}, f32[16,256]{1,0:T(8,128)S(1)}, u32[]{:S(2)}, u32[]{:S(2)}) collective-permute-start(f32[16,256]{1,0:T(8,128)S(1)} %add.3.sums), channel_id=1, source_target_pairs={{0,4},{1,5},{2,6},{3,7},{4,0},{5,1},{6,2},{7,3},{8,12},{9,13},{10,... | collective-permute-start | bytes 49160 | tf_op jit(solution)/shard_map/ppermute | solution.py:397

commit v8 on v7

--- a/solution.py
+++ b/solution.py
@@ -215,7 +215,7 @@
     device = lax.axis_index("mode")
     share = octets * TILE
     spare = lead.shape[1] // (2 * TILE) - inner
-    both = jnp.concatenate([couple, kron, jnp.zeros((spare, inner), f32)], axis=0)
+    both = jnp.concatenate([couple, kron, jnp.zeros((modes.shape[1] - rim - inner, inner), f32)], axis=0)
     right = jnp.concatenate([kron, couple], axis=0).T
     per_mode(stack_split(couple), right, values, device ^ CORES, share, devices, modes)
     for part in range(octets):
@@ -444,7 +444,7 @@
         [basis, values, coupling, ("any", planes), slots_held],
         "tables",
         2.5,
-        [pltpu.VMEM((share, -(-(inner + rim) // TILE) * TILE, inner + rim), f32), pltpu.SemaphoreType.DMA],
+        [pltpu.VMEM((share, -(-(padded + rim) // (2 * TILE)) * 2 * TILE, inner + rim), f32), pltpu.SemaphoreType.DMA],
     )
     sums_out, sums_own, send, keep = kernel_call(
         functools.partial(

time: 27.8 us -> 27.7 us (level)
  transfers between devices with their start and end apart: 8 -> 8, of which waited for: 4 -> 4; matrix products, arithmetic and copies ran while one was open for 0% -> 0% of each run, Pallas kernels for 38% -> 37%
where the time goes in v8:
time: 27.7 us; the launch traced here: 27.6 us
  Pallas kernels  12.7 us (46%)
  starting transfers between devices  7.54 us (27%)
  waiting for transfers between devices  6.63 us (24%)
  between operations  0.73 us (3%)
    pallas_call x6, Pallas kernels, kernel_call(): pl.pallas_call(body, out_shape=outs, in_specs=in_specs, out_specs=out_spe...  12.7 us
    ppermute x1, waiting for transfers between devices, paired(): lax.ppermute(sums_out, 'mode', across)  3.72 us
    ppermute x3, starting transfers between devices, exchanges(): got.append((lax.ppermute(block, ('ex', 'ey'), moves), tuple(code)))  3.67 us
    ppermute x1, starting transfers between devices, paired(): first = lax.ppermute(own_raw, 'mode', across)  2.59 us
    ppermute x3, waiting for transfers between devices, exchanges(): got.append((lax.ppermute(block, ('ex', 'ey'), moves), tuple(code)))  1.88 us
    ppermute x1, waiting for transfers between devices, paired(): received = lax.ppermute(send, 'mode', across)  1.01 us
    ppermute x1, starting transfers between devices, paired(): received = lax.ppermute(send, 'mode', across)  0.68 us
  transfers between devices with their start and end apart: 8, of which 4 were waited for; matrix products, arithmetic and copies ran while one was open for 0% of the time, Pallas kernels for 37%

profile of v8, /device:TPU:0, one launch (start us, length us, event | category | flops | bytes accessed | tf_op | source)
XLA Modules:
  0.0 27.6 jit_solution(163608192229503307)
XLA Ops:
  0.6 1.1 %raw_rows.1 = (f32[24,16,256]{2,1,0:T(8,128)S(1)}, f32[7,7]{1,0:T(8,128)S(1)}, f32[7]{0:T(128)S(1)}, f32[32,49]{1,0:T(8,128)S(1)}, s32[32,256]{1,0:T(8,128)S(1)}) custom-call(f32[81,16,256]{2,1,0:T(8,128)} %bitcast.2, f32[7,7]{1,0:T(8,128)} %refs_0_.1, f32[7]{0:T(128)} %refs_1_.1, f32[32,49]{1,0:T(8,128)} %refs_2_.1, s32[32,256]{1,0:T(8,128)} %refs_6_.1), custom_call_target="tpu_custom_call" | custom-call | bytes 1500000 | tf_op jit(solution)/shard_map/raw_rows/pallas_call | solution.py:361
  1.7 0.5 %collective-permute-start = (f32[81,16,256]{2,1,0:T(8,128)}, f32[81,16,256]{2,1,0:T(8,128)S(1)}, u32[]{:S(2)}, u32[]{:S(2)}) collective-permute-start(f32[81,16,256]{2,1,0:T(8,128)} %bitcast.3), channel_id=1, source_target_pairs={{0,8},{8,0},{16,24},{24,16},{1,9},{9,1},{17,25},{25,17},{2,10},{10... | collective-permute-start | bytes 3981320 | tf_op jit(solution)/shard_map/ppermute | solution.py:431
  2.2 2.6 %collective-permute-start.5 = (f32[24,16,256]{2,1,0:T(8,128)S(1)}, f32[24,16,256]{2,1,0:T(8,128)S(1)}, u32[]{:S(2)}, u32[]{:S(2)}) collective-permute-start(f32[24,16,256]{2,1,0:T(8,128)S(1)} %get-tuple-element.38), channel_id=1, source_target_pairs={{0,16},{8,24},{16,0},{24,8},{1,17},{9,25},{17,1},{25,9},{2,18},{10... | collective-permute-start | bytes 1179656 | tf_op jit(solution)/shard_map/ppermute | solution.py:430
  4.8 3.3 %tables.1 = (bf16[4,512,392]{2,1,0:T(8,128)(2,1)S(1)}, bf16[2,800,192]{2,1,0:T(8,128)(2,1)S(1)}, bf16[2,800,200]{2,1,0:T(8,128)(2,1)S(1)}, bf16[2,800,256]{2,1,0...) custom-call(f32[7,7]{1,0:T(8,128)S(1)} %get-tuple-element.23.basis, ...), custom_call_target="tpu_custom_call" | custom-call | bytes 7500000 | tf_op jit(solution)/shard_map/tables/pallas_call | solution.py:361
  8.2 0.0 collective-permute-done.mate
  8.2 0.0 copy-start
  8.2 3.9 %near_spectra.1 = (f32[16,256]{1,0:T(8,128)S(1)}, f32[16,256]{1,0:T(8,128)S(1)}, f32[25,16,256]{2,1,0:T(8,128)S(1)}, f32[49,16,256]{2,1,0:T(8,128)S(1)}) custom-call(f32[81,16,256]{2,1,0:T(8,128)S(1)} %get-tuple-element.29.own, f32[81,16,256]{2,1,0:T(8,128)S(1)} %collective-permute-done.mate, bf16[8192,256]{1,0:T(8,128)(2,1)S(1)} %get-tuple-element.30.where, ...), custom_call_target="tpu_custom_call" | custom-call | bytes 9000000 | tf_op jit(solution)/shard_map/near_spectra/pallas_call | solution.py:361
  12.1 0.0 copy-start.1
  12.1 0.0 copy-start.2
  12.2 0.0 copy-start.3
  12.2 0.1 collective-permute-start.1
  12.3 3.7 %collective-permute-done.1 = f32[16,256]{1,0:T(8,128)S(1)} collective-permute-done((f32[16,256]{1,0:T(8,128)S(1)}, f32[16,256]{1,0:T(8,128)S(1)}, u32[]{:S(2)}, u32[]{:S(2)}) %collective-permute-start.1) | collective-permute-done | bytes 16416 | tf_op jit(solution)/shard_map/ppermute | solution.py:467
  16.0 0.7 %collective-permute-start.7 = (f32[25,16,256]{2,1,0:T(8,128)S(1)}, f32[25,16,256]{2,1,0:T(8,128)S(1)}, u32[]{:S(2)}, u32[]{:S(2)}) collective-permute-start(f32[25,16,256]{2,1,0:T(8,128)S(1)} %get-tuple-element.42), channel_id=1, source_target_pairs={{0,16},{8,24},{16,0},{24,8},{1,17},{9,25},{17,1},{25,9},{2,18},{10... | collective-permute-start | bytes 1228808 | tf_op jit(solution)/shard_map/ppermute | solution.py:469
  16.7 0.0 collective-permute-done.5.first
  16.7 0.0 collective-permute-start.6
  16.7 1.6 %collective-permute-start.2 = (f32[16,256]{1,0:T(8,128)S(1)}, f32[16,256]{1,0:T(8,128)S(1)}, u32[]{:S(2)}, u32[]{:S(2)}) collective-permute-start(f32[16,256]{1,0:T(8,128)S(1)} %add.3.sums), channel_id=1, source_target_pairs={{0,1},{2,3},{4,5},{6,7},{1,0},{3,2},{5,4},{7,6},{8,9},{10,11},{12,... | collective-permute-start | bytes 49160 | tf_op jit(solution)/shard_map/ppermute | solution.py:397
  18.3 1.5 %collective-permute-start.3 = (f32[16,256]{1,0:T(8,128)S(1)}, f32[16,256]{1,0:T(8,128)S(1)}, u32[]{:S(2)}, u32[]{:S(2)}) collective-permute-start(f32[16,256]{1,0:T(8,128)S(1)} %add.3.sums), channel_id=1, source_target_pairs={{1,2},{5,6},{0,4},{3,7},{2,1},{6,5},{4,0},{7,3},{9,10},{13,14},{8,... | collective-permute-start | bytes 49160 | tf_op jit(solution)/shard_map/ppermute | solution.py:397
  19.8 0.5 %collective-permute-start.4 = (f32[16,256]{1,0:T(8,128)S(1)}, f32[16,256]{1,0:T(8,128)S(1)}, u32[]{:S(2)}, u32[]{:S(2)}) collective-permute-start(f32[16,256]{1,0:T(8,128)S(1)} %add.3.sums), channel_id=1, source_target_pairs={{0,4},{1,5},{2,6},{3,7},{4,0},{5,1},{6,2},{7,3},{8,12},{9,13},{10,... | collective-permute-start | bytes 49160 | tf_op jit(solution)/shard_map/ppermute | solution.py:397
  20.3 0.0 collective-permute-done.6.second
  20.3 1.3 %far_spectra.1.refs_8_ = f32[49,16,256]{2,1,0:T(8,128)S(1)} custom-call(f32[49,16,256]{2,1,0:T(8,128)S(1)} %get-tuple-element.37.keep, f32[24,16,256]{2,1,0:T(8,128)S(1)} %collective-permute-done.5.first, f32[24,16,256]{2,1,0:T(8,128)S(1)} %collective-permute-done.6.second, bf16[2,800,192]{2,1,0:T(8,128)(2,1)S(1)} %get-tuple-element.39.lead, ...), custom_call_target="tpu_custom_call" | custom-call | bytes 4500000 | tf_op jit(solution)/shard_map/far_spectra/pallas_call | solution.py:361
  21.7 0.0 collective-permute-done.2.refs_0_
  21.7 0.4 %collective-permute-done.3.refs_1_ = f32[16,256]{1,0:T(8,128)S(1)} collective-permute-done((f32[16,256]{1,0:T(8,128)S(1)}, f32[16,256]{1,0:T(8,128)S(1)}, u32[]{:S(2)}, u32[]{:S(2)}) %collective-permute-start.3) | collective-permute-done | bytes 16416 | tf_op jit(solution)/shard_map/ppermute | solution.py:397
  22.1 1.5 %collective-permute-done.4.refs_2_ = f32[16,256]{1,0:T(8,128)S(1)} collective-permute-done((f32[16,256]{1,0:T(8,128)S(1)}, f32[16,256]{1,0:T(8,128)S(1)}, u32[]{:S(2)}, u32[]{:S(2)}) %collective-permute-start.4) | collective-permute-done | bytes 16416 | tf_op jit(solution)/shard_map/ppermute | solution.py:397
  23.5 0.0 copy-done
  23.5 0.0 copy-done.1
  23.6 0.0 copy-done.2
  23.6 0.0 copy-done.3
  23.6 1.8 %back_solve.1 = (f32[49,16,256]{2,1,0:T(8,128)S(1)}, f32[16,1,256]{2,1,0:T(1,128)}) custom-call(f32[16,256]{1,0:T(8,128)S(1)} %add.3.sums, f32[16,256]{1,0:T(8,128)S(1)} %collective-permute-done.2.refs_0_, f32[16,256]{1,0:T(8,128)S(1)} %collective-permute-done.3.refs_1_, f32[16,256]{1,0:T(8,128)S(1)} %collective-permute-done.4.refs_2_, ...), custom_call_target="tpu_custom_call" | custom-call | bytes 6000000 | tf_op jit(solution)/shard_map/back_solve/pallas_call | solution.py:361
  25.4 1.0 %collective-permute-done.7.received = f32[25,16,256]{2,1,0:T(8,128)S(1)} collective-permute-done((f32[25,16,256]{2,1,0:T(8,128)S(1)}, f32[25,16,256]{2,1,0:T(8,128)S(1)}, u32[]{:S(2)}, u32[]{:S(2)}) %collective-permute-start.7) | collective-permute-done | bytes 409632 | tf_op jit(solution)/shard_map/ppermute | solution.py:469
  26.4 1.2 %interior_solve.1 = f32[49,16,256]{2,1,0:T(8,128)} custom-call(f32[49,16,256]{2,1,0:T(8,128)S(1)} %get-tuple-element.41.base, f32[25,16,256]{2,1,0:T(8,128)S(1)} %collective-permute-done.7.received, bf16[2,800,200]{2,1,0:T(8,128)(2,1)S(1)} %get-tuple-element.40.rest), custom_call_target="tpu_custom_call" | custom-call | bytes 3000000 | tf_op jit(solution)/shard_map/interior_solve/pallas_call | solution.py:361
  (1 shorter events, 0.0 us)
Async XLA Ops:
  1.7 6.4 %collective-permute-start = (f32[81,16,256]{2,1,0:T(8,128)}, f32[81,16,256]{2,1,0:T(8,128)S(1)}, u32[]{:S(2)}, u32[]{:S(2)}) collective-permute-start(f32[81,16,256]{2,1,0:T(8,128)} %bitcast.3), channel_id=1, source_target_pairs={{0,8},{8,0},{16,24},{24,16},{1,9},{9,1},{17,25},{25,17},{2,10},{10... | collective-permute-start | bytes 3981320 | tf_op jit(solution)/shard_map/ppermute | solution.py:431
  2.2 14.4 %collective-permute-start.5 = (f32[24,16,256]{2,1,0:T(8,128)S(1)}, f32[24,16,256]{2,1,0:T(8,128)S(1)}, u32[]{:S(2)}, u32[]{:S(2)}) collective-permute-start(f32[24,16,256]{2,1,0:T(8,128)S(1)} %get-tuple-element.38), channel_id=1, source_target_pairs={{0,16},{8,24},{16,0},{24,8},{1,17},{9,25},{17,1},{25,9},{2,18},{10... | collective-permute-start | bytes 1179656 | tf_op jit(solution)/shard_map/ppermute | solution.py:430
  8.2 15.4 %copy-start = (f32[16,256,256]{2,1,0:T(8,128)S(1)}, f32[16,256,256]{2,1,0:T(8,128)}, u32[]{:S(2)}) copy-start(f32[16,256,256]{2,1,0:T(8,128)} %refs_5_.1) | copy-start | bytes 12582916
  12.1 11.4 %copy-start.1 = (s32[32,256]{1,0:T(8,128)S(1)}, s32[32,256]{1,0:T(8,128)}, u32[]{:S(2)}) copy-start(s32[32,256]{1,0:T(8,128)} %refs_6_.1) | copy-start | bytes 98308
  12.1 11.4 %copy-start.2 = (s32[1,256]{1,0:T(1,128)S(1)}, s32[1,256]{1,0:T(1,128)}, u32[]{:S(2)}) copy-start(s32[1,256]{1,0:T(1,128)} %refs_3_.3) | copy-start | bytes 3076
  12.2 11.4 %copy-start.3 = (s32[1,256]{1,0:T(1,128)S(1)}, s32[1,256]{1,0:T(1,128)}, u32[]{:S(2)}) copy-start(s32[1,256]{1,0:T(1,128)} %refs_4_.1) | copy-start | bytes 3076
  12.2 3.8 %collective-permute-start.1 = (f32[16,256]{1,0:T(8,128)S(1)}, f32[16,256]{1,0:T(8,128)S(1)}, u32[]{:S(2)}, u32[]{:S(2)}) collective-permute-start(f32[16,256]{1,0:T(8,128)S(1)} %get-tuple-element.33), channel_id=1, source_target_pairs={{0,16},{8,24},{16,0},{24,8},{1,17},{9,25},{17,1},{25,9},{2,18},{10... | collective-permute-start | bytes 49160 | tf_op jit(solution)/shard_map/ppermute | solution.py:467
  16.0 10.4 %collective-permute-start.7 = (f32[25,16,256]{2,1,0:T(8,128)S(1)}, f32[25,16,256]{2,1,0:T(8,128)S(1)}, u32[]{:S(2)}, u32[]{:S(2)}) collective-permute-start(f32[25,16,256]{2,1,0:T(8,128)S(1)} %get-tuple-element.42), channel_id=1, source_target_pairs={{0,16},{8,24},{16,0},{24,8},{1,17},{9,25},{17,1},{25,9},{2,18},{10... | collective-permute-start | bytes 1228808 | tf_op jit(solution)/shard_map/ppermute | solution.py:469
  16.7 3.7 %collective-permute-start.6 = (f32[24,16,256]{2,1,0:T(8,128)S(1)}, f32[24,16,256]{2,1,0:T(8,128)S(1)}, u32[]{:S(2)}, u32[]{:S(2)}) collective-permute-start(f32[24,16,256]{2,1,0:T(8,128)S(1)} %collective-permute-done.5.first), channel_id=1, source_target_pairs={{0,8},{8,0},{16,24},{24,16},{1,9},{9,1},{17,25},{25,17},{2,10},{10... | collective-permute-start | bytes 1179656 | tf_op jit(solution)/shard_map/ppermute | solution.py:470
  16.7 5.0 %collective-permute-start.2 = (f32[16,256]{1,0:T(8,128)S(1)}, f32[16,256]{1,0:T(8,128)S(1)}, u32[]{:S(2)}, u32[]{:S(2)}) collective-permute-start(f32[16,256]{1,0:T(8,128)S(1)} %add.3.sums), channel_id=1, source_target_pairs={{0,1},{2,3},{4,5},{6,7},{1,0},{3,2},{5,4},{7,6},{8,9},{10,11},{12,... | collective-permute-start | bytes 49160 | tf_op jit(solution)/shard_map/ppermute | solution.py:397
  18.3 3.7 %collective-permute-start.3 = (f32[16,256]{1,0:T(8,128)S(1)}, f32[16,256]{1,0:T(8,128)S(1)}, u32[]{:S(2)}, u32[]{:S(2)}) collective-permute-start(f32[16,256]{1,0:T(8,128)S(1)} %add.3.sums), channel_id=1, source_target_pairs={{1,2},{5,6},{0,4},{3,7},{2,1},{6,5},{4,0},{7,3},{9,10},{13,14},{8,... | collective-permute-start | bytes 49160 | tf_op jit(solution)/shard_map/ppermute | solution.py:397
  19.8 3.7 %collective-permute-start.4 = (f32[16,256]{1,0:T(8,128)S(1)}, f32[16,256]{1,0:T(8,128)S(1)}, u32[]{:S(2)}, u32[]{:S(2)}) collective-permute-start(f32[16,256]{1,0:T(8,128)S(1)} %add.3.sums), channel_id=1, source_target_pairs={{0,4},{1,5},{2,6},{3,7},{4,0},{5,1},{6,2},{7,3},{8,12},{9,13},{10,... | collective-permute-start | bytes 49160 | tf_op jit(solution)/shard_map/ppermute | solution.py:397

commit v9 on v8

--- a/solution.py
+++ b/solution.py
@@ -426,7 +426,6 @@
     )
     eigen_basis, eigen_values, coupling, slots_held = small
     basis, values = ("smem", eigen_basis), ("smem", eigen_values)
-    planes, own_raw = lax.optimization_barrier((planes, own_raw))
     first = lax.ppermute(own_raw, "mode", across)
     mate_planes = lax.ppermute(planes, "mode", mates)
     tall = 2 * TILE

time: 27.7 us -> 27.8 us (level)
  transfers between devices with their start and end apart: 8 -> 8, of which waited for: 4 -> 4; matrix products, arithmetic and copies ran while one was open for 0% -> 0% of each run, Pallas kernels for 37% -> 41%
where the time goes in v9:
time: 27.8 us; the launch traced here: 27.6 us
  Pallas kernels  12.7 us (46%)
  starting transfers between devices  7.61 us (27%)
  waiting for transfers between devices  6.61 us (24%)
  between operations  0.73 us (3%)
    pallas_call x6, Pallas kernels, kernel_call(): pl.pallas_call(body, out_shape=outs, in_specs=in_specs, out_specs=out_spe...  12.7 us
    ppermute x1, waiting for transfers between devices, paired(): lax.ppermute(sums_out, 'mode', across)  3.71 us
    ppermute x3, starting transfers between devices, exchanges(): got.append((lax.ppermute(block, ('ex', 'ey'), moves), tuple(code)))  3.67 us
    ppermute x1, starting transfers between devices, paired(): first = lax.ppermute(own_raw, 'mode', across)  2.6 us
    ppermute x3, waiting for transfers between devices, exchanges(): got.append((lax.ppermute(block, ('ex', 'ey'), moves), tuple(code)))  1.88 us
    ppermute x1, waiting for transfers between devices, paired(): received = lax.ppermute(send, 'mode', across)  1.01 us
    ppermute x1, starting transfers between devices, paired(): received = lax.ppermute(send, 'mode', across)  0.73 us
  transfers between devices with their start and end apart: 8, of which 4 were waited for; matrix products, arithmetic and copies ran while one was open for 0% of the time, Pallas kernels for 41%

profile of v9, /device:TPU:0, one launch (start us, length us, event | category | flops | bytes accessed | tf_op | source)
XLA Modules:
  0.0 27.6 jit_solution(8899966243805610106)
XLA Ops:
  0.6 0.5 %collective-permute-start = (f32[81,16,256]{2,1,0:T(8,128)}, f32[81,16,256]{2,1,0:T(8,128)S(1)}, u32[]{:S(2)}, u32[]{:S(2)}) collective-permute-start(f32[81,16,256]{2,1,0:T(8,128)} %bitcast.2), channel_id=1, source_target_pairs={{0,8},{8,0},{16,24},{24,16},{1,9},{9,1},{17,25},{25,17},{2,10},{10... | collective-permute-start | bytes 3981320 | tf_op jit(solution)/shard_map/ppermute | solution.py:430
  1.1 1.1 %raw_rows.1 = (f32[24,16,256]{2,1,0:T(8,128)S(1)}, f32[7,7]{1,0:T(8,128)S(1)}, f32[7]{0:T(128)S(1)}, f32[32,49]{1,0:T(8,128)S(1)}, s32[32,256]{1,0:T(8,128)S(1)}) custom-call(f32[81,16,256]{2,1,0:T(8,128)} %bitcast.3, f32[7,7]{1,0:T(8,128)} %refs_0_.1, f32[7]{0:T(128)} %refs_1_.1, f32[32,49]{1,0:T(8,128)} %refs_2_.1, s32[32,256]{1,0:T(8,128)} %refs_6_.1), custom_call_target="tpu_custom_call" | custom-call | bytes 1500000 | tf_op jit(solution)/shard_map/raw_rows/pallas_call | solution.py:361
  2.2 2.6 %collective-permute-start.5 = (f32[24,16,256]{2,1,0:T(8,128)S(1)}, f32[24,16,256]{2,1,0:T(8,128)S(1)}, u32[]{:S(2)}, u32[]{:S(2)}) collective-permute-start(f32[24,16,256]{2,1,0:T(8,128)S(1)} %get-tuple-element.34), channel_id=1, source_target_pairs={{0,16},{8,24},{16,0},{24,8},{1,17},{9,25},{17,1},{25,9},{2,18},{10... | collective-permute-start | bytes 1179656 | tf_op jit(solution)/shard_map/ppermute | solution.py:429
  4.8 3.3 %tables.1 = (bf16[4,512,392]{2,1,0:T(8,128)(2,1)S(1)}, bf16[2,800,192]{2,1,0:T(8,128)(2,1)S(1)}, bf16[2,800,200]{2,1,0:T(8,128)(2,1)S(1)}, bf16[2,800,256]{2,1,0...) custom-call(f32[7,7]{1,0:T(8,128)S(1)} %get-tuple-element.21.basis, ...), custom_call_target="tpu_custom_call" | custom-call | bytes 7500000 | tf_op jit(solution)/shard_map/tables/pallas_call | solution.py:361
  8.2 0.0 collective-permute-done.mate
  8.2 0.0 copy-start
  8.2 3.9 %near_spectra.1 = (f32[16,256]{1,0:T(8,128)S(1)}, f32[16,256]{1,0:T(8,128)S(1)}, f32[25,16,256]{2,1,0:T(8,128)S(1)}, f32[49,16,256]{2,1,0:T(8,128)S(1)}) custom-call(f32[81,16,256]{2,1,0:T(8,128)S(1)} %get-tuple-element.25.own, f32[81,16,256]{2,1,0:T(8,128)S(1)} %collective-permute-done.mate, bf16[8192,256]{1,0:T(8,128)(2,1)S(1)} %get-tuple-element.26.where, ...), custom_call_target="tpu_custom_call" | custom-call | bytes 9000000 | tf_op jit(solution)/shard_map/near_spectra/pallas_call | solution.py:361
  12.1 0.0 copy-start.1
  12.1 0.0 copy-start.2
  12.2 0.0 copy-start.3
  12.2 0.1 collective-permute-start.1
  12.3 3.7 %collective-permute-done.1 = f32[16,256]{1,0:T(8,128)S(1)} collective-permute-done((f32[16,256]{1,0:T(8,128)S(1)}, f32[16,256]{1,0:T(8,128)S(1)}, u32[]{:S(2)}, u32[]{:S(2)}) %collective-permute-start.1) | collective-permute-done | bytes 16416 | tf_op jit(solution)/shard_map/ppermute | solution.py:466
  16.0 0.7 %collective-permute-start.7 = (f32[25,16,256]{2,1,0:T(8,128)S(1)}, f32[25,16,256]{2,1,0:T(8,128)S(1)}, u32[]{:S(2)}, u32[]{:S(2)}) collective-permute-start(f32[25,16,256]{2,1,0:T(8,128)S(1)} %get-tuple-element.38), channel_id=1, source_target_pairs={{0,16},{8,24},{16,0},{24,8},{1,17},{9,25},{17,1},{25,9},{2,18},{10... | collective-permute-start | bytes 1228808 | tf_op jit(solution)/shard_map/ppermute | solution.py:468
  16.7 0.0 collective-permute-done.5.first
  16.7 0.0 collective-permute-start.6
  16.7 1.6 %collective-permute-start.2 = (f32[16,256]{1,0:T(8,128)S(1)}, f32[16,256]{1,0:T(8,128)S(1)}, u32[]{:S(2)}, u32[]{:S(2)}) collective-permute-start(f32[16,256]{1,0:T(8,128)S(1)} %add.3.sums), channel_id=1, source_target_pairs={{0,1},{2,3},{4,5},{6,7},{1,0},{3,2},{5,4},{7,6},{8,9},{10,11},{12,... | collective-permute-start | bytes 49160 | tf_op jit(solution)/shard_map/ppermute | solution.py:397
  18.4 1.5 %collective-permute-start.3 = (f32[16,256]{1,0:T(8,128)S(1)}, f32[16,256]{1,0:T(8,128)S(1)}, u32[]{:S(2)}, u32[]{:S(2)}) collective-permute-start(f32[16,256]{1,0:T(8,128)S(1)} %add.3.sums), channel_id=1, source_target_pairs={{1,2},{5,6},{0,4},{3,7},{2,1},{6,5},{4,0},{7,3},{9,10},{13,14},{8,... | collective-permute-start | bytes 49160 | tf_op jit(solution)/shard_map/ppermute | solution.py:397
  19.9 0.5 %collective-permute-start.4 = (f32[16,256]{1,0:T(8,128)S(1)}, f32[16,256]{1,0:T(8,128)S(1)}, u32[]{:S(2)}, u32[]{:S(2)}) collective-permute-start(f32[16,256]{1,0:T(8,128)S(1)} %add.3.sums), channel_id=1, source_target_pairs={{0,4},{1,5},{2,6},{3,7},{4,0},{5,1},{6,2},{7,3},{8,12},{9,13},{10,... | collective-permute-start | bytes 49160 | tf_op jit(solution)/shard_map/ppermute | solution.py:397
  20.4 0.0 collective-permute-done.6.second
  20.4 1.3 %far_spectra.1.refs_8_ = f32[49,16,256]{2,1,0:T(8,128)S(1)} custom-call(f32[49,16,256]{2,1,0:T(8,128)S(1)} %get-tuple-element.33.keep, f32[24,16,256]{2,1,0:T(8,128)S(1)} %collective-permute-done.5.first, f32[24,16,256]{2,1,0:T(8,128)S(1)} %collective-permute-done.6.second, bf16[2,800,192]{2,1,0:T(8,128)(2,1)S(1)} %get-tuple-element.35.lead, ...), custom_call_target="tpu_custom_call" | custom-call | bytes 4500000 | tf_op jit(solution)/shard_map/far_spectra/pallas_call | solution.py:361
  21.7 0.0 collective-permute-done.2.refs_0_
  21.7 0.4 %collective-permute-done.3.refs_1_ = f32[16,256]{1,0:T(8,128)S(1)} collective-permute-done((f32[16,256]{1,0:T(8,128)S(1)}, f32[16,256]{1,0:T(8,128)S(1)}, u32[]{:S(2)}, u32[]{:S(2)}) %collective-permute-start.3) | collective-permute-done | bytes 16416 | tf_op jit(solution)/shard_map/ppermute | solution.py:397
  22.1 1.5 %collective-permute-done.4.refs_2_ = f32[16,256]{1,0:T(8,128)S(1)} collective-permute-done((f32[16,256]{1,0:T(8,128)S(1)}, f32[16,256]{1,0:T(8,128)S(1)}, u32[]{:S(2)}, u32[]{:S(2)}) %collective-permute-start.4) | collective-permute-done | bytes 16416 | tf_op jit(solution)/shard_map/ppermute | solution.py:397
  23.6 0.0 copy-done
  23.6 0.0 copy-done.1
  23.6 0.0 copy-done.2
  23.6 0.0 copy-done.3
  23.6 1.8 %back_solve.1 = (f32[49,16,256]{2,1,0:T(8,128)S(1)}, f32[16,1,256]{2,1,0:T(1,128)}) custom-call(f32[16,256]{1,0:T(8,128)S(1)} %add.3.sums, f32[16,256]{1,0:T(8,128)S(1)} %collective-permute-done.2.refs_0_, f32[16,256]{1,0:T(8,128)S(1)} %collective-permute-done.3.refs_1_, f32[16,256]{1,0:T(8,128)S(1)} %collective-permute-done.4.refs_2_, ...), custom_call_target="tpu_custom_call" | custom-call | bytes 6000000 | tf_op jit(solution)/shard_map/back_solve/pallas_call | solution.py:361
  25.4 1.0 %collective-permute-done.7.received = f32[25,16,256]{2,1,0:T(8,128)S(1)} collective-permute-done((f32[25,16,256]{2,1,0:T(8,128)S(1)}, f32[25,16,256]{2,1,0:T(8,128)S(1)}, u32[]{:S(2)}, u32[]{:S(2)}) %collective-permute-start.7) | collective-permute-done | bytes 409632 | tf_op jit(solution)/shard_map/ppermute | solution.py:468
  26.4 1.2 %interior_solve.1 = f32[49,16,256]{2,1,0:T(8,128)} custom-call(f32[49,16,256]{2,1,0:T(8,128)S(1)} %get-tuple-element.37.base, f32[25,16,256]{2,1,0:T(8,128)S(1)} %collective-permute-done.7.received, bf16[2,800,200]{2,1,0:T(8,128)(2,1)S(1)} %get-tuple-element.36.rest), custom_call_target="tpu_custom_call" | custom-call | bytes 3000000 | tf_op jit(solution)/shard_map/interior_solve/pallas_call | solution.py:361
  (1 shorter events, 0.0 us)
Async XLA Ops:
  0.6 7.5 %collective-permute-start = (f32[81,16,256]{2,1,0:T(8,128)}, f32[81,16,256]{2,1,0:T(8,128)S(1)}, u32[]{:S(2)}, u32[]{:S(2)}) collective-permute-start(f32[81,16,256]{2,1,0:T(8,128)} %bitcast.2), channel_id=1, source_target_pairs={{0,8},{8,0},{16,24},{24,16},{1,9},{9,1},{17,25},{25,17},{2,10},{10... | collective-permute-start | bytes 3981320 | tf_op jit(solution)/shard_map/ppermute | solution.py:430
  2.2 14.5 %collective-permute-start.5 = (f32[24,16,256]{2,1,0:T(8,128)S(1)}, f32[24,16,256]{2,1,0:T(8,128)S(1)}, u32[]{:S(2)}, u32[]{:S(2)}) collective-permute-start(f32[24,16,256]{2,1,0:T(8,128)S(1)} %get-tuple-element.34), channel_id=1, source_target_pairs={{0,16},{8,24},{16,0},{24,8},{1,17},{9,25},{17,1},{25,9},{2,18},{10... | collective-permute-start | bytes 1179656 | tf_op jit(solution)/shard_map/ppermute | solution.py:429
  8.2 15.4 %copy-start = (f32[16,256,256]{2,1,0:T(8,128)S(1)}, f32[16,256,256]{2,1,0:T(8,128)}, u32[]{:S(2)}) copy-start(f32[16,256,256]{2,1,0:T(8,128)} %refs_5_.1) | copy-start | bytes 12582916
  12.1 11.5 %copy-start.1 = (s32[32,256]{1,0:T(8,128)S(1)}, s32[32,256]{1,0:T(8,128)}, u32[]{:S(2)}) copy-start(s32[32,256]{1,0:T(8,128)} %refs_6_.1) | copy-start | bytes 98308
  12.1 11.5 %copy-start.2 = (s32[1,256]{1,0:T(1,128)S(1)}, s32[1,256]{1,0:T(1,128)}, u32[]{:S(2)}) copy-start(s32[1,256]{1,0:T(1,128)} %refs_3_.3) | copy-start | bytes 3076
  12.2 11.5 %copy-start.3 = (s32[1,256]{1,0:T(1,128)S(1)}, s32[1,256]{1,0:T(1,128)}, u32[]{:S(2)}) copy-start(s32[1,256]{1,0:T(1,128)} %refs_4_.1) | copy-start | bytes 3076
  12.2 3.8 %collective-permute-start.1 = (f32[16,256]{1,0:T(8,128)S(1)}, f32[16,256]{1,0:T(8,128)S(1)}, u32[]{:S(2)}, u32[]{:S(2)}) collective-permute-start(f32[16,256]{1,0:T(8,128)S(1)} %get-tuple-element.29), channel_id=1, source_target_pairs={{0,16},{8,24},{16,0},{24,8},{1,17},{9,25},{17,1},{25,9},{2,18},{10... | collective-permute-start | bytes 49160 | tf_op jit(solution)/shard_map/ppermute | solution.py:466
  16.0 10.4 %collective-permute-start.7 = (f32[25,16,256]{2,1,0:T(8,128)S(1)}, f32[25,16,256]{2,1,0:T(8,128)S(1)}, u32[]{:S(2)}, u32[]{:S(2)}) collective-permute-start(f32[25,16,256]{2,1,0:T(8,128)S(1)} %get-tuple-element.38), channel_id=1, source_target_pairs={{0,16},{8,24},{16,0},{24,8},{1,17},{9,25},{17,1},{25,9},{2,18},{10... | collective-permute-start | bytes 1228808 | tf_op jit(solution)/shard_map/ppermute | solution.py:468
  16.7 3.7 %collective-permute-start.6 = (f32[24,16,256]{2,1,0:T(8,128)S(1)}, f32[24,16,256]{2,1,0:T(8,128)S(1)}, u32[]{:S(2)}, u32[]{:S(2)}) collective-permute-start(f32[24,16,256]{2,1,0:T(8,128)S(1)} %collective-permute-done.5.first), channel_id=1, source_target_pairs={{0,8},{8,0},{16,24},{24,16},{1,9},{9,1},{17,25},{25,17},{2,10},{10... | collective-permute-start | bytes 1179656 | tf_op jit(solution)/shard_map/ppermute | solution.py:469
  16.7 5.0 %collective-permute-start.2 = (f32[16,256]{1,0:T(8,128)S(1)}, f32[16,256]{1,0:T(8,128)S(1)}, u32[]{:S(2)}, u32[]{:S(2)}) collective-permute-start(f32[16,256]{1,0:T(8,128)S(1)} %add.3.sums), channel_id=1, source_target_pairs={{0,1},{2,3},{4,5},{6,7},{1,0},{3,2},{5,4},{7,6},{8,9},{10,11},{12,... | collective-permute-start | bytes 49160 | tf_op jit(solution)/shard_map/ppermute | solution.py:397
  18.4 3.7 %collective-permute-start.3 = (f32[16,256]{1,0:T(8,128)S(1)}, f32[16,256]{1,0:T(8,128)S(1)}, u32[]{:S(2)}, u32[]{:S(2)}) collective-permute-start(f32[16,256]{1,0:T(8,128)S(1)} %add.3.sums), channel_id=1, source_target_pairs={{1,2},{5,6},{0,4},{3,7},{2,1},{6,5},{4,0},{7,3},{9,10},{13,14},{8,... | collective-permute-start | bytes 49160 | tf_op jit(solution)/shard_map/ppermute | solution.py:397
  19.9 3.7 %collective-permute-start.4 = (f32[16,256]{1,0:T(8,128)S(1)}, f32[16,256]{1,0:T(8,128)S(1)}, u32[]{:S(2)}, u32[]{:S(2)}) collective-permute-start(f32[16,256]{1,0:T(8,128)S(1)} %add.3.sums), channel_id=1, source_target_pairs={{0,4},{1,5},{2,6},{3,7},{4,0},{5,1},{6,2},{7,3},{8,12},{9,13},{10,... | collective-permute-start | bytes 49160 | tf_op jit(solution)/shard_map/ppermute | solution.py:397
